TPU v7x, 32 devices: a whole 2x2x4 slice. The times are simulated.
32 devices in a mesh: dp: 8 (over z, y), mp: 4 (over x, core).
Axes of the slice: x: 2, y: 2, z: 4, core: 2. Of those that a mesh axis runs over, the one named last changes fastest.
Arguments:
- activations: bfloat16 [4096, 2048], P('dp'), may hold values from -6 to 6
- cotangent: bfloat16 [4096, 2048], P('dp'), may hold values from -6 to 6
- positions: int32 [4096], P('dp'), may hold values from -1 to 255, as said below
- w_qkv: float32 [2, 3, 2048, 2048], P(None, None, 'dp', 'mp'), may hold values from -0.125 to 0.125
- w_out: float32 [2, 2048, 2048], P(None, 'mp', 'dp'), may hold values from -0.5 to 0.5
- w_up: float32 [2, 2048, 8192], P(None, 'dp', 'mp'), may hold values from -0.125 to 0.125
- w_down: float32 [2, 8192, 2048], P(None, 'mp', 'dp'), may hold values from -0.0625 to 0.0625
- vec_model: float32 [2, 4, 2048], P(None, None, 'dp')
- vec_head: float32 [2, 3, 2048], P(None, None, ('mp', 'dp')), may hold values from -2 to 2
- vec_ffn: float32 [2, 8192], P(None, ('mp', 'dp')), may hold values from -2 to 2
- first_qkv: float32 [2, 3, 2048, 2048], P(None, None, 'dp', 'mp'), may hold values from -32 to 32
- first_out: float32 [2, 2048, 2048], P(None, 'mp', 'dp'), may hold values from -14 to 14
- first_up: float32 [2, 2048, 8192], P(None, 'dp', 'mp'), may hold values from -14 to 14
- first_down: float32 [2, 8192, 2048], P(None, 'mp', 'dp'), may hold values from -20 to 20
- first_model: float32 [2, 4, 2048], P(None, None, 'dp'), may hold values from -40 to 40
- first_head: float32 [2, 3, 2048], P(None, None, ('mp', 'dp')), may hold values from -32 to 32
- first_ffn: float32 [2, 8192], P(None, ('mp', 'dp')), may hold values from -14 to 14
- second_qkv: float32 [2, 3, 2048, 2048], P(None, None, 'dp', 'mp'), may hold values from 108.544 to 430.08
- second_out: float32 [2, 2048, 2048], P(None, 'mp', 'dp'), may hold values from 21.7088 to 86.016
- second_up: float32 [2, 2048, 8192], P(None, 'dp', 'mp'), may hold values from 21.7088 to 86.016
- second_down: float32 [2, 8192, 2048], P(None, 'mp', 'dp'), may hold values from 54.272 to 215.04
- second_model: float32 [2, 4, 2048], P(None, None, 'dp'), may hold values from 217.088 to 860.16
- second_head: float32 [2, 3, 2048], P(None, None, ('mp', 'dp')), may hold values from 108.544 to 430.08
- second_ffn: float32 [2, 8192], P(None, ('mp', 'dp')), may hold values from 21.7088 to 86.016
Outputs:
- result: float32 [4096, 2048], P('dp')
- grad_input: float32 [4096, 2048], P('dp')
- grad_qkv: float32 [2, 3, 2048, 2048], P(None, None, 'dp', 'mp')
- next_first_qkv: float32 [2, 3, 2048, 2048], P(None, None, 'dp', 'mp')
- next_second_qkv: float32 [2, 3, 2048, 2048], P(None, None, 'dp', 'mp')
- next_w_qkv: float32 [2, 3, 2048, 2048], P(None, None, 'dp', 'mp')
- grad_out: float32 [2, 2048, 2048], P(None, 'mp', 'dp')
- next_first_out: float32 [2, 2048, 2048], P(None, 'mp', 'dp')
- next_second_out: float32 [2, 2048, 2048], P(None, 'mp', 'dp')
- next_w_out: float32 [2, 2048, 2048], P(None, 'mp', 'dp')
- grad_up: float32 [2, 2048, 8192], P(None, 'dp', 'mp')
- next_first_up: float32 [2, 2048, 8192], P(None, 'dp', 'mp')
- next_second_up: float32 [2, 2048, 8192], P(None, 'dp', 'mp')
- next_w_up: float32 [2, 2048, 8192], P(None, 'dp', 'mp')
- grad_down: float32 [2, 8192, 2048], P(None, 'mp', 'dp')
- next_first_down: float32 [2, 8192, 2048], P(None, 'mp', 'dp')
- next_second_down: float32 [2, 8192, 2048], P(None, 'mp', 'dp')
- next_w_down: float32 [2, 8192, 2048], P(None, 'mp', 'dp')
- grad_model: float32 [2, 4, 2048], P(None, None, 'dp')
- next_first_model: float32 [2, 4, 2048], P(None, None, 'dp')
- next_second_model: float32 [2, 4, 2048], P(None, None, 'dp')
- next_vec_model: float32 [2, 4, 2048], P(None, None, 'dp')
- grad_head: float32 [2, 3, 2048], P(None, None, ('mp', 'dp'))
- next_first_head: float32 [2, 3, 2048], P(None, None, ('mp', 'dp'))
- next_second_head: float32 [2, 3, 2048], P(None, None, ('mp', 'dp'))
- next_vec_head: float32 [2, 3, 2048], P(None, None, ('mp', 'dp'))
- grad_ffn: float32 [2, 8192], P(None, ('mp', 'dp'))
- next_first_ffn: float32 [2, 8192], P(None, ('mp', 'dp'))
- next_second_ffn: float32 [2, 8192], P(None, ('mp', 'dp'))
- next_vec_ffn: float32 [2, 8192], P(None, ('mp', 'dp'))
Inputs may be any that keep to these rules, and one draw needn't show every extreme that they name: Each aligned block of 256 slots holds whole sequences one after another from its start, positions counting 0, 1, 2, ... in each, then empty slots; at least half of every block's slots are used, and some block holds one sequence of 256 tokens.
All inputs are finite; a program needn't handle non-finite values.
Results may differ from a plain program's by a relative error of at most 0.025.
Values may be sent and summed in bfloat16 or wider, within the bound.
No kernel may reach another device: no remote copies, remote signals or barrier semaphores. Data moves between devices by JAX's collectives and lax.ppermute only.
A program may use at most 384 MiB of HBM per device.

v0:
```python
import math

import jax
import jax.numpy as jnp
from jax import lax
from jax.sharding import PartitionSpec as P

D = 2048
HEAD_DIM = 64
ROT = 32
FF = 8192
LAYERS = 2
MICRO = 2
STEP = 10
ROWS = 256


BETA_ONE = 0.9
BETA_TWO = 0.95
ADAM_EPS = 1e-08
DECAY = 0.1
NORM_EPS = 1e-05
MASKED = -1e30


def layer_norm(hidden, gain, shift):
    centre = hidden - jnp.mean(hidden, -1, keepdims=True)
    spread = jnp.mean(centre * centre, -1, keepdims=True)
    return centre * lax.rsqrt(spread + NORM_EPS) * gain + shift


def tables(positions):
    places = jnp.maximum(positions, 0).astype(jnp.float32)
    frequency = 10000.0 ** (-(2.0 / ROT) * jnp.arange(ROT // 2).astype(jnp.float32))
    angles = places[:, None] * frequency[None, :]
    return (jnp.cos(angles), jnp.sin(angles))


def rotate(values, cosine, sine):
    half_rot = cosine.shape[-1]
    lower_half = values[..., :half_rot]
    upper_half = values[..., half_rot : 2 * half_rot]
    remain = values[..., 2 * half_rot :]
    cos_cast = cosine[:, None, :]
    sin_cast = sine[:, None, :]
    return jnp.concatenate(
        [
            lower_half * cos_cast - upper_half * sin_cast,
            upper_half * cos_cast + lower_half * sin_cast,
            remain,
        ],
        -1,
    )


def visible(places):
    count = places.shape[-1]
    row_ids = jnp.arange(count, dtype=jnp.int32)[:, None]
    col_ids = jnp.arange(count, dtype=jnp.int32)[None, :]
    starts = row_ids - jnp.maximum(places, 0)[..., :, None]
    return (col_ids <= row_ids) & (col_ids >= starts)


def gelu_tanh(values):
    return jax.nn.gelu(values, approximate=True)


def fetch_forward(params, layer_index):
    weights_qkv, weights_out, weights_up, weights_down, model_vec, head_vec, ffn_vec = [
        piece[layer_index].astype(jnp.bfloat16) for piece in params
    ]
    return (
        lax.all_gather(weights_qkv, "dp", axis=1, tiled=True),
        lax.all_gather(weights_out, "dp", axis=1, tiled=True),
        lax.all_gather(weights_up, "dp", axis=0, tiled=True),
        lax.all_gather(weights_down, "dp", axis=1, tiled=True),
        lax.all_gather(model_vec, "dp", axis=1, tiled=True),
        lax.all_gather(head_vec, "dp", axis=1, tiled=True),
        lax.all_gather(ffn_vec, "dp", axis=0, tiled=True),
    )


def fetch_backward(params, layer_index):
    weights_qkv, weights_out, weights_up, weights_down, model_vec, head_vec, ffn_vec = [
        piece[layer_index].astype(jnp.bfloat16) for piece in params
    ]
    return (
        lax.all_gather(weights_qkv, "dp", axis=1, tiled=True),
        lax.all_gather(weights_out, "dp", axis=1, tiled=True),
        lax.all_gather(weights_up, "dp", axis=0, tiled=True),
        lax.all_gather(weights_down, "dp", axis=1, tiled=True),
        lax.all_gather(model_vec, "dp", axis=1, tiled=True),
        lax.all_gather(head_vec, "dp", axis=1, tiled=True),
        lax.all_gather(ffn_vec, "dp", axis=0, tiled=True),
    )


def reduce_micro(grads):
    grad_qkv, grad_wout, grad_up, grad_down, grad_model, grad_head, grad_ffn = grads
    return (
        lax.psum_scatter(
            grad_qkv.astype(jnp.bfloat16), "dp", scatter_dimension=1, tiled=True
        ).astype(jnp.float32),
        lax.psum_scatter(
            grad_wout.astype(jnp.bfloat16), "dp", scatter_dimension=1, tiled=True
        ).astype(jnp.float32),
        lax.psum_scatter(
            grad_up.astype(jnp.bfloat16), "dp", scatter_dimension=0, tiled=True
        ).astype(jnp.float32),
        lax.psum_scatter(
            grad_down.astype(jnp.bfloat16), "dp", scatter_dimension=1, tiled=True
        ).astype(jnp.float32),
        lax.psum_scatter(
            grad_model.astype(jnp.bfloat16), "dp", scatter_dimension=1, tiled=True
        ).astype(jnp.float32),
        lax.psum_scatter(
            grad_head.astype(jnp.bfloat16), "dp", scatter_dimension=1, tiled=True
        ).astype(jnp.float32),
        lax.psum_scatter(
            grad_ffn.astype(jnp.bfloat16), "dp", scatter_dimension=0, tiled=True
        ).astype(jnp.float32),
    )


def add_trees(first_tree, second_tree):
    if first_tree is None:
        return tuple(second_tree)
    return tuple((left + right for left, right in zip(first_tree, second_tree)))


def slice_saved(saved, first_row, row_count, first_block, block_count):
    normed, queries, keys_rot, values, log_total, heads_out, gate_in, activated = saved

    def rows(array):
        return lax.slice_in_dim(array, first_row, first_row + row_count, axis=0)

    def blocks(array):
        return lax.slice_in_dim(array, first_block, first_block + block_count, axis=0)

    return (
        rows(normed),
        blocks(queries),
        blocks(keys_rot),
        blocks(values),
        blocks(log_total),
        rows(heads_out),
        rows(gate_in),
        rows(activated),
    )


def masked_scores(queries, keys_rot, mask):
    score_scale = HEAD_DIM ** (-0.5)
    scores = (
        jnp.einsum("bqhe,bkhe->bhqk", queries, keys_rot, preferred_element_type=jnp.float32)
        * score_scale
    )
    return jnp.where(mask[:, None], scores, MASKED)


def forward_layer(hidden, loaded, cosine, sine, mask):
    weights_qkv, weights_out, weights_up, weights_down, model_vec, head_vec, ffn_vec = loaded
    model_vec = model_vec.astype(jnp.float32)
    row_count = hidden.shape[0]
    blocks = row_count // ROWS
    local_heads = weights_qkv.shape[2] // HEAD_DIM
    normed = layer_norm(hidden, model_vec[0], model_vec[1]).astype(jnp.bfloat16)
    project = (
        jnp.einsum("rd,cde->cre", normed, weights_qkv, preferred_element_type=jnp.float32)
        + head_vec.astype(jnp.float32)[:, None, :]
    )
    project = project.reshape(3, row_count, local_heads, HEAD_DIM)
    shape_four = (blocks, ROWS, local_heads, HEAD_DIM)
    queries = rotate(project[0], cosine, sine).astype(jnp.bfloat16).reshape(shape_four)
    keys_rot = rotate(project[1], cosine, sine).astype(jnp.bfloat16).reshape(shape_four)
    values = project[2].astype(jnp.bfloat16).reshape(shape_four)
    scores = masked_scores(queries, keys_rot, mask)
    row_max = jnp.max(scores, -1, keepdims=True)
    exponent = jnp.exp(scores - row_max)
    totals = jnp.sum(exponent, -1, keepdims=True)
    attn_probs = exponent / totals
    log_total = row_max + jnp.log(totals)
    mixture = jnp.einsum(
        "bhqk,bkhe->bqhe",
        attn_probs.astype(jnp.bfloat16),
        values,
        preferred_element_type=jnp.float32,
    )
    heads_out = mixture.reshape(row_count, -1).astype(jnp.bfloat16)
    attention = jnp.dot(heads_out, weights_out, preferred_element_type=jnp.float32)
    gate_in = jnp.dot(normed, weights_up, preferred_element_type=jnp.float32) + ffn_vec.astype(
        jnp.float32
    )
    activated = gelu_tanh(gate_in).astype(jnp.bfloat16)
    branch_part = attention + jnp.dot(activated, weights_down, preferred_element_type=jnp.float32)
    branch = lax.psum(branch_part.astype(jnp.bfloat16), "mp").astype(jnp.float32)
    result = hidden + branch + model_vec[2] + model_vec[3]
    return (result, (normed, queries, keys_rot, values, log_total, heads_out, gate_in, activated))


def backward_layer(grad_next, hidden, saved, loaded, cosine, sine, mask):
    normed, queries, keys_rot, values, log_total, heads_out, gate_in, activated = saved
    weights_qkv, weights_out, weights_up, weights_down, model_vec, head_vec, ffn_vec = loaded
    model_vec = model_vec.astype(jnp.float32)
    row_count = hidden.shape[0]
    shape_four = queries.shape
    grad_low = grad_next.astype(jnp.bfloat16)
    bias_grad = jnp.sum(grad_next, 0)
    grad_down = jnp.einsum("rf,rd->fd", activated, grad_low, preferred_element_type=jnp.float32)
    grad_act = jnp.einsum("rd,fd->rf", grad_low, weights_down, preferred_element_type=jnp.float32)
    grad_gate = jax.vjp(gelu_tanh, gate_in)[1](grad_act)[0].astype(jnp.bfloat16)
    grad_up = jnp.einsum("rd,rf->df", normed, grad_gate, preferred_element_type=jnp.float32)
    grad_ffn = jnp.sum(grad_gate, 0, dtype=jnp.float32)
    grad_wout = jnp.einsum("rc,rd->cd", heads_out, grad_low, preferred_element_type=jnp.float32)
    grad_heads = (
        jnp.einsum("rd,cd->rc", grad_low, weights_out, preferred_element_type=jnp.float32)
        .astype(jnp.bfloat16)
        .reshape(shape_four)
    )
    scores = masked_scores(queries, keys_rot, mask)
    attn_probs = jnp.exp(scores - log_total)
    grad_probs = jnp.einsum(
        "bqhe,bkhe->bhqk", grad_heads, values, preferred_element_type=jnp.float32
    )
    row_dot = jnp.sum(attn_probs * grad_probs, -1, keepdims=True)
    grad_scores = (attn_probs * (grad_probs - row_dot)).astype(jnp.bfloat16)
    score_scale = HEAD_DIM ** (-0.5)
    grad_queries = (
        jnp.einsum("bhqk,bkhe->bqhe", grad_scores, keys_rot, preferred_element_type=jnp.float32)
        * score_scale
    )
    grad_keys = (
        jnp.einsum("bhqk,bqhe->bkhe", grad_scores, queries, preferred_element_type=jnp.float32)
        * score_scale
    )
    grad_values = jnp.einsum(
        "bhqk,bqhe->bkhe",
        attn_probs.astype(jnp.bfloat16),
        grad_heads,
        preferred_element_type=jnp.float32,
    )
    head_shape = (row_count, shape_four[2], HEAD_DIM)

    def turn(piece):
        return rotate(piece, cosine, sine)

    pull_turn = jax.vjp(turn, jnp.zeros(head_shape, jnp.float32))[1]
    grad_project = jnp.stack(
        [
            pull_turn(grad_queries.reshape(head_shape))[0],
            pull_turn(grad_keys.reshape(head_shape))[0],
            grad_values.reshape(head_shape),
        ]
    )
    grad_project = grad_project.reshape(3, row_count, -1).astype(jnp.bfloat16)
    grad_head_vec = jnp.sum(grad_project, 1, dtype=jnp.float32)
    grad_qkv = jnp.einsum("rd,cre->cde", normed, grad_project, preferred_element_type=jnp.float32)
    normed_part = jnp.einsum(
        "cre,cde->rd", grad_project, weights_qkv, preferred_element_type=jnp.float32
    )
    normed_part = normed_part + jnp.einsum(
        "rf,df->rd", grad_gate, weights_up, preferred_element_type=jnp.float32
    )
    grad_normed = lax.psum(normed_part.astype(jnp.bfloat16), "mp").astype(jnp.float32)
    pull_norm = jax.vjp(layer_norm, hidden, model_vec[0], model_vec[1])[1]
    grad_hidden, grad_gain, grad_shift = pull_norm(grad_normed)
    grad_model = jnp.stack([grad_gain, grad_shift, bias_grad, bias_grad])
    return (
        grad_next + grad_hidden,
        (grad_qkv, grad_wout, grad_up, grad_down, grad_model, grad_head_vec, grad_ffn),
    )


def adamw(weight, grad, first, second, rate, decay):
    first_new = BETA_ONE * first + (1.0 - BETA_ONE) * grad
    second_new = BETA_TWO * second + (1.0 - BETA_TWO) * grad * grad
    first_hat = first_new / (1.0 - BETA_ONE**STEP)
    second_hat = second_new / (1.0 - BETA_TWO**STEP)
    weight_new = weight - rate * (first_hat / (jnp.sqrt(second_hat) + ADAM_EPS) + decay * weight)
    return (first_new, second_new, weight_new)


def per_device(
    activations,
    cotangent,
    positions,
    w_qkv,
    w_out,
    w_up,
    w_down,
    vec_model,
    vec_head,
    vec_ffn,
    first_qkv,
    first_out,
    first_up,
    first_down,
    first_model,
    first_head,
    first_ffn,
    second_qkv,
    second_out,
    second_up,
    second_down,
    second_model,
    second_head,
    second_ffn,
):
    cosine, sine = tables(positions)
    mask = visible(positions.reshape(-1, ROWS))
    params = (w_qkv, w_out, w_up, w_down, vec_model, vec_head, vec_ffn)
    hidden = activations.astype(jnp.float32)
    inputs_kept = []
    saved_kept = []
    loaded_kept = []
    for layer_index in range(LAYERS):
        loaded = fetch_forward(params, layer_index)
        inputs_kept.append(hidden)
        hidden, saved = forward_layer(hidden, loaded, cosine, sine, mask)
        saved_kept.append(saved)
        loaded_kept.append(loaded)
    live = (positions >= 0).astype(jnp.float32)[:, None]
    grad_next = cotangent.astype(jnp.float32) * live
    micro_rows = grad_next.shape[0] // MICRO
    micro_blocks = micro_rows // ROWS
    shard_grads = [None] * LAYERS
    for layer_index in reversed(range(LAYERS)):
        loaded = fetch_backward(params, layer_index)
        pieces = []
        totals = None
        for micro_index in range(MICRO):
            first_row = micro_index * micro_rows
            first_block = micro_index * micro_blocks
            saved_part = slice_saved(
                saved_kept[layer_index], first_row, micro_rows, first_block, micro_blocks
            )
            grad_part, grads = backward_layer(
                lax.slice_in_dim(grad_next, first_row, first_row + micro_rows, axis=0),
                lax.slice_in_dim(
                    inputs_kept[layer_index], first_row, first_row + micro_rows, axis=0
                ),
                saved_part,
                loaded,
                lax.slice_in_dim(cosine, first_row, first_row + micro_rows, axis=0),
                lax.slice_in_dim(sine, first_row, first_row + micro_rows, axis=0),
                lax.slice_in_dim(mask, first_block, first_block + micro_blocks, axis=0),
            )
            pieces.append(grad_part)
            totals = add_trees(totals, reduce_micro(grads))
        shard_grads[layer_index] = totals
        grad_next = jnp.concatenate(pieces, 0)
    stacked = [
        jnp.stack([shard_grads[layer_index][which] for layer_index in range(LAYERS)])
        for which in range(7)
    ]
    grad_qkv, grad_out, grad_up, grad_down, grad_model, grad_head, grad_ffn = stacked
    rate_in = 3.0 / math.sqrt(D)
    next_first_qkv, next_second_qkv, next_w_qkv = adamw(
        w_qkv, grad_qkv, first_qkv, second_qkv, rate_in, DECAY
    )
    next_first_out, next_second_out, next_w_out = adamw(
        w_out, grad_out, first_out, second_out, 12.0 / math.sqrt(D), DECAY
    )
    next_first_up, next_second_up, next_w_up = adamw(
        w_up, grad_up, first_up, second_up, rate_in, DECAY
    )
    next_first_down, next_second_down, next_w_down = adamw(
        w_down, grad_down, first_down, second_down, 3.0 / math.sqrt(FF), DECAY
    )
    next_first_model, next_second_model, next_vec_model = adamw(
        vec_model, grad_model, first_model, second_model, 0.6, 0.0
    )
    next_first_head, next_second_head, next_vec_head = adamw(
        vec_head, grad_head, first_head, second_head, 0.6, 0.0
    )
    next_first_ffn, next_second_ffn, next_vec_ffn = adamw(
        vec_ffn, grad_ffn, first_ffn, second_ffn, 0.6, 0.0
    )
    return (
        hidden,
        grad_next,
        grad_qkv,
        next_first_qkv,
        next_second_qkv,
        next_w_qkv,
        grad_out,
        next_first_out,
        next_second_out,
        next_w_out,
        grad_up,
        next_first_up,
        next_second_up,
        next_w_up,
        grad_down,
        next_first_down,
        next_second_down,
        next_w_down,
        grad_model,
        next_first_model,
        next_second_model,
        next_vec_model,
        grad_head,
        next_first_head,
        next_second_head,
        next_vec_head,
        grad_ffn,
        next_first_ffn,
        next_second_ffn,
        next_vec_ffn,
    )


def solution(mesh):
    return jax.shard_map(
        per_device,
        mesh=mesh,
        in_specs=(
            P("dp", None),
            P("dp", None),
            P("dp"),
            P(None, None, "dp", "mp"),
            P(None, "mp", "dp"),
            P(None, "dp", "mp"),
            P(None, "mp", "dp"),
            P(None, None, "dp"),
            P(None, None, ("mp", "dp")),
            P(None, ("mp", "dp")),
            P(None, None, "dp", "mp"),
            P(None, "mp", "dp"),
            P(None, "dp", "mp"),
            P(None, "mp", "dp"),
            P(None, None, "dp"),
            P(None, None, ("mp", "dp")),
            P(None, ("mp", "dp")),
            P(None, None, "dp", "mp"),
            P(None, "mp", "dp"),
            P(None, "dp", "mp"),
            P(None, "mp", "dp"),
            P(None, None, "dp"),
            P(None, None, ("mp", "dp")),
            P(None, ("mp", "dp")),
        ),
        out_specs=(
            P("dp", None),
            P("dp", None),
            P(None, None, "dp", "mp"),
            P(None, None, "dp", "mp"),
            P(None, None, "dp", "mp"),
            P(None, None, "dp", "mp"),
            P(None, "mp", "dp"),
            P(None, "mp", "dp"),
            P(None, "mp", "dp"),
            P(None, "mp", "dp"),
            P(None, "dp", "mp"),
            P(None, "dp", "mp"),
            P(None, "dp", "mp"),
            P(None, "dp", "mp"),
            P(None, "mp", "dp"),
            P(None, "mp", "dp"),
            P(None, "mp", "dp"),
            P(None, "mp", "dp"),
            P(None, None, "dp"),
            P(None, None, "dp"),
            P(None, None, "dp"),
            P(None, None, "dp"),
            P(None, None, ("mp", "dp")),
            P(None, None, ("mp", "dp")),
            P(None, None, ("mp", "dp")),
            P(None, None, ("mp", "dp")),
            P(None, ("mp", "dp")),
            P(None, ("mp", "dp")),
            P(None, ("mp", "dp")),
            P(None, ("mp", "dp")),
        ),
        check_vma=False,
    )
```

profile of v0, /device:TPU:0, one launch (start us, length us, event | category | flops | bytes accessed | tf_op | source)
XLA Modules:
  0.0 3657.4 jit_solution(16130011664628739747)
XLA Ops:
  72.6 31.7 all-gather.2
  136.3 110.0 %all-gather.27.cloned.1.call-done = bf16[1,2048,2048]{2,1,0:T(8,128)(2,1)} async-done(((bf16[1,256,2048]{2,1,0:T(8,128)(2,1)}), bf16[1,2048,2048]{2,1,0:T(8,128)(2,1)}) %all-gather.27.cloned.1.call-update) | async-done | bytes 8388624 | tf_op jit(solution)/shard_map/all_gather | solution.py:75
  258.4 114.1 %all-gather.29.cloned.1.call-done = bf16[1,2048,2048]{2,1,0:T(8,128)(2,1)} async-done(((bf16[1,2048,256]{2,1,0:T(8,128)(2,1)}), bf16[1,2048,2048]{2,1,0:T(8,128)(2,1)}) %all-gather.29.cloned.1.call-update) | async-done | bytes 8388624 | tf_op jit(solution)/shard_map/all_gather | solution.py:76
  383.1 41.2 %all-gather.25.cloned.1.call-done = bf16[1,512,2048]{2,1,0:T(8,128)(2,1)} async-done(((bf16[1,512,256]{2,1,0:T(8,128)(2,1)}), bf16[1,512,2048]{2,1,0:T(8,128)(2,1)}) %all-gather.25.cloned.1.call-update) | async-done | bytes 2097168 | tf_op jit(solution)/shard_map/all_gather | solution.py:74
  452.1 31.3 all-gather.9
  538.2 96.3 %all-gather.31.cloned.1.call-done = bf16[1,3,2048,512]{2,3,1,0:T(8,128)(2,1)} async-done(((bf16[1,3,256,512]{2,3,1,0:T(8,128)(2,1)}), bf16[1,3,2048,512]{2,3,1,0:T(8,128)(2,1)}) %all-gather.31.cloned.1.call-update) | async-done | bytes 6291472 | tf_op jit(solution)/shard_map/all_gather | solution.py:73
  692.2 68.4 %all-gather.35.cloned.1.call-done = bf16[1,2048,2048]{2,1,0:T(8,128)(2,1)} async-done(((bf16[1,256,2048]{2,1,0:T(8,128)(2,1)}), bf16[1,2048,2048]{2,1,0:T(8,128)(2,1)}) %all-gather.35.cloned.1.call-update) | async-done | bytes 8388624 | tf_op jit(solution)/shard_map/all_gather | solution.py:75
  772.9 114.1 %all-gather.37.cloned.1.call-done = bf16[1,2048,2048]{2,1,0:T(8,128)(2,1)} async-done(((bf16[1,2048,256]{2,1,0:T(8,128)(2,1)}), bf16[1,2048,2048]{2,1,0:T(8,128)(2,1)}) %all-gather.37.cloned.1.call-update) | async-done | bytes 8388624 | tf_op jit(solution)/shard_map/all_gather | solution.py:76
  928.2 37.7 %all-reduce.39.cloned.1.call-done = (bf16[256,2048]{1,0:T(8,128)(2,1)}, bf16[256,2048]{1,0:T(8,128)(2,1)}) async-done(((bf16[256,2048]{1,0:T(8,128)(2,1)}, bf16[256,2048]{1,0:T(8,128)(2,1)}), (bf16[256,2048]{1,0:T(8,128)(2,1)}, bf16[256,2048]{1,0:T(8,128)(2,1)})) %all-reduce.39.cloned.1.call-update) | async-done | bytes 2097168 | tf_op jit(solution)/shard_map/psum | solution.py:264
  1063.6 71.8 %all-reduce.37.cloned.1.call-done = (bf16[512,2048]{1,0:T(8,128)(2,1)}, bf16[256,2048]{1,0:T(8,128)(2,1)}, bf16[256,2048]{1,0:T(8,128)(2,1)}) async-done(((bf16[512,2048]{1,0:T(8,128)(2,1)}, bf16[256,2048]{1,0:T(8,128)(2,1)}, bf16[256,2048]{1,0:T(8,128)(2,1)}), (bf16[512,2048]{1,0:T(8,128)(2,1)}, bf16[256,2048]{1,0:T(8,128)(2,1)}, bf16[256,2048]{1,0:T(8,128)(2,1)})) %all-reduce.37.cloned.1.call-update) | async-done | bytes 4194320 | tf_op jit(solution)/shard_map/psum | solution.py:196
  1264.4 35.6 all-reduce.28
  1327.7 62.6 %reduce-scatter.81.cloned.1.call-done = bf16[64,3]{1,0:T(8,128)(2,1)} async-done(((bf16[512,3]{1,0:T(8,128)(2,1)}), bf16[64,3]{1,0:T(8,128)(2,1)}) %reduce-scatter.81.cloned.1.call-update) | async-done | bytes 400
  1393.6 61.4 %reduce-scatter.79.cloned.1.call-done = bf16[256,4]{1,0:T(8,128)(2,1)} async-done(((bf16[2048,4]{1,0:T(8,128)(2,1)}), bf16[256,4]{1,0:T(8,128)(2,1)}) %reduce-scatter.79.cloned.1.call-update) | async-done | bytes 2064
  1455.8 63.2 %reduce-scatter.77.cloned.1.call-done = bf16[256,4]{1,0:T(8,128)(2,1)} async-done(((bf16[2048,4]{1,0:T(8,128)(2,1)}), bf16[256,4]{1,0:T(8,128)(2,1)}) %reduce-scatter.77.cloned.1.call-update) | async-done | bytes 2064
  1531.1 53.1 %reduce-scatter.75.cloned.1.call-done = bf16[256,4]{1,0:T(8,128)(2,1)} async-done(((bf16[2048,4]{1,0:T(8,128)(2,1)}), bf16[256,4]{1,0:T(8,128)(2,1)}) %reduce-scatter.75.cloned.1.call-update) | async-done | bytes 2064
  1585.1 63.4 %reduce-scatter.73.cloned.1.call-done = bf16[256,4]{1,0:T(8,128)(2,1)} async-done(((bf16[2048,4]{1,0:T(8,128)(2,1)}), bf16[256,4]{1,0:T(8,128)(2,1)}) %reduce-scatter.73.cloned.1.call-update) | async-done | bytes 2064
  1650.2 70.2 %reduce-scatter.55.cloned.1.call-done = bf16[512,256]{1,0:T(8,128)(2,1)} async-done(((bf16[512,2048]{1,0:T(8,128)(2,1)}), bf16[512,256]{1,0:T(8,128)(2,1)}) %reduce-scatter.55.cloned.1.call-update) | async-done | bytes 262160 | tf_op jit(solution)/shard_map/reduce_scatter | solution.py:104
  1720.3 71.9 %reduce-scatter.53.cloned.1.call-done = bf16[512,256]{1,0:T(8,128)(2,1)} async-done(((bf16[512,2048]{1,0:T(8,128)(2,1)}), bf16[512,256]{1,0:T(8,128)(2,1)}) %reduce-scatter.53.cloned.1.call-update) | async-done | bytes 262160 | tf_op jit(solution)/shard_map/reduce_scatter | solution.py:104
  1793.4 70.7 %reduce-scatter.51.cloned.1.call-done = bf16[512,256]{1,0:T(8,128)(2,1)} async-done(((bf16[512,2048]{1,0:T(8,128)(2,1)}), bf16[512,256]{1,0:T(8,128)(2,1)}) %reduce-scatter.51.cloned.1.call-update) | async-done | bytes 262160 | tf_op jit(solution)/shard_map/reduce_scatter | solution.py:104
  1864.1 71.4 %reduce-scatter.49.cloned.1.call-done = bf16[512,256]{1,0:T(8,128)(2,1)} async-done(((bf16[512,2048]{1,0:T(8,128)(2,1)}), bf16[512,256]{1,0:T(8,128)(2,1)}) %reduce-scatter.49.cloned.1.call-update) | async-done | bytes 262160 | tf_op jit(solution)/shard_map/reduce_scatter | solution.py:104
  1940.0 116.7 %reduce-scatter.47.cloned.1.call-done = bf16[3,256,512]{1,2,0:T(8,128)(2,1)} async-done(((bf16[3,2048,512]{1,2,0:T(8,128)(2,1)}), bf16[3,256,512]{1,2,0:T(8,128)(2,1)}) %reduce-scatter.47.cloned.1.call-update) | async-done | bytes 786448 | tf_op jit(solution)/shard_map/reduce_scatter | solution.py:101
  2056.8 121.6 %reduce-scatter.45.cloned.1.call-done = bf16[3,256,512]{1,2,0:T(8,128)(2,1)} async-done(((bf16[3,2048,512]{1,2,0:T(8,128)(2,1)}), bf16[3,256,512]{1,2,0:T(8,128)(2,1)}) %reduce-scatter.45.cloned.1.call-update) | async-done | bytes 786448 | tf_op jit(solution)/shard_map/reduce_scatter | solution.py:101
  2181.0 118.8 %reduce-scatter.43.cloned.1.call-done = bf16[3,256,512]{1,2,0:T(8,128)(2,1)} async-done(((bf16[3,2048,512]{1,2,0:T(8,128)(2,1)}), bf16[3,256,512]{1,2,0:T(8,128)(2,1)}) %reduce-scatter.43.cloned.1.call-update) | async-done | bytes 786448 | tf_op jit(solution)/shard_map/reduce_scatter | solution.py:101
  2299.8 121.4 %reduce-scatter.41.cloned.1.call-done = bf16[3,256,512]{1,2,0:T(8,128)(2,1)} async-done(((bf16[3,2048,512]{1,2,0:T(8,128)(2,1)}), bf16[3,256,512]{1,2,0:T(8,128)(2,1)}) %reduce-scatter.41.cloned.1.call-update) | async-done | bytes 786448 | tf_op jit(solution)/shard_map/reduce_scatter | solution.py:101
  2443.4 130.1 %reduce-scatter.63.cloned.1.call-done = bf16[256,2048]{1,0:T(8,128)(2,1)} async-done(((bf16[2048,2048]{1,0:T(8,128)(2,1)}), bf16[256,2048]{1,0:T(8,128)(2,1)}) %reduce-scatter.63.cloned.1.call-update) | async-done | bytes 1048592 | tf_op jit(solution)/shard_map/reduce_scatter | solution.py:107
  2573.5 151.7 %reduce-scatter.61.cloned.1.call-done = bf16[256,2048]{1,0:T(8,128)(2,1)} async-done(((bf16[2048,2048]{1,0:T(8,128)(2,1)}), bf16[256,2048]{1,0:T(8,128)(2,1)}) %reduce-scatter.61.cloned.1.call-update) | async-done | bytes 1048592 | tf_op jit(solution)/shard_map/reduce_scatter | solution.py:107
  2728.5 149.1 %reduce-scatter.71.cloned.1.call-done = bf16[2048,256]{1,0:T(8,128)(2,1)} async-done(((bf16[2048,2048]{1,0:T(8,128)(2,1)}), bf16[2048,256]{1,0:T(8,128)(2,1)}) %reduce-scatter.71.cloned.1.call-update) | async-done | bytes 1048592 | tf_op jit(solution)/shard_map/reduce_scatter | solution.py:110
  2877.6 152.1 %reduce-scatter.69.cloned.1.call-done = bf16[2048,256]{1,0:T(8,128)(2,1)} async-done(((bf16[2048,2048]{1,0:T(8,128)(2,1)}), bf16[2048,256]{1,0:T(8,128)(2,1)}) %reduce-scatter.69.cloned.1.call-update) | async-done | bytes 1048592 | tf_op jit(solution)/shard_map/reduce_scatter | solution.py:110
  3031.4 150.4 %reduce-scatter.59.cloned.1.call-done = bf16[256,2048]{1,0:T(8,128)(2,1)} async-done(((bf16[2048,2048]{1,0:T(8,128)(2,1)}), bf16[256,2048]{1,0:T(8,128)(2,1)}) %reduce-scatter.59.cloned.1.call-update) | async-done | bytes 1048592 | tf_op jit(solution)/shard_map/reduce_scatter | solution.py:107
  3181.8 151.5 %reduce-scatter.57.cloned.1.call-done = bf16[256,2048]{1,0:T(8,128)(2,1)} async-done(((bf16[2048,2048]{1,0:T(8,128)(2,1)}), bf16[256,2048]{1,0:T(8,128)(2,1)}) %reduce-scatter.57.cloned.1.call-update) | async-done | bytes 1048592 | tf_op jit(solution)/shard_map/reduce_scatter | solution.py:107
  3346.2 139.6 %reduce-scatter.67.cloned.1.call-done = bf16[2048,256]{1,0:T(8,128)(2,1)} async-done(((bf16[2048,2048]{1,0:T(8,128)(2,1)}), bf16[2048,256]{1,0:T(8,128)(2,1)}) %reduce-scatter.67.cloned.1.call-update) | async-done | bytes 1048592 | tf_op jit(solution)/shard_map/reduce_scatter | solution.py:110
  3485.8 152.1 %reduce-scatter.65.cloned.1.call-done = bf16[2048,256]{1,0:T(8,128)(2,1)} async-done(((bf16[2048,2048]{1,0:T(8,128)(2,1)}), bf16[2048,256]{1,0:T(8,128)(2,1)}) %reduce-scatter.65.cloned.1.call-update) | async-done | bytes 1048592 | tf_op jit(solution)/shard_map/reduce_scatter | solution.py:110
  (715 shorter events, 644.6 us)
Async XLA Ops:
  12.6 233.7 %all-gather.27.cloned.1.call-start = ((), (), s32[]{:S(2)}) async-start(), calls=%async_computation.43 | async-start | bytes 9437184 | tf_op jit(solution)/shard_map/all_gather | solution.py:75
  16.6 355.9 %all-gather.29.cloned.1.call-start = ((), (), s32[]{:S(2)}) async-start(), calls=%async_computation.44 | async-start | bytes 9437184 | tf_op jit(solution)/shard_map/all_gather | solution.py:76
  20.5 403.8 %all-gather.25.cloned.1.call-start = ((), (), s32[]{:S(2)}) async-start(), calls=%async_computation.42 | async-start | bytes 2359296 | tf_op jit(solution)/shard_map/all_gather | solution.py:74
  21.6 494.5 %all-gather.33.cloned.1.call-start = ((), (), s32[]{:S(2)}) async-start(), calls=%async_computation.46 | async-start | bytes 2359296 | tf_op jit(solution)/shard_map/all_gather | solution.py:74
  22.1 509.5 %all-reduce.35.cloned.1.call-start = ((), (), s32[]{:S(2)}) async-start(), calls=%async_computation.24 | async-start | bytes 4194304 | tf_op jit(solution)/shard_map/psum | solution.py:196
  430.9 329.6 %all-gather.35.cloned.1.call-start = ((), (), s32[]{:S(2)}) async-start(), calls=%async_computation.47 | async-start | bytes 9437184 | tf_op jit(solution)/shard_map/all_gather | solution.py:75
  431.7 455.3 %all-gather.37.cloned.1.call-start = ((), (), s32[]{:S(2)}) async-start(), calls=%async_computation.48 | async-start | bytes 9437184 | tf_op jit(solution)/shard_map/all_gather | solution.py:76
  432.4 533.5 %all-reduce.39.cloned.1.call-start = ((), (), s32[]{:S(2)}) async-start(), calls=%async_computation.58 | async-start | bytes 4194304 | tf_op jit(solution)/shard_map/psum | solution.py:264
  916.0 219.5 %all-reduce.37.cloned.1.call-start = ((), (), s32[]{:S(2)}) async-start(), calls=%async_computation.57 | async-start | bytes 8388608 | tf_op jit(solution)/shard_map/psum | solution.py:196
  1054.9 208.7 %reduce-scatter.85.cloned.1.call-start = ((), (), s32[]{:S(2)}) async-start(), calls=%async_computation.55 | async-start | bytes 147456
  1056.0 271.0 %reduce-scatter.83.cloned.1.call-start = ((), (), s32[]{:S(2)}) async-start(), calls=%async_computation.54 | async-start | bytes 147456
  1058.1 332.3 %reduce-scatter.81.cloned.1.call-start = ((), (), s32[]{:S(2)}) async-start(), calls=%async_computation.53 | async-start | bytes 147456
  1060.5 394.4 %reduce-scatter.79.cloned.1.call-start = ((), (), s32[]{:S(2)}) async-start(), calls=%async_computation.52 | async-start | bytes 589824
  1062.3 456.7 %reduce-scatter.77.cloned.1.call-start = ((), (), s32[]{:S(2)}) async-start(), calls=%async_computation.51 | async-start | bytes 589824
  1063.6 520.6 %reduce-scatter.75.cloned.1.call-start = ((), (), s32[]{:S(2)}) async-start(), calls=%async_computation.50 | async-start | bytes 589824
  1144.8 503.7 %reduce-scatter.73.cloned.1.call-start = ((), (), s32[]{:S(2)}) async-start(), calls=%async_computation.49 | async-start | bytes 589824
  1146.0 574.3 %reduce-scatter.55.cloned.1.call-start = ((), (), s32[]{:S(2)}) async-start(), calls=%async_computation.32 | async-start | bytes 2359296 | tf_op jit(solution)/shard_map/reduce_scatter | solution.py:104
  1149.2 643.1 %reduce-scatter.53.cloned.1.call-start = ((), (), s32[]{:S(2)}) async-start(), calls=%async_computation.31 | async-start | bytes 2359296 | tf_op jit(solution)/shard_map/reduce_scatter | solution.py:104
  1152.2 711.9 %reduce-scatter.51.cloned.1.call-start = ((), (), s32[]{:S(2)}) async-start(), calls=%async_computation.30 | async-start | bytes 2359296 | tf_op jit(solution)/shard_map/reduce_scatter | solution.py:104
  1155.5 779.9 %reduce-scatter.49.cloned.1.call-start = ((), (), s32[]{:S(2)}) async-start(), calls=%async_computation.29 | async-start | bytes 2359296 | tf_op jit(solution)/shard_map/reduce_scatter | solution.py:104
  1159.2 897.6 %reduce-scatter.47.cloned.1.call-start = ((), (), s32[]{:S(2)}) async-start(), calls=%async_computation.28 | async-start | bytes 7077888 | tf_op jit(solution)/shard_map/reduce_scatter | solution.py:101
  1164.7 1013.7 %reduce-scatter.45.cloned.1.call-start = ((), (), s32[]{:S(2)}) async-start(), calls=%async_computation.27 | async-start | bytes 7077888 | tf_op jit(solution)/shard_map/reduce_scatter | solution.py:101
  1171.3 1128.5 %reduce-scatter.43.cloned.1.call-start = ((), (), s32[]{:S(2)}) async-start(), calls=%async_computation.26 | async-start | bytes 7077888 | tf_op jit(solution)/shard_map/reduce_scatter | solution.py:101
  1178.4 1242.9 %reduce-scatter.41.cloned.1.call-start = ((), (), s32[]{:S(2)}) async-start(), calls=%async_computation.25 | async-start | bytes 7077888 | tf_op jit(solution)/shard_map/reduce_scatter | solution.py:101
  1184.8 1388.7 %reduce-scatter.63.cloned.1.call-start = ((), (), s32[]{:S(2)}) async-start(), calls=%async_computation.36 | async-start | bytes 9437184 | tf_op jit(solution)/shard_map/reduce_scatter | solution.py:107
  1192.2 1533.1 %reduce-scatter.61.cloned.1.call-start = ((), (), s32[]{:S(2)}) async-start(), calls=%async_computation.35 | async-start | bytes 9437184 | tf_op jit(solution)/shard_map/reduce_scatter | solution.py:107
  1199.5 1678.1 %reduce-scatter.71.cloned.1.call-start = ((), (), s32[]{:S(2)}) async-start(), calls=%async_computation.40 | async-start | bytes 9437184 | tf_op jit(solution)/shard_map/reduce_scatter | solution.py:110
  1206.8 1822.9 %reduce-scatter.69.cloned.1.call-start = ((), (), s32[]{:S(2)}) async-start(), calls=%async_computation.39 | async-start | bytes 9437184 | tf_op jit(solution)/shard_map/reduce_scatter | solution.py:110
  1214.3 1967.5 %reduce-scatter.59.cloned.1.call-start = ((), (), s32[]{:S(2)}) async-start(), calls=%async_computation.34 | async-start | bytes 9437184 | tf_op jit(solution)/shard_map/reduce_scatter | solution.py:107
  1221.3 2112.0 %reduce-scatter.57.cloned.1.call-start = ((), (), s32[]{:S(2)}) async-start(), calls=%async_computation.33 | async-start | bytes 9437184 | tf_op jit(solution)/shard_map/reduce_scatter | solution.py:107
  1228.3 2257.5 %reduce-scatter.67.cloned.1.call-start = ((), (), s32[]{:S(2)}) async-start(), calls=%async_computation.38 | async-start | bytes 9437184 | tf_op jit(solution)/shard_map/reduce_scatter | solution.py:110
  1236.5 2401.4 %reduce-scatter.65.cloned.1.call-start = ((), (), s32[]{:S(2)}) async-start(), calls=%async_computation.37 | async-start | bytes 9437184 | tf_op jit(solution)/shard_map/reduce_scatter | solution.py:110
  (177 other events, 5015.4 us)
Sparse Core Ops, SparseCore 0:
  12.7 107.6 all-gather.22
  123.0 123.2 all-gather.26
  248.9 123.5 all-gather.28
  426.8 52.0 all-gather.32
  534.5 100.0 all-gather.30
  637.4 123.1 all-gather.34
  763.4 123.5 all-gather.36
  1049.5 85.9 all-reduce.36
  1138.9 60.9 reduce-scatter.86
  1203.6 59.8 reduce-scatter.84
  1267.1 59.8 reduce-scatter.82
  1330.5 59.8 reduce-scatter.80
  1393.9 60.9 reduce-scatter.78
  1458.1 60.8 reduce-scatter.76
  1523.1 61.0 reduce-scatter.74
  1587.6 60.9 reduce-scatter.72
  1652.9 67.3 reduce-scatter.54
  1724.9 67.3 reduce-scatter.52
  1796.8 67.2 reduce-scatter.50
  1868.0 67.3 reduce-scatter.48
  1939.3 117.3 reduce-scatter.46
  2060.8 117.5 reduce-scatter.44
  2182.2 117.5 reduce-scatter.42
  2303.7 117.4 reduce-scatter.40
  2425.3 148.2 reduce-scatter.62
  2577.2 148.0 reduce-scatter.60
  2729.2 148.3 reduce-scatter.70
  2881.2 148.4 reduce-scatter.68
  3033.7 148.0 reduce-scatter.58
  3185.3 147.9 reduce-scatter.56
  3337.4 148.3 reduce-scatter.66
  3489.4 148.4 reduce-scatter.64
  (3 shorter events, 148.8 us)
where the time goes:
time: 3670 us; the launch traced here: 3660 us
  waiting for transfers between devices  2950 us (80%)
  matrix products  246 us (7%)
  blocking collectives  190 us (5%)
  local copies, waits for them, and re-layouts  128 us (3%)
  other arithmetic  123 us (3%)
    reduce_scatter x4, waiting for transfers between devices, reduce_micro(): lax.psum_scatter(grad_down.astype(jnp.bfloat16), 'dp', scatter_dimension=...  593 us
    reduce_scatter x4, waiting for transfers between devices, reduce_micro(): lax.psum_scatter(grad_up.astype(jnp.bfloat16), 'dp', scatter_dimension=0,...  584 us
    reduce_scatter x4, waiting for transfers between devices, reduce_micro(): lax.psum_scatter(grad_qkv.astype(jnp.bfloat16), 'dp', scatter_dimension=1...  479 us
    unnamed x43, waiting for transfers between devices  343 us
    reduce_scatter x4, waiting for transfers between devices, reduce_micro(): lax.psum_scatter(grad_wout.astype(jnp.bfloat16), 'dp', scatter_dimension=...  284 us
    all_gather x2, waiting for transfers between devices, fetch_forward(): lax.all_gather(weights_down, 'dp', axis=1, tiled=True)  228 us
    all_gather x2, waiting for transfers between devices, fetch_forward(): lax.all_gather(weights_up, 'dp', axis=0, tiled=True)  178 us
    all_gather x2, waiting for transfers between devices, fetch_forward(): lax.all_gather(weights_qkv, 'dp', axis=1, tiled=True)  110 us
  transfers between devices with their start and end apart: 35, of which 33 were waited for; matrix products, arithmetic and copies ran while one was open for 9% of the time, Pallas kernels for 0%

commit v1 on v0

v1 whole, which is shorter than its diff:
```python
import math

import jax
import jax.numpy as jnp
import numpy as np
from jax import lax
from jax.experimental import pallas as pl
from jax.experimental.pallas import tpu as pltpu
from jax.sharding import Mesh
from jax.sharding import PartitionSpec as P

D = 2048
HEAD_DIM = 64
ROT = 32
FF = 8192
LAYERS = 2
STEP = 10
ROWS = 256
ZS = 4
HALF = 128
PAIR = 2 * HEAD_DIM

BETA_ONE = 0.9
BETA_TWO = 0.95
ADAM_EPS = 1e-08
DECAY = 0.1
NORM_EPS = 1e-05
MASKED = -1e30
BF = jnp.bfloat16
F32 = jnp.float32
VMEM_LIMIT = 58 * 2**20
SMALL_COST = pl.CostEstimate(flops=1024, bytes_accessed=1024, transcendentals=0)


def shift_z(array, step):
    return lax.ppermute(array, "z", [(i, (i + step) % ZS) for i in range(ZS)])


def swap(array, axis):
    return lax.ppermute(array, axis, [(0, 1), (1, 0)])


def dot_nt(left, right):
    return lax.dot_general(left, right, (((1,), (1,)), ((), ())), preferred_element_type=F32)


def dot_nn(left, right):
    return lax.dot_general(left, right, (((1,), (0,)), ((), ())), preferred_element_type=F32)


def dot_tn(left, right):
    return lax.dot_general(left, right, (((0,), (0,)), ((), ())), preferred_element_type=F32)


def turn(values, table):
    return (
        values * table[:, :PAIR]
        + pltpu.roll(values, PAIR - ROT // 2, 1) * table[:, PAIR : 2 * PAIR]
        + pltpu.roll(values, ROT // 2, 1) * table[:, 2 * PAIR :]
    )


def turn_back(grads, table):
    return (
        grads * table[:, :PAIR]
        - pltpu.roll(grads, PAIR - ROT // 2, 1) * table[:, PAIR : 2 * PAIR]
        - pltpu.roll(grads, ROT // 2, 1) * table[:, 2 * PAIR :]
    )


def low_lanes():
    return lax.broadcasted_iota(jnp.int32, (ROWS, PAIR), 1) < HEAD_DIM


def head_only(values, head):
    low_half = low_lanes()
    mine = low_half if head == 0 else jnp.logical_not(low_half)
    return jnp.where(mine, values, jnp.zeros_like(values))


def attend(queries, keys, values, mask):
    outs, logs = [], []
    for head in range(2):
        scores = dot_nt(head_only(queries, head), keys) + mask
        top = jnp.max(scores, -1, keepdims=True)
        exponent = jnp.exp(scores - top)
        total = jnp.sum(exponent, -1, keepdims=True)
        outs.append(dot_nn((exponent * (1.0 / total)).astype(BF), values))
        logs.append(jnp.broadcast_to(top + jnp.log(total), (ROWS, PAIR)))
    low_half = low_lanes()
    return jnp.where(low_half, *outs), jnp.where(low_half, *logs)


def attend_back(queries, keys, values, logs, grad, mask):
    grads = []
    for head in range(2):
        at = head * HEAD_DIM
        scores = dot_nt(head_only(queries, head), keys) + mask
        probs = jnp.exp(scores - logs[:, at : at + 1])
        grad_probs = dot_nt(head_only(grad, head), values)
        row_dot = jnp.sum(probs * grad_probs, -1, keepdims=True)
        grad_scores = (probs * (grad_probs - row_dot)).astype(BF)
        grads.append(
            (
                dot_nn(grad_scores, keys),
                dot_tn(grad_scores, queries),
                dot_tn(probs.astype(BF), grad),
            )
        )
    low_half = low_lanes()
    return [jnp.where(low_half, one, two) for one, two in zip(*grads)]


def cut_of(kind):
    return {"front": 3 * PAIR, "back": 2 * PAIR, "both": 6 * PAIR}[kind]


def nt_cols(left, segment):
    chunks, first, last = segment
    total, at = 0.0, 0
    for chunk in chunks:
        total = total + dot_nt(left[:, at : at + chunk.shape[1]], chunk[first:last])
        at += chunk.shape[1]
    return total


def nn_cols(left, segment):
    chunks, first, last = segment
    parts = [dot_nn(left, chunk[first:last]) for chunk in chunks]
    return parts[0] if len(parts) == 1 else jnp.concatenate(parts, 1)


def times_t(left, weights, x):
    near, on_y, on_x, far = weights
    half = left.shape[1] // 2
    lower, upper = left[:, :half], left[:, half:]
    if x == 0:
        return nt_cols(lower, near) + nt_cols(upper, on_y)
    parts = [nt_cols(upper, segment) for segment in far]
    return nt_cols(lower, on_x) + (parts[0] if len(parts) == 1 else jnp.concatenate(parts, 1))


def times(left, weights):
    near, on_y, on_x, far = weights
    n = near[2] - near[1]
    own, other = left[:, :n], left[:, n:]
    lower = nn_cols(own, near) + nn_cols(other, on_x)
    upper, at = nn_cols(own, on_y), 0
    for segment in far:
        rows = segment[2] - segment[1]
        upper = upper + nn_cols(other[:, at : at + rows], segment)
        at += rows
    return lower, upper


def bind(layout, refs):
    chunks = lambda part: (tuple(refs[at] for at in part[0]), part[1], part[2])
    near, on_y, on_x, far = layout
    return chunks(near), chunks(on_y), chunks(on_x), [chunks(part) for part in far]


def lanes_of(z_ref, k, y, dd):
    return pl.ds(pl.multiple_of(y * ZS * dd + (z_ref[0] - k + ZS) % ZS * dd, dd), dd)


def take_rows(z_ref, sources, relative, target=None):
    dd = relative.shape[1] // (2 * ZS)
    for slot in range(ZS):

        @pl.when(pl.program_id(0) == slot)
        def _():
            for core in range(2):
                source = sources[core * ZS + slot]
                rows = slice(core * HALF, (core + 1) * HALF)
                for y in range(2):
                    for k in range(ZS):
                        to = (y * ZS + k) * dd
                        relative[rows, to : to + dd] = source[:, lanes_of(z_ref, k, y, dd)]
                if target is not None:
                    target[core, 0] = source[...]


def put(ref, at, value):
    width = value.shape[1]
    ref[:, :, :, at : at + width] = value.astype(ref.dtype).reshape(2, 1, HALF, width)


def get(ref, at, width):
    return ref[:, :, :, at : at + width].reshape(ROWS, width)


def put_parts(z_ref, halves, own_ref, other_ref):
    for y, value in enumerate(halves):
        dd = value.shape[1] // ZS
        for k in range(ZS):
            lanes = lanes_of(z_ref, k, y, dd)
            part = value[:, k * dd : (k + 1) * dd].astype(BF)
            own_ref[0, :, lanes] = part[:HALF]
            other_ref[0, :, lanes] = part[HALF:]


def front_kernel(layouts, count, z_ref, *refs):
    rows, refs = refs[:8], refs[8:]
    weights, refs = refs[:count], refs[count:]
    fronts = bind(layouts[0], weights)
    bias_ref, table_ref, mask_ref, normed_ref, qkv_ref, log_ref, left_ref, slope_ref = refs[:8]
    relative = refs[-1]
    take_rows(z_ref, rows, relative, normed_ref)
    normed = relative[...]
    table = get(table_ref, 0, 3 * PAIR)
    n = fronts[0][2] - fronts[0][1]
    ffn_n = n - 3 * PAIR
    root = math.sqrt(2.0 / math.pi)
    for x in range(2):
        both = times_t(normed, fronts, x) + bias_ref[:, x * n : (x + 1) * n]
        gate = both[:, 3 * PAIR :]
        square = gate * gate
        bend = jnp.tanh(root * gate * (1.0 + 0.044715 * square))
        half_up = 0.5 + 0.5 * bend
        put(left_ref, x * (PAIR + ffn_n) + PAIR, gate * half_up)
        slope = half_up + (0.5 * gate) * (1.0 - bend * bend) * (
            root + (3.0 * 0.044715 * root) * square
        )
        put(slope_ref, x * ffn_n, slope)
        queries = turn(both[:, :PAIR], table).astype(BF) * jnp.asarray(HEAD_DIM**-0.5, BF)
        keys = turn(both[:, PAIR : 2 * PAIR], table).astype(BF)
        values = both[:, 2 * PAIR : 3 * PAIR].astype(BF)
        out, logs = attend(queries, keys, values, mask_ref[0])
        for which, value in enumerate((queries, keys, values)):
            put(qkv_ref, (3 * x + which) * PAIR, value)
        put(left_ref, x * (PAIR + ffn_n), out)
        put(log_ref, x * PAIR, logs)
    if len(layouts) > 1:
        backs = bind(layouts[1], weights)
        put_parts(z_ref, times(get(left_ref, 0, left_ref.shape[-1]), backs), *refs[8:10])


def slot_spec(width):
    return pl.BlockSpec((2, 1, HALF, width), lambda k: (0, k, 0, 0))


def fixed(shape):
    return pl.BlockSpec(
        shape, lambda *_: (0,) * len(shape), pipeline_mode=pl.Buffered(buffer_count=1)
    )


def slot_shape(width, kind):
    return jax.ShapeDtypeStruct((2, ZS, HALF, width), kind)


SMEM_SPEC = pl.BlockSpec(memory_space=pltpu.SMEM)
ANY_SPEC = pl.BlockSpec(memory_space=pl.ANY)
MASK_SPEC = pl.BlockSpec((1, ROWS, ROWS), lambda k: (k, 0, 0))
PART_SPEC = pl.BlockSpec((1, HALF, D), lambda k: (k, 0, 0))
PART_SHAPE = jax.ShapeDtypeStruct((ZS, HALF, D), BF)
ALL_ROWS = 2 * ZS * HALF
RELATIVE = pltpu.VMEM((ROWS, D), BF)


def front(z_array, rows, layouts, weights, bias, table, mask):
    n = bias.shape[1] // 2
    ffn_n = n - 3 * PAIR
    widths = [(D, BF), (6 * PAIR, BF), (2 * PAIR, F32), (2 * (PAIR + ffn_n), BF), (2 * ffn_n, BF)]
    parts = 2 * (len(layouts) - 1)
    return pl.pallas_call(
        lambda *refs: front_kernel(layouts, len(weights), *refs),
        grid=(ZS,),
        in_specs=[SMEM_SPEC]
        + [fixed(a.shape) for a in (*rows, *weights, bias)]
        + [slot_spec(3 * PAIR), MASK_SPEC],
        out_specs=[slot_spec(width) for width, _ in widths] + [PART_SPEC] * parts,
        out_shape=[slot_shape(*pair) for pair in widths] + [PART_SHAPE] * parts,
        scratch_shapes=[RELATIVE],
        compiler_params=pltpu.CompilerParams(vmem_limit_bytes=VMEM_LIMIT),
        cost_estimate=SMALL_COST,
        name="block_front",
    )(z_array, *rows, *weights, bias, table, mask)


def back_kernel(layout, z_ref, left_ref, *refs):
    left = get(left_ref, 0, left_ref.shape[-1])
    put_parts(z_ref, times(left, bind(layout, refs[:-2])), *refs[-2:])


def back(z_array, left, layout, weights):
    return pl.pallas_call(
        lambda *refs: back_kernel(layout, *refs),
        grid=(ZS,),
        in_specs=[SMEM_SPEC, slot_spec(left.shape[-1])] + [fixed(a.shape) for a in weights],
        out_specs=[PART_SPEC] * 2,
        out_shape=[PART_SHAPE] * 2,
        compiler_params=pltpu.CompilerParams(vmem_limit_bytes=VMEM_LIMIT),
        cost_estimate=SMALL_COST,
        name="block_back",
    )(z_array, left, *weights)


def reverse_kernel(layouts, count, z_ref, *refs):
    rows, refs = refs[:8], refs[8:]
    weights, refs = refs[:count], refs[count:]
    fronts, backs = [bind(layout, weights) for layout in layouts]
    slope_ref, qkv_ref, log_ref, table_ref, mask_ref = refs[:5]
    left_ref, own_ref, other_ref, sums_ref, relative = refs[5:]
    take_rows(z_ref, rows, relative)
    grad = relative[...]
    table = get(table_ref, 0, 3 * PAIR)
    n = fronts[0][2] - fronts[0][1]
    ffn_n = n - 3 * PAIR
    for x in range(2):
        both = times_t(grad, backs, x)
        gate = both[:, PAIR:] * get(slope_ref, x * ffn_n, ffn_n).astype(F32)
        put(left_ref, x * n + 3 * PAIR, gate)
        queries, keys, values = [get(qkv_ref, (3 * x + which) * PAIR, PAIR) for which in range(3)]
        grads = attend_back(
            queries, keys, values, get(log_ref, x * PAIR, PAIR), both[:, :PAIR].astype(BF), mask_ref[0]
        )
        grads = [turn_back(grads[0] * HEAD_DIM**-0.5, table), turn_back(grads[1], table), grads[2]]
        for which, value in enumerate(grads):
            put(left_ref, x * n + which * PAIR, value)
    left = get(left_ref, 0, left_ref.shape[-1])
    put_parts(z_ref, times(left, fronts), own_ref, other_ref)
    sums = jnp.sum(left.astype(F32), 0, keepdims=True)

    @pl.when(pl.program_id(0) == 0)
    def _():
        sums_ref[...] = sums

    @pl.when(pl.program_id(0) > 0)
    def _():
        sums_ref[...] += sums


def reverse(z_array, rows, layouts, weights, slope, qkv, logs, table, mask):
    _, first, last = layouts[0][0]
    n = last - first
    return pl.pallas_call(
        lambda *refs: reverse_kernel(layouts, len(weights), *refs),
        grid=(ZS,),
        in_specs=[SMEM_SPEC]
        + [fixed(a.shape) for a in (*rows, *weights)]
        + [slot_spec(a.shape[-1]) for a in (slope, qkv, logs, table)]
        + [MASK_SPEC],
        out_specs=[slot_spec(2 * n), PART_SPEC, PART_SPEC]
        + [pl.BlockSpec((1, 2 * n), lambda k: (0, 0))],
        out_shape=[slot_shape(2 * n, BF), PART_SHAPE, PART_SHAPE]
        + [jax.ShapeDtypeStruct((1, 2 * n), F32)],
        scratch_shapes=[RELATIVE],
        compiler_params=pltpu.CompilerParams(vmem_limit_bytes=VMEM_LIMIT),
        cost_estimate=SMALL_COST,
        name="block_reverse",
    )(z_array, *rows, *weights, slope, qkv, logs, table, mask)


def centred(hidden):
    centre = hidden - jnp.mean(hidden, -1, keepdims=True)
    rstd = lax.rsqrt(jnp.mean(centre * centre, -1, keepdims=True) + NORM_EPS)
    return centre * rstd, rstd


def model_row(ref, layer, which):
    return ref[layer * 4 + which : layer * 4 + which + 1].astype(F32)


def add_parts(refs):
    total = refs[0][...]
    for ref in refs[1:]:
        total = total + ref[...].astype(F32)
    return total


def norm_kernel(layer, final, hidden_ref, *refs):
    hidden = hidden_ref[...].astype(F32)
    parts, (model_ref, *outs) = refs[: len(refs) - 2 - (not final)], refs[len(refs) - 2 - (not final) :]
    if parts:
        bias = model_row(model_ref, layer - 1, 2) + model_row(model_ref, layer - 1, 3)
        hidden = hidden + add_parts(parts) + bias
    outs[0][...] = hidden.astype(outs[0].dtype)
    if not final:
        xhat, _ = centred(hidden)
        outs[1][...] = (
            xhat * model_row(model_ref, layer, 0) + model_row(model_ref, layer, 1)
        ).astype(BF)


def norm(layer, final, hidden, parts, model_vec):
    shapes = [jax.ShapeDtypeStruct((HALF, D), kind) for kind in ((BF,) if final else (F32, BF))]
    return pl.pallas_call(
        lambda *refs: norm_kernel(layer, final, *refs),
        out_shape=shapes,
        compiler_params=pltpu.CompilerParams(vmem_limit_bytes=VMEM_LIMIT),
        cost_estimate=SMALL_COST,
        name="norm",
    )(hidden, *parts, model_vec)


def norm_back_kernel(layer, count, grad_ref, hidden_ref, *refs):
    parts, model_ref, (next_ref, low_ref, sums_ref) = refs[:count], refs[count], refs[-3:]
    grad_next = grad_ref[...].astype(F32)
    grad_normed = add_parts(parts)
    xhat, rstd = centred(hidden_ref[...].astype(F32))
    sums_ref[...] = jnp.concatenate(
        [
            jnp.sum(grad_normed * xhat, 0, keepdims=True),
            jnp.sum(grad_normed, 0, keepdims=True),
            jnp.sum(grad_next, 0, keepdims=True),
            jnp.zeros((5, grad_next.shape[1]), F32),
        ],
        0,
    )
    scaled = grad_normed * model_row(model_ref, layer, 0)
    grad = grad_next + rstd * (
        scaled
        - jnp.mean(scaled, -1, keepdims=True)
        - xhat * jnp.mean(scaled * xhat, -1, keepdims=True)
    )
    next_ref[...] = grad
    low_ref[...] = grad.astype(BF)


def norm_back(layer, grad_next, hidden, parts, model_vec, earlier=()):
    vmem = pl.BlockSpec(memory_space=pltpu.VMEM)
    return pl.pallas_call(
        lambda *refs: norm_back_kernel(layer, len(parts), *refs),
        in_specs=[vmem] * (3 + len(parts)) + [ANY_SPEC] * len(earlier),
        out_shape=[
            jax.ShapeDtypeStruct((HALF, D), F32),
            jax.ShapeDtypeStruct((HALF, D), BF),
            jax.ShapeDtypeStruct((8, D), F32),
        ],
        compiler_params=pltpu.CompilerParams(vmem_limit_bytes=VMEM_LIMIT),
        cost_estimate=SMALL_COST,
        name="norm_back",
    )(grad_next, hidden, *parts, model_vec, *earlier)


def fold_kernel(count, z_ref, own_ref, other_ref, *refs):
    outs = refs[len(refs) - count :]
    totals = [own_ref[k].astype(F32) + other_ref[k].astype(F32) for k in range(ZS)]
    for k in range(ZS):
        outs[k][...] = totals[k].astype(outs[k].dtype)
    if len(outs) > ZS:
        outs[ZS][...] = jnp.where(z_ref[0] == 0, totals[1], totals[3]).astype(BF)


def fold(z_array, own, other, kinds, earlier=()):
    return pl.pallas_call(
        lambda *refs: fold_kernel(len(kinds), *refs),
        in_specs=[pl.BlockSpec(memory_space=pltpu.SMEM)]
        + [pl.BlockSpec(memory_space=pltpu.VMEM)] * 2
        + [ANY_SPEC] * len(earlier),
        out_shape=[jax.ShapeDtypeStruct((HALF, D), kind) for kind in kinds],
        compiler_params=pltpu.CompilerParams(vmem_limit_bytes=VMEM_LIMIT),
        cost_estimate=SMALL_COST,
        name="fold",
    )(z_array, own, other, *earlier)


class Place:
    def __init__(self, ny):
        self.ny = ny
        self.z = lax.axis_index("z")
        self.y = lax.axis_index("y")
        self.x = lax.axis_index("x")
        self.c = lax.axis_index("c")

    def own_first(self, lower, upper, index, axis):
        mine = jnp.where(index == 0, lower, upper)
        other = jnp.where(index == 0, upper, lower)
        return jnp.concatenate([mine, other], axis)

    def to_local(self, array):
        parts = array.reshape(*array.shape[:-1], ZS, self.ny, -1)
        parts = jnp.swapaxes(parts, -2, -3).reshape(*array.shape[:-1], 2, -1)
        lower, upper = parts[..., 0, :], parts[..., 1, :]
        if self.ny == 2:
            return self.own_first(lower, upper, self.y, -1)
        return jnp.concatenate([lower, upper], -1)

    def from_local(self, array):
        half = array.shape[-1] // 2
        lower, upper = array[..., :half], array[..., half:]
        if self.ny == 2:
            array = self.own_first(lower, upper, self.y, -1)
        parts = array.reshape(*array.shape[:-1], self.ny, ZS, -1)
        return jnp.swapaxes(parts, -2, -3).reshape(*array.shape)

    def y_columns(self, array):
        if self.ny == 2:
            return jnp.concatenate([array, swap(array, "y")], -1)
        return lax.all_gather(array, "y", axis=array.ndim - 1, tiled=True)

    def y_place(self, array):
        if self.ny == 2:
            other = swap(array, "y")
            return self.own_first(array, other, self.y, -1)
        return lax.all_gather(array, "y", axis=array.ndim - 1, tiled=True)


def after(array, *earlier):
    return lax.optimization_barrier((array, *earlier))[0]


def gather_z(array):
    return [array] + [shift_z(array, k) for k in range(1, ZS)]


def line_z(array, pairs):
    return lax.ppermute(array, "z", pairs)


def gather_rows(rows, *earlier):
    mine = gather_z(rows)
    return mine + [swap(after(part, *earlier) if earlier else part, "c") for part in mine]


def gather_line(place, rows, *deadlines, second=()):
    far = swap(rows, "c")
    up_one = line_z(rows, [(0, 1), (1, 2), (2, 3)])
    down_one = line_z(rows, [(3, 2), (2, 1), (1, 0)])
    up_one, down_one = after(up_one, far, *second), after(down_one, *second)
    up_two = line_z(up_one, [(1, 2), (2, 3)])
    down_two = line_z(down_one, [(2, 1), (1, 0)])
    two = up_two + down_two
    if deadlines:
        two = after(two, *deadlines)
    far_two = swap(two, "c")
    end = after(line_z(two, [(2, 3), (1, 0)]), far_two)
    one = jnp.where(place.z == 0, end, up_one)
    three = jnp.where(place.z == ZS - 1, end, down_one)
    return [rows, one, two, three, far, swap(one, "c"), far_two, swap(three, "c")]


def scatter_rows(z_array, parts, *earlier):
    own, other = parts
    if earlier:
        other = after(other, *earlier)
    terms = fold(z_array, own, swap(other, "c"), (F32, BF, BF, BF))
    return [terms[0]] + [shift_z(terms[k], -k) for k in range(1, ZS)]


def scatter_line(z_array, parts, first=(), then=(), mid=(), last=(), tokens=()):
    own, other = parts
    if first:
        other = after(other, *first)
    other = swap(other, "c")
    if then:
        other = after(other, *then)
    own, one, two, three, end = fold(z_array, own, other, (F32, F32, F32, F32, BF), tokens)
    end = line_z(end, [(0, 1), (3, 2)])
    two = (two + end.astype(F32)).astype(BF)
    if mid:
        two = after(two, *mid)
    down_two = line_z(two, [(2, 1), (3, 2)])
    up_two = line_z(two, [(1, 2), (0, 1)])
    one = (one + down_two.astype(F32)).astype(BF)
    three = (three + up_two.astype(F32)).astype(BF)
    if last:
        one, three = after(one, *last), after(three, *last)
    down_one = line_z(one, [(1, 0), (2, 1), (3, 2)])
    up_one = line_z(three, [(0, 1), (1, 2), (2, 3)])
    return [own, down_one, up_one]


def whole_spec(shape):
    return pl.BlockSpec(shape, lambda *_: (0,) * len(shape))


def quarter(z_ref, k, sign):
    return (z_ref[0] + sign * k + ZS) % ZS


def weight_specs(kind, layer, dd, heads_n, ffn_n, sign):
    fronts = [
        pl.BlockSpec((1, 3, dd, heads_n), lambda k, z: (layer, 0, 0, quarter(z, k, sign))),
        pl.BlockSpec((1, dd, ffn_n), lambda k, z: (layer, 0, quarter(z, k, sign))),
    ]
    backs = [
        pl.BlockSpec((1, heads_n, dd), lambda k, z: (layer, quarter(z, k, sign), 0)),
        pl.BlockSpec((1, ffn_n, dd), lambda k, z: (layer, quarter(z, k, sign), 0)),
    ]
    return {"front": fronts, "back": backs, "both": fronts + backs}[kind]


def pack_kernel(kind, z_ref, *refs):
    refs, outs = refs[:-ZS], refs[-ZS:]
    parts = []
    if kind != "back":
        parts += [refs[0][0, which].T for which in range(3)] + [refs[1][0].T]
    if kind != "front":
        parts += [refs[-2][0], refs[-1][0]]
    block = jnp.concatenate(parts, 0).astype(BF)
    for k in range(ZS):

        @pl.when(pl.program_id(0) == k)
        def _():
            outs[k][...] = block


def pack(kind, layer, z_array, arrays, dd, heads_n, ffn_n):
    n = {"front": 3 * heads_n + ffn_n, "back": heads_n + ffn_n, "both": 4 * heads_n + 2 * ffn_n}[kind]
    return pl.pallas_call(
        lambda *refs: pack_kernel(kind, *refs),
        grid_spec=pltpu.PrefetchScalarGridSpec(
            num_scalar_prefetch=1,
            grid=(ZS,),
            in_specs=weight_specs(kind, layer, dd, heads_n, ffn_n, 1),
            out_specs=[whole_spec((n, dd))] * ZS,
        ),
        out_shape=[jax.ShapeDtypeStruct((n, dd), BF)] * ZS,
        compiler_params=pltpu.CompilerParams(vmem_limit_bytes=VMEM_LIMIT),
        cost_estimate=pl.CostEstimate(
            flops=0, bytes_accessed=6 * ZS * n * dd, transcendentals=0
        ),
        name="pack_" + kind,
    )(z_array, *arrays)


def stack_kernel(*refs):
    dd = refs[0].shape[1]
    for at, ref in enumerate(refs[:-1]):
        refs[-1][:, at * dd : (at + 1) * dd] = ref[...]


def stack(pieces):
    n, dd = pieces[0].shape
    if dd % 128:
        return jnp.concatenate(pieces, 1)
    return pl.pallas_call(
        stack_kernel,
        out_shape=jax.ShapeDtypeStruct((n, len(pieces) * dd), BF),
        compiler_params=pltpu.CompilerParams(vmem_limit_bytes=VMEM_LIMIT),
        cost_estimate=SMALL_COST,
        name="stack",
    )(*pieces)


def stack_rows_kernel(*refs):
    for at, ref in enumerate(refs[:-1]):
        refs[-1][at * HALF : (at + 1) * HALF] = ref[...]


def stack_rows(rows):
    return pl.pallas_call(
        stack_rows_kernel,
        out_shape=jax.ShapeDtypeStruct((len(rows) * HALF, D), BF),
        compiler_params=pltpu.CompilerParams(vmem_limit_bytes=VMEM_LIMIT),
        cost_estimate=SMALL_COST,
        name="stack_rows",
    )(*rows)


def spread_xy(kind, near, *earlier):
    cut = cut_of(kind)
    on_x, on_y = swap(near, "x"), swap(near, "y")
    one, two = on_x[:cut], on_y[cut:]
    if earlier:
        one, two = after(one, *earlier), after(two, *earlier)
    return near, on_y, on_x, swap(one, "y"), swap(two, "x")


def weight_grads(kind, left, right, cut):
    n, half = left.shape[1] // 2, right.shape[1] // 2
    cut = min(cut, n)
    lower, upper = right[:, :half], right[:, half:]
    own, other = left[:, :n], left[:, n:]
    return [
        dot_tn(one, two).astype(BF) if one.shape[1] else jnp.zeros((0, half), BF)
        for one, two in (
            (other[:, :cut], upper),
            (other[:, cut:], upper),
            (own, upper),
            (other, lower),
            (own, lower),
        )
    ]


def bump_kernel(count, *refs):
    parts, (one_ref, two_ref), (y_ref, x_ref) = refs[: 2 * count], refs[2 * count :][:2], refs[-2:]
    at = 0
    for on_y, on_x in zip(parts[:count], parts[count:]):
        rows = slice(at, at + on_y.shape[0])
        y_ref[rows] = on_y[...]
        x_ref[rows] = on_x[...]
        at += on_y.shape[0]
    cut = one_ref.shape[0]
    y_ref[:cut] = add_low(y_ref[:cut], one_ref[...])
    x_ref[cut:] = add_low(x_ref[cut:], two_ref[...])


def bump(on_y, on_x, far_one, far_two, earlier=()):
    n = sum(part.shape[0] for part in on_y)
    vmem = pl.BlockSpec(memory_space=pltpu.VMEM)
    return pl.pallas_call(
        lambda *refs: bump_kernel(len(on_y), *refs),
        in_specs=[vmem] * (2 * len(on_y) + 2) + [ANY_SPEC] * len(earlier),
        out_shape=[jax.ShapeDtypeStruct((n, on_y[0].shape[1]), BF)] * 2,
        compiler_params=pltpu.CompilerParams(vmem_limit_bytes=VMEM_LIMIT),
        cost_estimate=SMALL_COST,
        name="bump",
    )(*on_y, *on_x, far_one, far_two, *earlier)


def split_kernel(count, z_ref, *refs):
    near, (y_ref, x_ref, *_), outs = refs[:count], refs[count:], refs[-ZS:]
    value = jnp.concatenate([part[...] for part in near], 0).astype(F32)
    value = (value + y_ref[...].astype(F32) + x_ref[...].astype(F32)).astype(BF)
    for k in range(ZS):

        @pl.when(pl.program_id(0) == k)
        def _():
            outs[k][...] = value


def split(z_array, near, from_y, from_x, earlier=()):
    n, width = from_y.shape
    dd = width // ZS
    return pl.pallas_call(
        lambda *refs: split_kernel(len(near), *refs),
        grid_spec=pltpu.PrefetchScalarGridSpec(
            num_scalar_prefetch=1,
            grid=(ZS,),
            in_specs=[
                pl.BlockSpec((part.shape[0], dd), lambda k, z: (0, quarter(z, k, 1)))
                for part in (*near, from_y, from_x)
            ]
            + [ANY_SPEC] * len(earlier),
            out_specs=[whole_spec((n, dd))] * ZS,
        ),
        out_shape=[jax.ShapeDtypeStruct((n, dd), BF)] * ZS,
        compiler_params=pltpu.CompilerParams(vmem_limit_bytes=VMEM_LIMIT),
        cost_estimate=SMALL_COST,
        name="split",
    )(z_array, *near, from_y, from_x, *earlier)


def add_low(left, right):
    return (left.astype(F32) + right.astype(F32)).astype(BF)


def sum_plain(place, grads):
    own = jnp.concatenate([jnp.concatenate([g[4], g[2]], 1) for g in grads], 0)
    other = [jnp.concatenate([g[3], jnp.concatenate([g[0], g[1]], 0)], 1) for g in grads]
    both = add_low(own, swap(jnp.concatenate(other, 0), "x"))
    total = lax.psum_scatter(both, "y", scatter_dimension=1, tiled=True)
    n, width = total.shape
    dd = width // ZS
    return [lax.dynamic_slice(total, (0, (place.z + k) % ZS * dd), (n, dd)) for k in range(ZS)]


def adam_kernel(kind, heads_n, ffn_n, offset, rates, z_ref, *refs):
    pieces, states, outs = refs[:ZS], refs[ZS : ZS + 6], refs[-9:-1]
    refs[-1][...] = jnp.zeros_like(refs[-1])
    for k in range(ZS):

        @pl.when(pl.program_id(0) == k)
        def _():
            split = (3 if kind == "front" else 1) * heads_n
            piece = pieces[k][offset : offset + split + ffn_n]
            if kind == "front":
                grads = [
                    jnp.stack(
                        [
                            piece[which * heads_n : (which + 1) * heads_n].astype(F32).T
                            for which in range(3)
                        ]
                    )[None],
                    piece[split:].astype(F32).T[None],
                ]
            else:
                grads = [piece[:split].astype(F32)[None], piece[split:].astype(F32)[None]]
            for at, grad in enumerate(grads):
                weight, first, second = [ref[...] for ref in states[at * 3 : at * 3 + 3]]
                outs[at * 4][...] = grad
                new = adamw(weight, grad, first, second, rates[at], DECAY)
                for ref, value in zip(outs[at * 4 + 1 : at * 4 + 4], new):
                    ref[...] = value


def adam(kind, layer, z_array, pieces, offset, states, rates, earlier, tokens, heads_n, ffn_n):
    n, dd = pieces[0].shape
    first, second = weight_specs(kind, layer, dd, heads_n, ffn_n, -1)
    shapes = [jax.ShapeDtypeStruct(states[at].shape, F32) for at in (0, 3) for _ in range(4)]
    earlier = list(earlier or [])
    return pl.pallas_call(
        lambda *refs: adam_kernel(kind, heads_n, ffn_n, offset, rates, *refs),
        grid_spec=pltpu.PrefetchScalarGridSpec(
            num_scalar_prefetch=1,
            grid=(ZS,),
            in_specs=[whole_spec((n, dd))] * ZS
            + [first] * 3
            + [second] * 3
            + [ANY_SPEC] * (len(earlier) + len(tokens)),
            out_specs=[first] * 4 + [second] * 4 + [whole_spec((8, 128))],
        ),
        out_shape=shapes + [jax.ShapeDtypeStruct((8, 128), F32)],
        input_output_aliases={1 + ZS + 6 + at: at for at in range(len(earlier))},
        compiler_params=pltpu.CompilerParams(vmem_limit_bytes=VMEM_LIMIT),
        cost_estimate=SMALL_COST,
        name="adam_" + kind,
    )(z_array, *pieces, *states, *earlier, *tokens)


def tables(positions):
    half = ROT // 2
    places = jnp.maximum(positions, 0).astype(F32)
    frequency = 10000.0 ** (-(2.0 / ROT) * jnp.arange(half).astype(F32))
    angles = places[..., None] * frequency
    both = jnp.concatenate([jnp.cos(angles), jnp.sin(angles)], -1)
    pick = np.zeros((ROT, 3, 2, HEAD_DIM), np.float32)
    for at in range(half):
        pick[at, 0, :, at] = pick[at, 0, :, half + at] = 1.0
        pick[half + at, 1, :, at] = -1.0
        pick[half + at, 2, :, half + at] = 1.0
    rest = np.zeros((3, 2, HEAD_DIM), np.float32)
    rest[0, :, ROT:] = 1.0
    table = jnp.dot(both, pick.reshape(ROT, -1), precision=lax.Precision.HIGHEST)
    return table + rest.reshape(-1)


def adamw(weight, grad, first, second, rate, decay):
    first_new = BETA_ONE * first + (1.0 - BETA_ONE) * grad
    second_new = BETA_TWO * second + (1.0 - BETA_TWO) * grad * grad
    first_hat = first_new / (1.0 - BETA_ONE**STEP)
    second_hat = second_new / (1.0 - BETA_TWO**STEP)
    weight_new = weight - rate * (first_hat / (jnp.sqrt(second_hat) + ADAM_EPS) + decay * weight)
    return (first_new, second_new, weight_new)


def source_lane(at, y):
    return (at % ZS) * 2 + (at // ZS + y) % 2


def take_kernel(place_ref, rows_ref, grads_ref, live_ref, start_ref, low_ref):
    dd = D // (2 * ZS)
    for at in range(2 * ZS):
        lanes = pl.ds(pl.multiple_of(source_lane(at, place_ref[1]) * dd, 128), dd)
        to = slice(at * dd, (at + 1) * dd)
        start_ref[:, to] = rows_ref[:, lanes]
        low_ref[:, to] = (grads_ref[:, lanes].astype(F32) * live_ref[...]).astype(BF)


def take(place, activations, cotangent, live):
    m = place.x * 2 + place.c
    if place.ny != 2:
        mine = [
            place.to_local(lax.dynamic_slice_in_dim(array, m * HALF, HALF, 0))
            for array in (activations, cotangent)
        ]
        return mine[0], (mine[1].astype(F32) * live).astype(BF)
    where = jnp.stack([m, place.y]).astype(jnp.int32)
    return pl.pallas_call(
        take_kernel,
        grid_spec=pltpu.PrefetchScalarGridSpec(
            num_scalar_prefetch=1,
            grid=(1,),
            in_specs=[pl.BlockSpec((HALF, D), lambda at, ref: (ref[0], 0))] * 2
            + [pl.BlockSpec((HALF, 1), lambda at, ref: (0, 0))],
            out_specs=[pl.BlockSpec((HALF, D), lambda at, ref: (0, 0))] * 2,
        ),
        out_shape=[jax.ShapeDtypeStruct((HALF, D), BF)] * 2,
        cost_estimate=pl.CostEstimate(flops=0, bytes_accessed=8 * HALF * D, transcendentals=0),
        name="take",
    )(where, activations, cotangent, live)


def give_kernel(place_ref, *refs):
    dd = D // (2 * ZS)
    for block in range(4):

        @pl.when(pl.program_id(0) == block)
        def _():
            for at in range(2 * ZS):
                lanes = pl.ds(pl.multiple_of(source_lane(at, place_ref[2]) * dd, 128), dd)
                refs[-1][:, lanes] = refs[block][:, at * dd : (at + 1) * dd].astype(F32)


def give(place, blocks):
    where = jnp.stack([place.x, place.c, place.y]).astype(jnp.int32)
    if place.ny != 2:
        result = jnp.zeros((4 * HALF, D), F32)
        for at, block in enumerate(blocks):
            row = ((place.x + at // 2) % 2) * 2 + (place.c + at % 2) % 2
            result = lax.dynamic_update_slice(
                result, place.from_local(block).astype(F32), (row * HALF, 0)
            )
        return result

    def target(at, ref):
        return (((ref[0] + at // 2) % 2) * 2 + (ref[1] + at % 2) % 2, 0)

    return pl.pallas_call(
        give_kernel,
        grid_spec=pltpu.PrefetchScalarGridSpec(
            num_scalar_prefetch=1,
            grid=(4,),
            in_specs=[whole_spec((HALF, D))] * 4,
            out_specs=pl.BlockSpec((HALF, D), target),
        ),
        out_shape=jax.ShapeDtypeStruct((4 * HALF, D), F32),
        compiler_params=pltpu.CompilerParams(vmem_limit_bytes=VMEM_LIMIT),
        cost_estimate=SMALL_COST,
        name="give",
    )(where, *blocks)


def per_device(
    ny,
    activations,
    cotangent,
    positions,
    w_qkv,
    w_out,
    w_up,
    w_down,
    vec_model,
    vec_head,
    vec_ffn,
    first_qkv,
    first_out,
    first_up,
    first_down,
    first_model,
    first_head,
    first_ffn,
    second_qkv,
    second_out,
    second_up,
    second_down,
    second_model,
    second_head,
    second_ffn,
):
    place = Place(ny)
    dd = w_up.shape[1]
    heads_n = w_qkv.shape[3] // ZS
    ffn_n = w_up.shape[2] // ZS
    sizes = (dd, heads_n, ffn_n)
    z_array = place.z.reshape(1).astype(jnp.int32)

    model_own = vec_model.astype(BF).reshape(LAYERS * 4, dd)
    head_own, ffn_own = vec_head.astype(BF), vec_ffn.astype(BF)
    if ny == 2:
        first = jnp.concatenate(
            [model_own.reshape(-1), head_own.reshape(-1), ffn_own.reshape(-1)]
        )
        far = swap(first, "y")
        ends = [model_own.size, model_own.size + head_own.size, first.size]
        model_far, head_far, ffn_far = [
            far[start:end].reshape(own.shape)
            for start, end, own in zip([0] + ends, ends, (model_own, head_own, ffn_own))
        ]
        model_y = jnp.stack([model_own, model_far], 1)
        head_y = place.own_first(head_own, head_far, place.y, -1)
        ffn_y = place.own_first(ffn_own, ffn_far, place.y, -1)
    else:
        model_y = lax.all_gather(model_own, "y", axis=1)
        head_y = lax.all_gather(head_own, "y", axis=2, tiled=True)
        ffn_y = lax.all_gather(ffn_own, "y", axis=1, tiled=True)
    slim = jnp.concatenate([head_y.reshape(LAYERS, -1), ffn_y], 1)
    places_x = lax.dynamic_slice_in_dim(positions, place.x * ROWS, ROWS)
    places_x = place.own_first(places_x[:HALF], places_x[HALF:], place.c, 0)
    if ny == 2:
        pieces_front = pack("front", 0, z_array, (w_qkv, w_up), *sizes)
        slim = after(slim, *pieces_front)
    mine = jnp.concatenate([model_y.reshape(-1), places_x.astype(BF)])
    slim_x = swap(slim, "x")
    bias = jnp.concatenate([slim, slim_x], 1).astype(F32)
    packed = jnp.stack(
        [mine] + [lax.ppermute(mine, "z", [(i, i ^ k) for i in range(ZS)]) for k in range(1, ZS)]
    )
    if ny == 2:
        pieces_front = [after(piece, packed, slim_x) for piece in pieces_front]
        came_front = [pieces_front[0]] + [shift_z(pieces_front[k], k) for k in range(1, ZS)]
        on_x, on_y = swap(pieces_front[0], "x"), swap(pieces_front[0], "y")
        later_z = after(z_array, on_x, on_y)
        pieces_next = pack("both", 1, later_z, (w_qkv, w_up, w_out, w_down), *sizes)
        pieces_back = pack("back", 0, later_z, (w_out, w_down), *sizes)
        cut = cut_of("front")
        ready = *pieces_next, *pieces_back
        far_one, far_two = after(on_x[:cut], *ready), after(on_y[cut:], *ready)
        own_front = pieces_front[0], on_y, on_x, swap(far_one, "y"), swap(far_two, "x")
    everyone = jnp.arange(ZS, dtype=jnp.int32)
    by_z = jnp.take(packed, everyone ^ place.z, axis=0)
    model_vec = by_z[:, : LAYERS * 4 * ny * dd].reshape(ZS, LAYERS * 4, ny, dd)
    model_vec = model_vec.transpose(1, 2, 0, 3).reshape(LAYERS * 4, D)
    places = jnp.take(by_z[:, LAYERS * 4 * ny * dd :], (place.z - everyone) % ZS, axis=0)
    places = places.astype(F32).astype(jnp.int32)

    order = (jnp.arange(ROWS, dtype=jnp.int32) + place.c * HALF) % ROWS
    starts = order - jnp.maximum(places, 0)
    seen = (order[None, None, :] <= order[None, :, None]) & (
        order[None, None, :] >= starts[:, :, None]
    )
    mask = jnp.where(seen, 0.0, MASKED).astype(F32)
    table = tables(jnp.swapaxes(places.reshape(ZS, 2, HALF), 0, 1))

    mine = place.x * ROWS + place.c * HALF
    live = (lax.dynamic_slice_in_dim(positions, mine, HALF) >= 0).astype(F32)[:, None]
    if ny == 2:
        live = after(live, *own_front[1:3])
    start, last_low = take(place, activations, cotangent, live)

    kernel_z = z_array if ny == 2 else jnp.zeros_like(z_array)
    n_front, n_back = 3 * heads_n + ffn_n, heads_n + ffn_n
    n_both = n_front + n_back
    arrays = {"front": (w_qkv, w_up), "back": (w_out, w_down), "both": (w_qkv, w_up, w_out, w_down)}

    def packed_pieces(kind, layer):
        return pack(kind, layer, z_array, arrays[kind], *sizes)

    def send_z(pieces, *earlier):
        if earlier:
            pieces = [pieces[0]] + [after(piece, *earlier) for piece in pieces[1:]]
        return [pieces[0]] + [shift_z(pieces[k], k) for k in range(1, ZS)]

    def spread_plain(kind, layer):
        pieces = send_z(packed_pieces(kind, layer))
        n = pieces[0].shape[0]
        joined = jnp.zeros((n, ZS * dd), BF)
        for k, piece in enumerate(pieces):
            joined = lax.dynamic_update_slice(joined, piece, (0, (place.z - k) % ZS * dd))
        own = place.y_columns(joined).reshape(n, 2, ZS, -1)
        own = jnp.concatenate([own[:, :, :1], own[:, :, :0:-1]], 2).reshape(n, D)
        other = swap(own, "x")
        cut, half = cut_of(kind), D // 2
        return own[:, :half], own[:, half:], other[:, :half], other[:cut, half:], other[cut:, half:]

    def layout_of(kind, chunks, first=0):
        n, cut = {"front": n_front, "back": n_back}[kind], cut_of(kind)
        ids = [tuple(5 * c + at for c in range(chunks)) for at in range(5)]
        far = [(ids[3], 0, cut), (ids[4], 0, n - cut)]
        return (*((ids[at], 0, n) for at in range(3)), far)

    both_cut = cut_of("both")
    ids = [(at,) for at in range(5)]
    merged = (
        (*((ids[at], 0, n_front) for at in range(3)), [(ids[3], 0, both_cut), (ids[4], 0, n_front - both_cut)]),
        (*((ids[at], n_front, n_both) for at in range(3)), [(ids[4], n_front - both_cut, n_both - both_cut)]),
    )

    hidden, normed = norm(0, False, start, (), model_vec)
    if ny == 2:
        came_front[1] = after(came_front[1], start)
        came_back = send_z(pieces_back, *came_front[1:])
        rest_front = list(
            spread_xy("front", stack([after(came_front[1], *own_front[3:]), *came_front[2:]]))
        )
        fronts = [*own_front, *rest_front]
        rest_front[1] = after(rest_front[1], table, mask)
        near_back = stack([came_back[0], after(came_back[1], *rest_front[3:]), *came_back[2:]])
        on_x, on_y = swap(near_back, "x"), swap(near_back, "y")
        rows = gather_line(
            place, after(normed, *came_back[1:]), near_back, second=rest_front[1:3]
        )
        came_next = send_z(pieces_next, *rows[1:4])
    else:
        rows = gather_line(place, normed)
        fronts = spread_plain("front", 0)
        backs = spread_plain("back", 0)
    layouts = layout_of("front", 2 if ny == 2 else 1), layout_of("back", 1)
    shift = len(fronts)
    move = lambda part: (tuple(at + shift for at in part[0]), *part[1:])
    joint = layouts[0], (*map(move, layouts[1][:3]), [move(part) for part in layouts[1][3]])

    normed, qkv, logs, left, slope = front(
        kernel_z, rows, layouts[:1], fronts, bias[0:1], table, mask
    )
    kept = [(hidden, normed, qkv, logs, left, slope)]
    if ny == 2:
        cut, ready = cut_of("back"), (left, came_next[1], came_next[3])
        far_one, far_two = after(on_x[:cut], *ready), after(on_y[cut:], *ready)
        backs = near_back, on_y, on_x, swap(far_one, "y"), swap(far_two, "x")
    own, other = back(kernel_z, left, layouts[1], backs)
    if ny == 2:
        near_next = stack([came_next[0], after(came_next[1], other), *came_next[2:]])
        spread = spread_xy("both", near_next)
        parts = scatter_line(z_array, (own, other), first=(near_next,))
        parts[2] = after(parts[2], *spread[1:3])
    else:
        spread = spread_plain("both", 1)
        parts = scatter_line(z_array, (own, other))
    hidden, normed = norm(1, False, hidden, parts, model_vec)
    if ny == 2:
        rows = gather_line(place, normed)
    else:
        rows = gather_line(place, normed)
    mine_z = rows[1:4]
    normed, qkv, logs, left, slope, own, other = front(
        kernel_z, rows, merged, spread, bias[1:2], table, mask
    )
    kept.append((hidden, normed, qkv, logs, left, slope))
    rows = gather_rows(after(last_low, *mine_z))
    rest = scatter_rows(z_array, (own, other), *rows[1:4])
    rows[4] = after(rows[4], rest[0])

    outs = {"front": None, "back": None}
    states = {
        "front": (w_qkv, first_qkv, second_qkv, w_up, first_up, second_up),
        "back": (w_out, first_out, second_out, w_down, first_down, second_down),
    }
    rate_in = 3.0 / math.sqrt(D)
    rates = {
        "front": (rate_in, rate_in),
        "back": (12.0 / math.sqrt(D), 3.0 / math.sqrt(FF)),
    }

    def flat(array):
        return array.reshape(ALL_ROWS, -1)

    def first_hop(grads, earlier=()):
        far_one = jnp.concatenate([g[0] for g in grads], 0) if len(grads) > 1 else grads[0][0]
        far_two = jnp.concatenate([g[1] for g in grads], 0) if len(grads) > 1 else grads[0][1]
        return bump(
            [g[2] for g in grads],
            [g[3] for g in grads],
            swap(far_one, "x"),
            swap(far_two, "y"),
            earlier,
        )

    def second_hop(on_y, on_x):
        return swap(on_y, "y"), swap(on_x, "x")

    def step(kind, layer, pieces, offset, tokens=()):
        *outs[kind], token = adam(
            kind, layer, z_array, pieces, offset, states[kind], rates[kind], outs[kind], tokens, heads_n, ffn_n
        )
        return token

    sums, slims = {}, {}
    hidden_in, normed, qkv, logs, left, slope = kept[1]
    left_grad, own, other, slims[1] = reverse(
        kernel_z, rows, merged, spread, slope, qkv, logs, table, mask
    )
    grads = [
        weight_grads("back", flat(left), stack_rows(rows), cut_of("back")),
        weight_grads("front", flat(left_grad), flat(normed), cut_of("front")),
    ]
    (result,) = norm(LAYERS, True, hidden, rest, model_vec)
    result_x = swap(result, "x")
    results = [result, swap(result, "c"), result_x, swap(result_x, "c")]
    if ny == 2:
        hops = [first_hop(grads[:1])]
        seconds = [second_hop(*hops[0])]
        parts = scatter_line(z_array, (own, other), rest[1:], last=(*hops[0], result_x))
        late_far = [after(part, *seconds[0], *parts[1:]) for part in grads[1][:2]]
        hops.append(first_hop([late_far + grads[1][2:]]))
        grad_next, low, sums[1] = norm_back(1, last_low, hidden_in, parts, model_vec)
        seconds.append(second_hop(*hops[1]))
        rows = gather_line(place, low, *hops[1], second=(results[1], results[3]))
        came_one = [send_z(split(z_array, grads[0][4:], *seconds[0]), *rows[5:]), None]
    else:
        parts = scatter_line(z_array, (own, other))
        grad_next, low, sums[1] = norm_back(1, last_low, hidden_in, parts, model_vec)
        rows = gather_line(place, low)
        came_one = [send_z(sum_plain(place, grads[:1])), sum_plain(place, grads[1:])]
    hidden_in, normed, qkv, logs, left, slope = kept[0]
    left_grad, own, other, slims[0] = reverse(
        kernel_z, rows, joint, [*fronts, *backs], slope, qkv, logs, table, mask
    )
    left_grad = after(left_grad, *came_one[0][1:])
    if ny == 2:
        came_one[1] = split(z_array, grads[1][4:], *seconds[1], [slims[0]])
    grads_front = weight_grads("front", flat(left_grad), flat(normed), cut_of("front"))
    came_one[1] = send_z(came_one[1], *came_one[0][1:])
    if ny == 2:
        hop_front = first_hop([grads_front])
        second_front = second_hop(*hop_front)
        rows = [after(row, hop_front[0]) for row in rows]
    grads_back = weight_grads("back", flat(left), stack_rows(rows), cut_of("back"))
    tokens = [step("back", 1, came_one[0], 0), step("front", 1, came_one[1], 0)]
    result_rows = give(place, results)
    if ny == 2:
        parts = scatter_line(
            z_array,
            (own, other),
            (came_one[1][1], came_one[1][3], *hop_front),
            came_one[1][2:3],
            second_front,
        )
        near_front = after(grads_front[4], *grads_back[:2])
        sum_front = split(z_array, [near_front], *second_front)
        came_front = send_z(sum_front)
        late_far = [after(part, *second_front) for part in grads_back[:2]]
        hop_back = first_hop([late_far + grads_back[2:]])
        second_back = second_hop(*(after(p, came_front[1], came_front[3]) for p in hop_back))
        sum_back = split(z_array, grads_back[4:], *second_back)
        came_back = send_z(sum_back)
        norm_parts = [*parts[:2], after(parts[2], *came_front[1:], *second_back)]
    else:
        parts = scatter_line(z_array, (own, other))
        came_front = send_z(sum_plain(place, [grads_front]))
        sum_back = sum_plain(place, [grads_back])
        came_back = send_z(sum_back)
        norm_parts = parts
    grad_next, low, sums[0] = norm_back(
        0, grad_next, hidden_in, norm_parts, model_vec, [*tokens, result_rows]
    )
    came_front = [came_front[0], *(after(piece, sum_back[0]) for piece in came_front[1:])]
    token = step("front", 0, came_front, 0)
    step("back", 0, came_back, 0, [token])
    late = sum_back[0]

    low_x = swap(low, "x")
    low, low_x = [after(part, *came_back[1:]) for part in (low, low_x)]
    both = after(jnp.concatenate([slims[0], slims[1]], 0), late)
    n = both.shape[1] // 2
    slim = both[:, :n] + swap(both[:, n:], "x")
    heads = slim[:, : 3 * heads_n].reshape(LAYERS, 3, ny, -1)
    ffns = slim[:, 3 * heads_n :].reshape(LAYERS, ny, -1)
    slim = jnp.concatenate([heads.swapaxes(1, 2).reshape(LAYERS, ny, -1), ffns], 2)
    if ny == 2:
        mine, far = [jnp.where(place.y == at, slim[:, 0], slim[:, 1]) for at in range(2)]
        slim = mine + swap(far, "y")
    else:
        slim = lax.psum_scatter(slim, "y", scatter_dimension=1, tiled=False)
    at = 3 * heads_n // ny
    grad_head = slim[:, :at].reshape(LAYERS, 3, -1)
    grad_ffn = slim[:, at:]

    total = jnp.stack([sums[layer][:3] for layer in range(LAYERS)])
    total = total + swap(total, "x")
    total = total + swap(total, "c")
    if ny == 2:
        half = D // 2
        total = total[..., :half] + swap(total[..., half:], "y")
    else:
        total = lax.psum_scatter(total, "y", scatter_dimension=2, tiled=True)
    grad_model = lax.dynamic_slice_in_dim(total, place.z * dd, dd, 2)
    for k in range(1, ZS):
        grad_model = grad_model + shift_z(
            lax.dynamic_slice_in_dim(total, (place.z + k) % ZS * dd, dd, 2), k
        )
    grad_model = jnp.concatenate([grad_model, grad_model[:, 2:]], 1)

    small = []
    for weight, grad, first, second in (
        (vec_model, grad_model, first_model, second_model),
        (vec_head, grad_head, first_head, second_head),
        (vec_ffn, grad_ffn, first_ffn, second_ffn),
    ):
        small.append(grad)
        small.extend(adamw(weight, grad, first, second, 0.6, 0.0))
    ones, twos = outs["front"], outs["back"]
    return (
        result_rows,
        give(place, [low, swap(low, "c"), low_x, swap(low_x, "c")]),
        *ones[:4],
        *twos[:4],
        *ones[4:],
        *twos[4:],
        *small,
    )


def solution(mesh):
    n_dp, n_mp = mesh.devices.shape
    ny = n_dp // ZS
    split = Mesh(mesh.devices.reshape(ZS, ny, n_mp // 2, 2), ("z", "y", "x", "c"))
    dp, mp = ("z", "y"), ("x", "c")
    both = ("x", "c", "z", "y")
    params = (
        P(None, None, dp, mp),
        P(None, mp, dp),
        P(None, dp, mp),
        P(None, mp, dp),
        P(None, None, dp),
        P(None, None, both),
        P(None, both),
    )
    tokens = (P(dp, None), P(dp, None))
    return jax.shard_map(
        lambda *arrays: per_device(ny, *arrays),
        mesh=split,
        in_specs=(*tokens, P(dp), *params, *params, *params),
        out_specs=(*tokens, *(spec for spec in params for _ in range(4))),
        check_vma=False,
    )
```

time: 3670 us -> 886 us (0.24)
  waiting for transfers between devices: 2950 us -> 280 us
  Pallas kernels: 0 us -> 288 us
  blocking collectives: 190 us -> 0 us
  matrix products: 246 us -> 70 us
  starting transfers between devices: 2.24 us -> 176 us
  other arithmetic: 123 us -> 25.2 us
  local copies, waits for them, and re-layouts: 128 us -> 35.5 us
    reduce_scatter x16 -> x0, waiting for transfers between devices: 1940 us -> none  [the longest x4 593 us: reduce_micro(): lax.psum_scatter(grad_down.astype(jnp.bfloat16), 'dp', scatter_dimension=...]
    all_gather x8 -> x0, waiting for transfers between devices: 557 us -> none  [the longest x2 228 us: fetch_forward(): lax.all_gather(weights_down, 'dp', axis=1, tiled=True)]
    unnamed x43 -> x0, waiting for transfers between devices: 343 us -> none
    pallas_call x0 -> x37, Pallas kernels: none -> 288 us  [the longest x2 67.2 us: reverse(): pl.pallas_call(lambda *refs: reverse_kernel(layouts, len(weights), *refs)...]
    ppermute x0 -> x128, waiting for transfers between devices: none -> 280 us  [the longest x30 136 us: line_z(): return lax.ppermute(array, 'z', pairs)]
    ppermute x0 -> x128, starting transfers between devices: none -> 176 us  [the longest x30 65.3 us: line_z(): return lax.ppermute(array, 'z', pairs)]
    dot_general x64 -> x21, matrix products: 246 us -> 70 us  [the longest x20 67.4 us: dot_tn(): lax.dot_general(left, right, (((0,), (0,)), ((), ())), preferred_element_...]
    all_gather x6 -> x0, blocking collectives: 154 us -> none  [the longest x2 63 us: fetch_forward(): lax.all_gather(head_vec, 'dp', axis=1, tiled=True)]
  transfers between devices with their start and end apart: 35 -> 128, of which waited for: 33 -> 45; matrix products, arithmetic and copies ran while one was open for 9% -> 12% of each run, Pallas kernels for 0% -> 30%
where the time goes in v1:
time: 886 us; the launch traced here: 878 us
  Pallas kernels  288 us (33%)
  waiting for transfers between devices  280 us (32%)
  starting transfers between devices  176 us (20%)
  matrix products  70 us (8%)
  local copies, waits for them, and re-layouts  35.5 us (4%)
  other arithmetic  25.2 us (3%)
    ppermute x30, waiting for transfers between devices, line_z(): return lax.ppermute(array, 'z', pairs)  136 us
    ppermute x30, waiting for transfers between devices, shift_z(): return lax.ppermute(array, 'z', [(i, (i + step) % ZS) for i in range(ZS)])  71.7 us
    ppermute x65, waiting for transfers between devices, swap(): return lax.ppermute(array, axis, [(0, 1), (1, 0)])  69.8 us
    dot_general x20, matrix products, dot_tn(): lax.dot_general(left, right, (((0,), (0,)), ((), ())), preferred_element_...  67.4 us
    pallas_call x2, Pallas kernels, reverse(): pl.pallas_call(lambda *refs: reverse_kernel(layouts, len(weights), *refs)...  67.2 us
    ppermute x30, starting transfers between devices, line_z(): return lax.ppermute(array, 'z', pairs)  65.3 us
    ppermute x30, starting transfers between devices, shift_z(): return lax.ppermute(array, 'z', [(i, (i + step) % ZS) for i in range(ZS)])  58.4 us
    pallas_call x2, Pallas kernels, front(): pl.pallas_call(lambda *refs: front_kernel(layouts, len(weights), *refs),...  52.1 us
  transfers between devices with their start and end apart: 128, of which 45 were waited for; matrix products, arithmetic and copies ran while one was open for 12% of the time, Pallas kernels for 30%

profile of v1, /device:TPU:0, one launch (start us, length us, event | category | flops | bytes accessed | tf_op | source)
XLA Modules:
  0.0 877.6 jit_solution(3104344016372754437)
XLA Ops:
  62.9 8.7 collective-permute-start.10
  80.5 6.6 collective-permute-done.12.refs_3_
  87.1 10.0 %collective-permute-done.11.refs_2_ = bf16[640,256]{1,0:T(8,128)(2,1)} collective-permute-done((bf16[640,256]{1,0:T(8,128)(2,1)}, bf16[640,256]{1,0:T(8,128)(2,1)}, u32[]{:S(2)}, u32[]{:S(2)}) %collective-permute-start.11) | collective-permute-done | bytes 327712 | tf_op jit(solution)/shard_map/ppermute | solution.py:36
  113.4 11.5 %collective-permute-done.21 = bf16[128,2048]{1,0:T(8,128)(2,1)S(1)} collective-permute-done((bf16[128,2048]{1,0:T(8,128)(2,1)S(1)}, bf16[128,2048]{1,0:T(8,128)(2,1)S(1)}, u32[]{:S(2)}, u32[]{:S(2)}) %collective-permute-start.21) | collective-permute-done | bytes 524320 | tf_op jit(solution)/shard_map/ppermute | solution.py:509
  132.7 11.7 %collective-permute-done.24 = bf16[128,2048]{1,0:T(8,128)(2,1)S(1)} collective-permute-done((bf16[128,2048]{1,0:T(8,128)(2,1)}, bf16[128,2048]{1,0:T(8,128)(2,1)S(1)}, u32[]{:S(2)}, u32[]{:S(2)}) %collective-permute-start.24) | collective-permute-done | bytes 524320 | tf_op jit(solution)/shard_map/ppermute | solution.py:509
  153.8 22.2 %block_front.2 = (bf16[2,4,128,2048]{3,2,1,0:T(8,128)(2,1)}, bf16[2,4,128,768]{3,2,1,0:T(8,128)(2,1)}, f32[2,4,128,256]{3,2,1,0:T(8,128)}, bf16[2,4,128,1280]{3,2,1,0:T(8,128)(2,1)}, bf16[2,4,128,1024]{3,2,1,0:T(8,128)(2,1)}) custom-call(s32[1]{0:T(128)} %bitcast.5.refs_0_, bf16[128,2048]{1,0:T(8,128)(2,1)} %get-tuple-element.247.refs_1_, ...), custom_call_target="tpu_custom_call" | custom-call | flops 1024 | bytes 1024 | tf_op jit(solution)/shard_map/block_front/pallas_call | solution.py:266
  176.1 9.1 %collective-permute-done.30.refs_1_ = bf16[1536,256]{1,0:T(8,128)(2,1)} collective-permute-done((bf16[1536,256]{1,0:T(8,128)(2,1)}, bf16[1536,256]{1,0:T(8,128)(2,1)}, u32[]{:S(2)}, u32[]{:S(2)}) %collective-permute-start.30) | collective-permute-done | bytes 786464 | tf_op jit(solution)/shard_map/ppermute | solution.py:36
  188.8 11.2 %collective-permute-done.32.refs_5_.refs_22_ = bf16[256,1024]{1,0:T(8,128)(2,1)S(1)} collective-permute-done((bf16[256,1024]{1,0:T(8,128)(2,1)S(1)}, bf16[256,1024]{1,0:T(8,128)(2,1)S(1)}, u32[]{:S(2)}, u32[]{:S(2)}) %collective-permute-start.32) | collective-permute-done | bytes 524320 | tf_op jit(solution)/shard_map/ppermute | solution.py:40
  205.2 11.0 %block_back.1 = (bf16[4,128,2048]{2,1,0:T(8,128)(2,1)}, bf16[4,128,2048]{2,1,0:T(8,128)(2,1)}) custom-call(s32[1]{0:T(128)} %bitcast.5.refs_0_, bf16[2,4,128,1280]{3,2,1,0:T(8,128)(2,1)} %get-tuple-element.262.refs_1_, bf16[640,1024]{1,0:T(8,128)(2,1)} %stack.69.refs_2_.refs_19_, bf16[640,1024]{1,0:T(8,128)(2,1)} %copy-done.3, bf16[640,1024]{1,0:T(8,128)(2,1)} %copy-done.5, ...), custom_call_target="tpu_custom_call" | custom-call | flops 1024 | bytes 1024 | tf_op jit(solution)/shard_map/block_back/pallas_call | solution.py:287
  216.2 6.6 collective-permute-done.34.refs_2_
  238.4 12.0 %collective-permute-done.36 = bf16[128,2048]{1,0:T(8,128)(2,1)S(1)} collective-permute-done((bf16[128,2048]{1,0:T(8,128)(2,1)}, bf16[128,2048]{1,0:T(8,128)(2,1)S(1)}, u32[]{:S(2)}, u32[]{:S(2)}) %collective-permute-start.36) | collective-permute-done | bytes 524320 | tf_op jit(solution)/shard_map/ppermute | solution.py:509
  256.9 10.3 %collective-permute-done.39 = bf16[128,2048]{1,0:T(8,128)(2,1)S(1)} collective-permute-done((bf16[128,2048]{1,0:T(8,128)(2,1)S(1)}, bf16[128,2048]{1,0:T(8,128)(2,1)S(1)}, u32[]{:S(2)}, u32[]{:S(2)}) %collective-permute-start.39) | collective-permute-done | bytes 524320 | tf_op jit(solution)/shard_map/ppermute | solution.py:509
  273.2 25.1 %collective-permute-done.41.refs_10_ = bf16[1536,1024]{1,0:T(8,128)(2,1)S(1)} collective-permute-done((bf16[1536,1024]{1,0:T(8,128)(2,1)}, bf16[1536,1024]{1,0:T(8,128)(2,1)S(1)}, u32[]{:S(2)}, u32[]{:S(2)}) %collective-permute-start.41) | collective-permute-done | bytes 3145760 | tf_op jit(solution)/shard_map/ppermute | solution.py:40
  309.5 7.2 collective-permute-done.43
  323.2 14.1 %collective-permute-done.47 = bf16[128,2048]{1,0:T(8,128)(2,1)S(1)} collective-permute-done((bf16[128,2048]{1,0:T(8,128)(2,1)S(1)}, bf16[128,2048]{1,0:T(8,128)(2,1)S(1)}, u32[]{:S(2)}, u32[]{:S(2)}) %collective-permute-start.47) | collective-permute-done | bytes 524320 | tf_op jit(solution)/shard_map/ppermute | solution.py:509
  338.8 13.2 %collective-permute-done.48 = bf16[128,2048]{1,0:T(8,128)(2,1)S(1)} collective-permute-done((bf16[128,2048]{1,0:T(8,128)(2,1)S(1)}, bf16[128,2048]{1,0:T(8,128)(2,1)S(1)}, u32[]{:S(2)}, u32[]{:S(2)}) %collective-permute-start.48) | collective-permute-done | bytes 524320 | tf_op jit(solution)/shard_map/ppermute | solution.py:509
  358.5 30.0 %block_front.3 = (bf16[2,4,128,2048]{3,2,1,0:T(8,128)(2,1)}, bf16[2,4,128,768]{3,2,1,0:T(8,128)(2,1)}, f32[2,4,128,256]{3,2,1,0:T(8,128)}, bf16[2,4,128,1280]{3,...) custom-call(s32[1]{0:T(128)} %bitcast.5.refs_0_, ...), custom_call_target="tpu_custom_call" | custom-call | flops 1024 | bytes 1024 | tf_op jit(solution)/shard_map/block_front/pallas_call | solution.py:266
  402.1 9.5 %collective-permute-start.58 = (bf16[128,2048]{1,0:T(8,128)(2,1)}, bf16[128,2048]{1,0:T(8,128)(2,1)S(1)}, u32[]{:S(2)}, u32[]{:S(2)}) collective-permute-start(bf16[128,2048]{1,0:T(8,128)(2,1)} %get-tuple-element.288), channel_id=1, source_target_pairs={{0,24},{8,0},{16,8},{24,16},{1,25},{9,1},{17,9},{25,17},{2,26},{10... | collective-permute-start | bytes 1572872 | tf_op jit(solution)/shard_map/ppermute | solution.py:36
  415.9 33.7 %block_reverse.2 = (bf16[2,4,128,1792]{3,2,1,0:T(8,128)(2,1)}, bf16[4,128,2048]{2,1,0:T(8,128)(2,1)}, bf16[4,128,2048]{2,1,0:T(8,128)(2,1)}, f32[1,1792]{1,0:T(1,128)}) custom-call(s32[1]{0:T(128)} %bitcast.5.refs_0_, bf16[128,2048]{1,0:T(8,128)(2,1)} %get-tuple-element.285.refs_1_.refs_0_, bf16[128,2048]{1,0:T(8,128)(2,1)} %copy-done.33, ...), custom_call_target="tpu_custom_call" | custom-call | flops 1024 | bytes 1024 | tf_op jit(solution)/shard_map/block_reverse/pallas_call | solution.py:337
  449.6 10.7 %collective-permute-done.59.refs_3_ = bf16[128,2048]{1,0:T(8,128)(2,1)S(1)} collective-permute-done((bf16[128,2048]{1,0:T(8,128)(2,1)}, bf16[128,2048]{1,0:T(8,128)(2,1)S(1)}, u32[]{:S(2)}, u32[]{:S(2)}) %collective-permute-start.59) | collective-permute-done | bytes 524320 | tf_op jit(solution)/shard_map/ppermute | solution.py:36
  479.9 6.2 collective-permute-done.69
  517.3 6.9 collective-permute-done.75.refs_4_
  558.3 6.6 collective-permute-done.80
  578.0 14.0 %collective-permute-done.85 = bf16[128,2048]{1,0:T(8,128)(2,1)S(1)} collective-permute-done((bf16[128,2048]{1,0:T(8,128)(2,1)S(1)}, bf16[128,2048]{1,0:T(8,128)(2,1)S(1)}, u32[]{:S(2)}, u32[]{:S(2)}) %collective-permute-start.85) | collective-permute-done | bytes 524320 | tf_op jit(solution)/shard_map/ppermute | solution.py:509
  610.5 33.5 %block_reverse.3 = (bf16[2,4,128,1792]{3,2,1,0:T(8,128)(2,1)}, bf16[4,128,2048]{2,1,0:T(8,128)(2,1)}, bf16[4,128,2048]{2,1,0:T(8,128)(2,1)}, f32[1,1792]{1,0:T(1,128)}) custom-call(s32[1]{0:T(128)} %bitcast.5.refs_0_, bf16[128,2048]{1,0:T(8,128)(2,1)} %get-tuple-element.351.refs_1_.refs_0_, bf16[128,2048]{1,0:T(8,128)(2,1)} %copy-done.11, ...), custom_call_target="tpu_custom_call" | custom-call | flops 1024 | bytes 1024 | tf_op jit(solution)/shard_map/block_reverse/pallas_call | solution.py:337
  703.7 11.7 %collective-permute-done.99.refs_3_ = bf16[896,256]{1,0:T(8,128)(2,1)S(1)} collective-permute-done((bf16[896,256]{1,0:T(8,128)(2,1)S(1)}, bf16[896,256]{1,0:T(8,128)(2,1)S(1)}, u32[]{:S(2)}, u32[]{:S(2)}) %collective-permute-start.99) | collective-permute-done | bytes 458784 | tf_op jit(solution)/shard_map/ppermute | solution.py:36
  760.4 8.5 collective-permute-done.105
  771.2 12.1 %collective-permute-start.106 = (bf16[128,2048]{1,0:T(8,128)(2,1)}, bf16[128,2048]{1,0:T(8,128)(2,1)S(1)}, u32[]{:S(2)}, u32[]{:S(2)}) collective-permute-start(bf16[128,2048]{1,0:T(8,128)(2,1)} %add_convert_fusion), channel_id=1, source_target_pairs={{0,8},{8,16},{16,24},{1,9},{9,17},{17,25},{2,10},{10,18},{18,26},{... | collective-permute-start | bytes 1572872 | tf_op jit(solution)/shard_map/ppermute | solution.py:509
  787.0 9.2 %adam_back.2 = (f32[2,512,256]{2,1,0:T(8,128)}, f32[2,512,256]{2,1,0:T(8,128)}, f32[2,512,256]{2,1,0:T(8,128)}, f32[2,512,256]{2,1,0:T(8,128)}, f32[2,2048,256]{...) custom-call(s32[1]{0:T(128)} %bitcast.5.refs_0_, ...), custom_call_target="tpu_custom_call" | custom-call | flops 1024 | bytes 1024 | tf_op jit(solution)/shard_map/adam_back/pallas_call | solution.py:786
  796.2 11.1 %adam_front.2 = (f32[2,3,256,512]{3,2,1,0:T(8,128)}, f32[2,3,256,512]{3,2,1,0:T(8,128)}, f32[2,3,256,512]{3,2,1,0:T(8,128)}, f32[2,3,256,512]{3,2,1,0:T(8,128)},...) custom-call(s32[1]{0:T(128)} %bitcast.5.refs_0_, ...), custom_call_target="tpu_custom_call" | custom-call | flops 1024 | bytes 1024 | tf_op jit(solution)/shard_map/adam_front/pallas_call | solution.py:786
  833.1 11.2 %adam_front.3 = (f32[2,3,256,512]{3,2,1,0:T(8,128)}, f32[2,3,256,512]{3,2,1,0:T(8,128)}, f32[2,3,256,512]{3,2,1,0:T(8,128)}, f32[2,3,256,512]{3,2,1,0:T(8,128)},...) custom-call(s32[1]{0:T(128)} %bitcast.5.refs_0_, ...), custom_call_target="tpu_custom_call", output_to_operand_aliasing={{0}: (11, {}), {1}: (12, {}), {2}: (13, {}), {3}: (14, {}),... | custom-call | flops 1024 | bytes 1024 | tf_op jit(solution)/shard_map/adam_front/pallas_call | solution.py:786
  861.9 9.1 %adam_back.3 = (f32[2,512,256]{2,1,0:T(8,128)}, f32[2,512,256]{2,1,0:T(8,128)}, f32[2,512,256]{2,1,0:T(8,128)}, f32[2,512,256]{2,1,0:T(8,128)}, f32[2,2048,256]{...) custom-call(s32[1]{0:T(128)} %bitcast.5.refs_0_, ...), custom_call_target="tpu_custom_call", output_to_operand_aliasing={{0}: (11, {}), {1}: (12, {}), {2}: (13, {}), {3}: (14, {}),... | custom-call | flops 1024 | bytes 1024 | tf_op jit(solution)/shard_map/adam_back/pallas_call | solution.py:786
  (619 shorter events, 460.3 us)
Async XLA Ops:
  24.5 31.6 %collective-permute-start.8 = (bf16[896,256]{1,0:T(8,128)(2,1)}, bf16[896,256]{1,0:T(8,128)(2,1)S(1)}, u32[]{:S(2)}, u32[]{:S(2)}) collective-permute-start(bf16[896,256]{1,0:T(8,128)(2,1)} %get-tuple-element.240), channel_id=1, source_target_pairs={{0,16},{8,24},{16,0},{24,8},{1,17},{9,25},{17,1},{25,9},{2,18},{10... | collective-permute-start | bytes 1376264 | tf_op jit(solution)/shard_map/ppermute | solution.py:36
  60.1 45.6 %collective-permute-start.17 = (bf16[896,768]{1,0:T(8,128)(2,1)}, bf16[896,768]{1,0:T(8,128)(2,1)S(1)}, u32[]{:S(2)}, u32[]{:S(2)}) collective-permute-start(bf16[896,768]{1,0:T(8,128)(2,1)} %stack.68.refs_14_), channel_id=1, source_target_pairs={{0,4},{4,0},{1,5},{5,1},{2,6},{6,2},{3,7},{7,3},{8,12},{12,8},{9,1... | collective-permute-start | bytes 4128776 | tf_op jit(solution)/shard_map/ppermute | solution.py:40
  61.6 45.8 %collective-permute-start.18 = (bf16[896,768]{1,0:T(8,128)(2,1)}, bf16[896,768]{1,0:T(8,128)(2,1)S(1)}, u32[]{:S(2)}, u32[]{:S(2)}) collective-permute-start(bf16[896,768]{1,0:T(8,128)(2,1)} %stack.68.refs_14_), channel_id=1, source_target_pairs={{0,2},{2,0},{1,3},{3,1},{4,6},{6,4},{5,7},{7,5},{8,10},{10,8},{9,1... | collective-permute-start | bytes 4128776 | tf_op jit(solution)/shard_map/ppermute | solution.py:40
  131.1 45.0 %collective-permute-start.28 = (bf16[640,1024]{1,0:T(8,128)(2,1)}, bf16[640,1024]{1,0:T(8,128)(2,1)S(1)}, u32[]{:S(2)}, u32[]{:S(2)}) collective-permute-start(bf16[640,1024]{1,0:T(8,128)(2,1)} %stack.69.refs_2_.refs_19_), channel_id=1, source_target_pairs={{0,4},{4,0},{1,5},{5,1},{2,6},{6,2},{3,7},{7,3},{8,12},{12,8},{9,1... | collective-permute-start | bytes 3932168 | tf_op jit(solution)/shard_map/ppermute | solution.py:40
  146.5 40.5 %collective-permute-start.29 = (bf16[640,1024]{1,0:T(8,128)(2,1)S(1)}, bf16[640,1024]{1,0:T(8,128)(2,1)S(1)}, u32[]{:S(2)}, u32[]{:S(2)}) collective-permute-start(bf16[640,1024]{1,0:T(8,128)(2,1)S(1)} %copy-done.1), channel_id=1, source_target_pairs={{0,2},{2,0},{1,3},{3,1},{4,6},{6,4},{5,7},{7,5},{8,10},{10,8},{9,1... | collective-permute-start | bytes 3932168 | tf_op jit(solution)/shard_map/ppermute | solution.py:40
  150.2 35.0 %collective-permute-start.30 = (bf16[1536,256]{1,0:T(8,128)(2,1)}, bf16[1536,256]{1,0:T(8,128)(2,1)}, u32[]{:S(2)}, u32[]{:S(2)}) collective-permute-start(bf16[1536,256]{1,0:T(8,128)(2,1)} %get-tuple-element.263), channel_id=1, source_target_pairs={{0,8},{8,16},{16,24},{24,0},{1,9},{9,17},{17,25},{25,1},{2,10},{10... | collective-permute-start | bytes 2359304 | tf_op jit(solution)/shard_map/ppermute | solution.py:36
  185.9 36.9 %collective-permute-start.34 = (bf16[1536,256]{1,0:T(8,128)(2,1)}, bf16[1536,256]{1,0:T(8,128)(2,1)}, u32[]{:S(2)}, u32[]{:S(2)}) collective-permute-start(bf16[1536,256]{1,0:T(8,128)(2,1)} %get-tuple-element.270), channel_id=1, source_target_pairs={{0,16},{8,24},{16,0},{24,8},{1,17},{9,25},{17,1},{25,9},{2,18},{10... | collective-permute-start | bytes 2359304 | tf_op jit(solution)/shard_map/ppermute | solution.py:36
  226.8 71.5 %collective-permute-start.41 = (bf16[1536,1024]{1,0:T(8,128)(2,1)}, bf16[1536,1024]{1,0:T(8,128)(2,1)S(1)}, u32[]{:S(2)}, u32[]{:S(2)}) collective-permute-start(bf16[1536,1024]{1,0:T(8,128)(2,1)} %stack.70.refs_9_), channel_id=1, source_target_pairs={{0,4},{4,0},{1,5},{5,1},{2,6},{6,2},{3,7},{7,3},{8,12},{12,8},{9,1... | collective-permute-start | bytes 9437192 | tf_op jit(solution)/shard_map/ppermute | solution.py:40
  229.3 70.5 %collective-permute-start.42 = (bf16[1536,1024]{1,0:T(8,128)(2,1)}, bf16[1536,1024]{1,0:T(8,128)(2,1)}, u32[]{:S(2)}, u32[]{:S(2)}) collective-permute-start(bf16[1536,1024]{1,0:T(8,128)(2,1)} %stack.70.refs_9_), channel_id=1, source_target_pairs={{0,2},{2,0},{1,3},{3,1},{4,6},{6,4},{5,7},{7,5},{8,10},{10,8},{9,1... | collective-permute-start | bytes 9437192 | tf_op jit(solution)/shard_map/ppermute | solution.py:40
  267.3 32.5 %collective-permute-start.40 = (bf16[128,2048]{1,0:T(8,128)(2,1)S(1)}, bf16[128,2048]{1,0:T(8,128)(2,1)S(1)}, u32[]{:S(2)}, u32[]{:S(2)}) collective-permute-start(bf16[128,2048]{1,0:T(8,128)(2,1)S(1)} %add_convert_fusion.6), channel_id=1, source_target_pairs={{0,8},{8,16},{16,24},{1,9},{9,17},{17,25},{2,10},{10,18},{18,26},{... | collective-permute-start | bytes 1572872 | tf_op jit(solution)/shard_map/ppermute | solution.py:509
  308.3 44.4 %collective-permute-start.52 = (bf16[768,1024]{1,0:T(8,128)(2,1)S(1)}, bf16[768,1024]{1,0:T(8,128)(2,1)S(1)}, u32[]{:S(2)}, u32[]{:S(2)}) collective-permute-start(bf16[768,1024]{1,0:T(8,128)(2,1)S(1)} %slice.242), channel_id=1, source_target_pairs={{0,4},{4,0},{1,5},{5,1},{2,6},{6,2},{3,7},{7,3},{8,12},{12,8},{9,1... | collective-permute-start | bytes 4718600 | tf_op jit(solution)/shard_map/ppermute | solution.py:40
  309.1 43.9 %collective-permute-start.53 = (bf16[768,1024]{1,0:T(8,128)(2,1)S(1)}, bf16[768,1024]{1,0:T(8,128)(2,1)S(1)}, u32[]{:S(2)}, u32[]{:S(2)}) collective-permute-start(bf16[768,1024]{1,0:T(8,128)(2,1)S(1)} %slice.243), channel_id=1, source_target_pairs={{0,2},{2,0},{1,3},{3,1},{4,6},{6,4},{5,7},{7,5},{8,10},{10,8},{9,1... | collective-permute-start | bytes 4718600 | tf_op jit(solution)/shard_map/ppermute | solution.py:40
  352.7 35.7 %collective-permute-start.54 = (bf16[128,2048]{1,0:T(8,128)(2,1)S(1)}, bf16[128,2048]{1,0:T(8,128)(2,1)S(1)}, u32[]{:S(2)}, u32[]{:S(2)}) collective-permute-start(bf16[128,2048]{1,0:T(8,128)(2,1)S(1)} %copy-done.8), channel_id=1, source_target_pairs={{0,8},{8,16},{16,24},{24,0},{1,9},{9,17},{17,25},{25,1},{2,10},{10... | collective-permute-start | bytes 1572872 | tf_op jit(solution)/shard_map/ppermute | solution.py:36
  352.7 38.4 %collective-permute-start.55 = (bf16[128,2048]{1,0:T(8,128)(2,1)S(1)}, bf16[128,2048]{1,0:T(8,128)(2,1)}, u32[]{:S(2)}, u32[]{:S(2)}) collective-permute-start(bf16[128,2048]{1,0:T(8,128)(2,1)S(1)} %copy-done.8), channel_id=1, source_target_pairs={{0,16},{8,24},{16,0},{24,8},{1,17},{9,25},{17,1},{25,9},{2,18},{10... | collective-permute-start | bytes 1572872 | tf_op jit(solution)/shard_map/ppermute | solution.py:36
  353.0 38.1 %collective-permute-start.56 = (bf16[128,2048]{1,0:T(8,128)(2,1)S(1)}, bf16[128,2048]{1,0:T(8,128)(2,1)}, u32[]{:S(2)}, u32[]{:S(2)}) collective-permute-start(bf16[128,2048]{1,0:T(8,128)(2,1)S(1)} %copy-done.8), channel_id=1, source_target_pairs={{0,24},{8,0},{16,8},{24,16},{1,25},{9,1},{17,9},{25,17},{2,26},{10... | collective-permute-start | bytes 1572872 | tf_op jit(solution)/shard_map/ppermute | solution.py:36
  402.1 47.5 %collective-permute-start.58 = (bf16[128,2048]{1,0:T(8,128)(2,1)}, bf16[128,2048]{1,0:T(8,128)(2,1)S(1)}, u32[]{:S(2)}, u32[]{:S(2)}) collective-permute-start(bf16[128,2048]{1,0:T(8,128)(2,1)} %get-tuple-element.288), channel_id=1, source_target_pairs={{0,24},{8,0},{16,8},{24,16},{1,25},{9,1},{17,9},{25,17},{2,26},{10... | collective-permute-start | bytes 1572872 | tf_op jit(solution)/shard_map/ppermute | solution.py:36
  411.6 48.7 %collective-permute-start.59 = (bf16[128,2048]{1,0:T(8,128)(2,1)}, bf16[128,2048]{1,0:T(8,128)(2,1)S(1)}, u32[]{:S(2)}, u32[]{:S(2)}) collective-permute-start(bf16[128,2048]{1,0:T(8,128)(2,1)} %get-tuple-element.289), channel_id=1, source_target_pairs={{0,16},{8,24},{16,0},{24,8},{1,17},{9,25},{17,1},{25,9},{2,18},{10... | collective-permute-start | bytes 1572872 | tf_op jit(solution)/shard_map/ppermute | solution.py:36
  414.5 45.8 %collective-permute-start.60 = (bf16[128,2048]{1,0:T(8,128)(2,1)}, bf16[128,2048]{1,0:T(8,128)(2,1)S(1)}, u32[]{:S(2)}, u32[]{:S(2)}) collective-permute-start(bf16[128,2048]{1,0:T(8,128)(2,1)} %get-tuple-element.290), channel_id=1, source_target_pairs={{0,8},{8,16},{16,24},{24,0},{1,9},{9,17},{17,25},{25,1},{2,10},{10... | collective-permute-start | bytes 1572872 | tf_op jit(solution)/shard_map/ppermute | solution.py:36
  509.7 31.6 %collective-permute-start.82 = (bf16[640,1024]{1,0:T(8,128)(2,1)}, bf16[640,1024]{1,0:T(8,128)(2,1)}, u32[]{:S(2)}, u32[]{:S(2)}) collective-permute-start(bf16[640,1024]{1,0:T(8,128)(2,1)} %get-tuple-element.304), channel_id=1, source_target_pairs={{0,2},{2,0},{1,3},{3,1},{4,6},{6,4},{5,7},{7,5},{8,10},{10,8},{9,1... | collective-permute-start | bytes 3932168 | tf_op jit(solution)/shard_map/ppermute | solution.py:40
  594.0 62.2 %collective-permute-start.89 = (bf16[896,1024]{1,0:T(8,128)(2,1)}, bf16[896,1024]{1,0:T(8,128)(2,1)}, u32[]{:S(2)}, u32[]{:S(2)}) collective-permute-start(bf16[896,1024]{1,0:T(8,128)(2,1)} %get-tuple-element.316), channel_id=1, source_target_pairs={{0,4},{4,0},{1,5},{5,1},{2,6},{6,2},{3,7},{7,3},{8,12},{12,8},{9,1... | collective-permute-start | bytes 5505032 | tf_op jit(solution)/shard_map/ppermute | solution.py:40
  595.4 60.7 %collective-permute-start.90 = (bf16[896,1024]{1,0:T(8,128)(2,1)}, bf16[896,1024]{1,0:T(8,128)(2,1)}, u32[]{:S(2)}, u32[]{:S(2)}) collective-permute-start(bf16[896,1024]{1,0:T(8,128)(2,1)} %get-tuple-element.317), channel_id=1, source_target_pairs={{0,2},{2,0},{1,3},{3,1},{4,6},{6,4},{5,7},{7,5},{8,10},{10,8},{9,1... | collective-permute-start | bytes 5505032 | tf_op jit(solution)/shard_map/ppermute | solution.py:40
  602.8 41.3 %collective-permute-start.93 = (bf16[640,256]{1,0:T(8,128)(2,1)}, bf16[640,256]{1,0:T(8,128)(2,1)S(1)}, u32[]{:S(2)}, u32[]{:S(2)}) collective-permute-start(bf16[640,256]{1,0:T(8,128)(2,1)} %get-tuple-element.332), channel_id=1, source_target_pairs={{0,24},{8,0},{16,8},{24,16},{1,25},{9,1},{17,9},{25,17},{2,26},{10... | collective-permute-start | bytes 983048 | tf_op jit(solution)/shard_map/ppermute | solution.py:36
  603.7 40.4 %collective-permute-start.92 = (bf16[640,256]{1,0:T(8,128)(2,1)}, bf16[640,256]{1,0:T(8,128)(2,1)S(1)}, u32[]{:S(2)}, u32[]{:S(2)}) collective-permute-start(bf16[640,256]{1,0:T(8,128)(2,1)} %get-tuple-element.330), channel_id=1, source_target_pairs={{0,16},{8,24},{16,0},{24,8},{1,17},{9,25},{17,1},{25,9},{2,18},{10... | collective-permute-start | bytes 983048 | tf_op jit(solution)/shard_map/ppermute | solution.py:36
  604.0 40.1 %collective-permute-start.91 = (bf16[640,256]{1,0:T(8,128)(2,1)}, bf16[640,256]{1,0:T(8,128)(2,1)S(1)}, u32[]{:S(2)}, u32[]{:S(2)}) collective-permute-start(bf16[640,256]{1,0:T(8,128)(2,1)} %get-tuple-element.328), channel_id=1, source_target_pairs={{0,8},{8,16},{16,24},{24,0},{1,9},{9,17},{17,25},{25,1},{2,10},{10... | collective-permute-start | bytes 983048 | tf_op jit(solution)/shard_map/ppermute | solution.py:36
  685.0 44.2 %collective-permute-start.101 = (bf16[896,1024]{1,0:T(8,128)(2,1)}, bf16[896,1024]{1,0:T(8,128)(2,1)}, u32[]{:S(2)}, u32[]{:S(2)}) collective-permute-start(bf16[896,1024]{1,0:T(8,128)(2,1)} %get-tuple-element.339), channel_id=1, source_target_pairs={{0,4},{4,0},{1,5},{5,1},{2,6},{6,2},{3,7},{7,3},{8,12},{12,8},{9,1... | collective-permute-start | bytes 5505032 | tf_op jit(solution)/shard_map/ppermute | solution.py:40
  686.4 42.8 %collective-permute-start.102 = (bf16[896,1024]{1,0:T(8,128)(2,1)}, bf16[896,1024]{1,0:T(8,128)(2,1)}, u32[]{:S(2)}, u32[]{:S(2)}) collective-permute-start(bf16[896,1024]{1,0:T(8,128)(2,1)} %get-tuple-element.340), channel_id=1, source_target_pairs={{0,2},{2,0},{1,3},{3,1},{4,6},{6,4},{5,7},{7,5},{8,10},{10,8},{9,1... | collective-permute-start | bytes 5505032 | tf_op jit(solution)/shard_map/ppermute | solution.py:40
  748.6 34.8 %collective-permute-start.103 = (bf16[128,2048]{1,0:T(8,128)(2,1)}, bf16[128,2048]{1,0:T(8,128)(2,1)}, u32[]{:S(2)}, u32[]{:S(2)}) collective-permute-start(bf16[128,2048]{1,0:T(8,128)(2,1)} %add_convert_fusion.2), channel_id=1, source_target_pairs={{16,8},{24,16},{17,9},{25,17},{18,10},{26,18},{19,11},{27,19},{20,... | collective-permute-start | bytes 1572872 | tf_op jit(solution)/shard_map/ppermute | solution.py:509
  752.9 63.8 %collective-permute-start.108 = (bf16[896,256]{1,0:T(8,128)(2,1)}, bf16[896,256]{1,0:T(8,128)(2,1)}, u32[]{:S(2)}, u32[]{:S(2)}) collective-permute-start(bf16[896,256]{1,0:T(8,128)(2,1)} %get-tuple-element.361), channel_id=1, source_target_pairs={{0,16},{8,24},{16,0},{24,8},{1,17},{9,25},{17,1},{25,9},{2,18},{10... | collective-permute-start | bytes 1376264 | tf_op jit(solution)/shard_map/ppermute | solution.py:36
  758.6 52.7 %collective-permute-start.113 = (bf16[640,1024]{1,0:T(8,128)(2,1)}, bf16[640,1024]{1,0:T(8,128)(2,1)S(1)}, u32[]{:S(2)}, u32[]{:S(2)}) collective-permute-start(bf16[640,1024]{1,0:T(8,128)(2,1)} %get-tuple-element.368), channel_id=1, source_target_pairs={{0,2},{2,0},{1,3},{3,1},{4,6},{6,4},{5,7},{7,5},{8,10},{10,8},{9,1... | collective-permute-start | bytes 3932168 | tf_op jit(solution)/shard_map/ppermute | solution.py:40
  759.1 52.2 %collective-permute-start.112 = (bf16[640,1024]{1,0:T(8,128)(2,1)}, bf16[640,1024]{1,0:T(8,128)(2,1)}, u32[]{:S(2)}, u32[]{:S(2)}) collective-permute-start(bf16[640,1024]{1,0:T(8,128)(2,1)} %get-tuple-element.366), channel_id=1, source_target_pairs={{0,4},{4,0},{1,5},{5,1},{2,6},{6,2},{3,7},{7,3},{8,12},{12,8},{9,1... | collective-permute-start | bytes 3932168 | tf_op jit(solution)/shard_map/ppermute | solution.py:40
  771.2 45.5 %collective-permute-start.106 = (bf16[128,2048]{1,0:T(8,128)(2,1)}, bf16[128,2048]{1,0:T(8,128)(2,1)S(1)}, u32[]{:S(2)}, u32[]{:S(2)}) collective-permute-start(bf16[128,2048]{1,0:T(8,128)(2,1)} %add_convert_fusion), channel_id=1, source_target_pairs={{0,8},{8,16},{16,24},{1,9},{9,17},{17,25},{2,10},{10,18},{18,26},{... | collective-permute-start | bytes 1572872 | tf_op jit(solution)/shard_map/ppermute | solution.py:509
  785.7 31.0 %collective-permute-start.104 = (bf16[128,2048]{1,0:T(8,128)(2,1)}, bf16[128,2048]{1,0:T(8,128)(2,1)}, u32[]{:S(2)}, u32[]{:S(2)}) collective-permute-start(bf16[128,2048]{1,0:T(8,128)(2,1)} %add_convert_fusion.1), channel_id=1, source_target_pairs={{8,0},{16,8},{24,16},{9,1},{17,9},{25,17},{10,2},{18,10},{26,18},{... | collective-permute-start | bytes 1572872 | tf_op jit(solution)/shard_map/ppermute | solution.py:509
  (210 other events, 2811.4 us)

commit v2 on v1

--- a/solution.py
+++ b/solution.py
@@ -18,6 +18,7 @@
 ROWS = 256
 ZS = 4
 HALF = 128
+ORDER = (0, 1, 3, 2)
 PAIR = 2 * HEAD_DIM
 
 BETA_ONE = 0.9
@@ -160,7 +161,7 @@
 
 
 def lanes_of(z_ref, k, y, dd):
-    return pl.ds(pl.multiple_of(y * ZS * dd + (z_ref[0] - k + ZS) % ZS * dd, dd), dd)
+    return pl.ds(pl.multiple_of(y * ZS * dd + (z_ref[0] - ORDER[k] + ZS) % ZS * dd, dd), dd)
 
 
 def take_rows(z_ref, sources, relative, target=None):
@@ -1022,7 +1023,7 @@
         for k, piece in enumerate(pieces):
             joined = lax.dynamic_update_slice(joined, piece, (0, (place.z - k) % ZS * dd))
         own = place.y_columns(joined).reshape(n, 2, ZS, -1)
-        own = jnp.concatenate([own[:, :, :1], own[:, :, :0:-1]], 2).reshape(n, D)
+        own = jnp.stack([own[:, :, -k % ZS] for k in ORDER], 2).reshape(n, D)
         other = swap(own, "x")
         cut, half = cut_of(kind), D // 2
         return own[:, :half], own[:, half:], other[:, :half], other[:cut, half:], other[cut:, half:]
@@ -1034,7 +1035,8 @@
         return (*((ids[at], 0, n) for at in range(3)), far)
 
     both_cut = cut_of("both")
-    ids = [(at,) for at in range(5)]
+    chunks = 3 if ny == 2 else 1
+    ids = [tuple(5 * c + at for c in range(chunks)) for at in range(5)]
     merged = (
         (*((ids[at], 0, n_front) for at in range(3)), [(ids[3], 0, both_cut), (ids[4], 0, n_front - both_cut)]),
         (*((ids[at], n_front, n_both) for at in range(3)), [(ids[4], n_front - both_cut, n_both - both_cut)]),
@@ -1045,11 +1047,11 @@
         came_front[1] = after(came_front[1], start)
         came_back = send_z(pieces_back, *came_front[1:])
         rest_front = list(
-            spread_xy("front", stack([after(came_front[1], *own_front[3:]), *came_front[2:]]))
+            spread_xy("front", stack([after(came_front[1], *own_front[3:]), *came_front[:1:-1]]))
         )
         fronts = [*own_front, *rest_front]
         rest_front[1] = after(rest_front[1], table, mask)
-        near_back = stack([came_back[0], after(came_back[1], *rest_front[3:]), *came_back[2:]])
+        near_back = stack([came_back[0], after(came_back[1], *rest_front[3:]), *came_back[:1:-1]])
         on_x, on_y = swap(near_back, "x"), swap(near_back, "y")
         rows = gather_line(
             place, after(normed, *came_back[1:]), near_back, second=rest_front[1:3]
@@ -1072,18 +1074,23 @@
         cut, ready = cut_of("back"), (left, came_next[1], came_next[3])
         far_one, far_two = after(on_x[:cut], *ready), after(on_y[cut:], *ready)
         backs = near_back, on_y, on_x, swap(far_one, "y"), swap(far_two, "x")
+        first_next = spread_xy("both", after(came_next[0], *backs[3:]))
+        mid_next = stack([came_next[1], came_next[3]])
+        left = after(left, mid_next)
     own, other = back(kernel_z, left, layouts[1], backs)
     if ny == 2:
-        near_next = stack([came_next[0], after(came_next[1], other), *came_next[2:]])
-        spread = spread_xy("both", near_next)
-        parts = scatter_line(z_array, (own, other), first=(near_next,))
-        parts[2] = after(parts[2], *spread[1:3])
+        last_piece = after(came_next[2], other)
+        mid_next = spread_xy("both", after(mid_next, *first_next[1:3]))
+        last_next = spread_xy("both", after(last_piece, *mid_next[1:3]))
+        spread = [*first_next, *mid_next, *last_next]
+        parts = scatter_line(z_array, (own, other), first=(last_piece, *first_next[1:3]))
+        parts[2] = after(parts[2], *mid_next[1:3], *first_next[3:])
     else:
         spread = spread_plain("both", 1)
         parts = scatter_line(z_array, (own, other))
     hidden, normed = norm(1, False, hidden, parts, model_vec)
     if ny == 2:
-        rows = gather_line(place, normed)
+        rows = gather_line(place, normed, second=(*last_next[1:3], *mid_next[3:]))
     else:
         rows = gather_line(place, normed)
     mine_z = rows[1:4]

time: 886 us -> 875 us (0.988)
  waiting for transfers between devices: 280 us -> 255 us
  starting transfers between devices: 176 us -> 190 us
    ppermute x30, waiting for transfers between devices: 136 us -> 118 us  [line_z(): return lax.ppermute(array, 'z', pairs)]
    ppermute x65 -> x73, starting transfers between devices: 48.1 us -> 59 us  [swap(): return lax.ppermute(array, axis, [(0, 1), (1, 0)])]
    ppermute x65 -> x73, waiting for transfers between devices: 69.8 us -> 65.4 us  [swap(): return lax.ppermute(array, axis, [(0, 1), (1, 0)])]
    unnamed x237 -> x267, local copies, waits for them, and re-layouts: 28.3 us -> 24 us
  transfers between devices with their start and end apart: 128 -> 136, of which waited for: 45 -> 46; matrix products, arithmetic and copies ran while one was open for 12% -> 12% of each run, Pallas kernels for 30% -> 31%
where the time goes in v2:
time: 875 us; the launch traced here: 866 us
  Pallas kernels  288 us (33%)
  waiting for transfers between devices  255 us (29%)
  starting transfers between devices  190 us (22%)
  matrix products  74.1 us (8%)
  local copies, waits for them, and re-layouts  32.1 us (4%)
  other arithmetic  23 us (3%)
    ppermute x30, waiting for transfers between devices, line_z(): return lax.ppermute(array, 'z', pairs)  118 us
    dot_general x20, matrix products, dot_tn(): lax.dot_general(left, right, (((0,), (0,)), ((), ())), preferred_element_...  70.7 us
    ppermute x30, starting transfers between devices, line_z(): return lax.ppermute(array, 'z', pairs)  69 us
    pallas_call x2, Pallas kernels, reverse(): pl.pallas_call(lambda *refs: reverse_kernel(layouts, len(weights), *refs)...  68.5 us
    ppermute x30, waiting for transfers between devices, shift_z(): return lax.ppermute(array, 'z', [(i, (i + step) % ZS) for i in range(ZS)])  68.2 us
    ppermute x73, waiting for transfers between devices, swap(): return lax.ppermute(array, axis, [(0, 1), (1, 0)])  65.4 us
    ppermute x73, starting transfers between devices, swap(): return lax.ppermute(array, axis, [(0, 1), (1, 0)])  59 us
    ppermute x30, starting transfers between devices, shift_z(): return lax.ppermute(array, 'z', [(i, (i + step) % ZS) for i in range(ZS)])  57.3 us
  transfers between devices with their start and end apart: 136, of which 46 were waited for; matrix products, arithmetic and copies ran while one was open for 12% of the time, Pallas kernels for 31%

profile of v2, /device:TPU:0, one launch (start us, length us, event | category | flops | bytes accessed | tf_op | source)
XLA Modules:
  0.0 865.8 jit_solution(1844736116775298786)
XLA Ops:
  32.6 5.8 pack_both.1
  62.8 8.7 %collective-permute-start.10 = (bf16[640,256]{1,0:T(8,128)(2,1)}, bf16[640,256]{1,0:T(8,128)(2,1)S(1)}, u32[]{:S(2)}, u32[]{:S(2)}) collective-permute-start(bf16[640,256]{1,0:T(8,128)(2,1)} %get-tuple-element.247), channel_id=1, source_target_pairs={{0,8},{8,16},{16,24},{24,0},{1,9},{9,17},{17,25},{25,1},{2,10},{10... | collective-permute-start | bytes 983048 | tf_op jit(solution)/shard_map/ppermute | solution.py:37
  80.4 6.6 collective-permute-done.12.refs_2_
  87.0 10.0 %collective-permute-done.11.refs_3_ = bf16[640,256]{1,0:T(8,128)(2,1)} collective-permute-done((bf16[640,256]{1,0:T(8,128)(2,1)}, bf16[640,256]{1,0:T(8,128)(2,1)}, u32[]{:S(2)}, u32[]{:S(2)}) %collective-permute-start.11) | collective-permute-done | bytes 327712 | tf_op jit(solution)/shard_map/ppermute | solution.py:37
  113.4 12.3 %collective-permute-done.21 = bf16[128,2048]{1,0:T(8,128)(2,1)S(1)} collective-permute-done((bf16[128,2048]{1,0:T(8,128)(2,1)S(1)}, bf16[128,2048]{1,0:T(8,128)(2,1)S(1)}, u32[]{:S(2)}, u32[]{:S(2)}) %collective-permute-start.21) | collective-permute-done | bytes 524320 | tf_op jit(solution)/shard_map/ppermute | solution.py:510
  132.5 12.5 %collective-permute-done.24 = bf16[128,2048]{1,0:T(8,128)(2,1)} collective-permute-done((bf16[128,2048]{1,0:T(8,128)(2,1)}, bf16[128,2048]{1,0:T(8,128)(2,1)}, u32[]{:S(2)}, u32[]{:S(2)}) %collective-permute-start.24) | collective-permute-done | bytes 524320 | tf_op jit(solution)/shard_map/ppermute | solution.py:510
  152.9 22.2 %block_front.2 = (bf16[2,4,128,2048]{3,2,1,0:T(8,128)(2,1)}, bf16[2,4,128,768]{3,2,1,0:T(8,128)(2,1)}, f32[2,4,128,256]{3,2,1,0:T(8,128)}, bf16[2,4,128,1280]{3,2,1,0:T(8,128)(2,1)}, bf16[2,4,128,1024]{3,2,1,0:T(8,128)(2,1)}) custom-call(s32[1]{0:T(128)} %bitcast.5.refs_0_, bf16[128,2048]{1,0:T(8,128)(2,1)} %get-tuple-element.252.refs_1_, ...), custom_call_target="tpu_custom_call" | custom-call | flops 1024 | bytes 1024 | tf_op jit(solution)/shard_map/block_front/pallas_call | solution.py:267
  175.1 9.6 %collective-permute-done.28.refs_0_ = bf16[1536,256]{1,0:T(8,128)(2,1)} collective-permute-done((bf16[1536,256]{1,0:T(8,128)(2,1)}, bf16[1536,256]{1,0:T(8,128)(2,1)}, u32[]{:S(2)}, u32[]{:S(2)}) %collective-permute-start.28) | collective-permute-done | bytes 786464 | tf_op jit(solution)/shard_map/ppermute | solution.py:37
  188.6 11.3 %collective-permute-done.32.refs_5_.refs_22_ = bf16[256,1024]{1,0:T(8,128)(2,1)S(1)} collective-permute-done((bf16[256,1024]{1,0:T(8,128)(2,1)S(1)}, bf16[256,1024]{1,0:T(8,128)(2,1)S(1)}, u32[]{:S(2)}, u32[]{:S(2)}) %collective-permute-start.32) | collective-permute-done | bytes 524320 | tf_op jit(solution)/shard_map/ppermute | solution.py:41
  210.2 11.1 %block_back.1 = (bf16[4,128,2048]{2,1,0:T(8,128)(2,1)}, bf16[4,128,2048]{2,1,0:T(8,128)(2,1)}) custom-call(s32[1]{0:T(128)} %bitcast.5.refs_0_, bf16[2,4,128,1280]{3,2,1,0:T(8,128)(2,1)} %get-tuple-element.270.refs_1_, bf16[640,1024]{1,0:T(8,128)(2,1)} %stack.69.refs_2_.refs_19_, bf16[640,1024]{1,0:T(8,128)(2,1)} %copy-done.5, bf16[640,1024]{1,0:T(8,128)(2,1)} %copy-done.7, ...), custom_call_target="tpu_custom_call" | custom-call | flops 1024 | bytes 1024 | tf_op jit(solution)/shard_map/block_back/pallas_call | solution.py:288
  237.6 11.7 %collective-permute-done.38 = bf16[128,2048]{1,0:T(8,128)(2,1)S(1)} collective-permute-done((bf16[128,2048]{1,0:T(8,128)(2,1)}, bf16[128,2048]{1,0:T(8,128)(2,1)S(1)}, u32[]{:S(2)}, u32[]{:S(2)}) %collective-permute-start.38) | collective-permute-done | bytes 524320 | tf_op jit(solution)/shard_map/ppermute | solution.py:510
  257.1 6.8 collective-permute-done.43.refs_15_
  296.8 8.9 %collective-permute-done.51.refs_17_ = bf16[768,512]{1,0:T(8,128)(2,1)S(1)} collective-permute-done((bf16[768,512]{1,0:T(8,128)(2,1)}, bf16[768,512]{1,0:T(8,128)(2,1)S(1)}, u32[]{:S(2)}, u32[]{:S(2)}) %collective-permute-start.51) | collective-permute-done | bytes 786464 | tf_op jit(solution)/shard_map/ppermute | solution.py:41
  310.1 12.1 %collective-permute-done.55 = bf16[128,2048]{1,0:T(8,128)(2,1)S(1)} collective-permute-done((bf16[128,2048]{1,0:T(8,128)(2,1)S(1)}, bf16[128,2048]{1,0:T(8,128)(2,1)S(1)}, u32[]{:S(2)}, u32[]{:S(2)}) %collective-permute-start.55) | collective-permute-done | bytes 524320 | tf_op jit(solution)/shard_map/ppermute | solution.py:510
  325.0 10.8 %collective-permute-done.56 = bf16[128,2048]{1,0:T(8,128)(2,1)S(1)} collective-permute-done((bf16[128,2048]{1,0:T(8,128)(2,1)S(1)}, bf16[128,2048]{1,0:T(8,128)(2,1)S(1)}, u32[]{:S(2)}, u32[]{:S(2)}) %collective-permute-start.56) | collective-permute-done | bytes 524320 | tf_op jit(solution)/shard_map/ppermute | solution.py:510
  341.9 30.6 %block_front.3 = (bf16[2,4,128,2048]{3,2,1,0:T(8,128)(2,1)}, bf16[2,4,128,768]{3,2,1,0:T(8,128)(2,1)}, f32[2,4,128,256]{3,2,1,0:T(8,128)}, bf16[2,4,128,1280]{3,...) custom-call(s32[1]{0:T(128)} %bitcast.5.refs_0_, ...), custom_call_target="tpu_custom_call" | custom-call | flops 1024 | bytes 1024 | tf_op jit(solution)/shard_map/block_front/pallas_call | solution.py:267
  375.9 6.2 collective-permute-done.65.refs_2_
  387.3 10.8 %collective-permute-start.66 = (bf16[128,2048]{1,0:T(8,128)(2,1)}, bf16[128,2048]{1,0:T(8,128)(2,1)S(1)}, u32[]{:S(2)}, u32[]{:S(2)}) collective-permute-start(bf16[128,2048]{1,0:T(8,128)(2,1)} %get-tuple-element.298), channel_id=1, source_target_pairs={{0,24},{8,0},{16,8},{24,16},{1,25},{9,1},{17,9},{25,17},{2,26},{10... | collective-permute-start | bytes 1572872 | tf_op jit(solution)/shard_map/ppermute | solution.py:37
  400.7 35.1 %block_reverse.2 = (bf16[2,4,128,1792]{3,2,1,0:T(8,128)(2,1)}, bf16[4,128,2048]{2,1,0:T(8,128)(2,1)}, bf16[4,128,2048]{2,1,0:T(8,128)(2,1)}, f32[1,1792]{1,0:T(1,128)}) custom-call(s32[1]{0:T(128)} %bitcast.5.refs_0_, bf16[128,2048]{1,0:T(8,128)(2,1)} %get-tuple-element.295.refs_1_.refs_0_, bf16[128,2048]{1,0:T(8,128)(2,1)} %copy-done.40, ...), custom_call_target="tpu_custom_call" | custom-call | flops 1024 | bytes 1024 | tf_op jit(solution)/shard_map/block_reverse/pallas_call | solution.py:338
  435.8 9.7 %collective-permute-done.67.refs_3_ = bf16[128,2048]{1,0:T(8,128)(2,1)S(1)} collective-permute-done((bf16[128,2048]{1,0:T(8,128)(2,1)}, bf16[128,2048]{1,0:T(8,128)(2,1)S(1)}, u32[]{:S(2)}, u32[]{:S(2)}) %collective-permute-start.67) | collective-permute-done | bytes 524320 | tf_op jit(solution)/shard_map/ppermute | solution.py:37
  502.4 7.2 collective-permute-done.83.refs_4_
  544.0 6.8 collective-permute-done.88
  563.7 13.3 %collective-permute-done.93 = bf16[128,2048]{1,0:T(8,128)(2,1)S(1)} collective-permute-done((bf16[128,2048]{1,0:T(8,128)(2,1)S(1)}, bf16[128,2048]{1,0:T(8,128)(2,1)S(1)}, u32[]{:S(2)}, u32[]{:S(2)}) %collective-permute-start.93) | collective-permute-done | bytes 524320 | tf_op jit(solution)/shard_map/ppermute | solution.py:510
  596.0 33.4 %block_reverse.3 = (bf16[2,4,128,1792]{3,2,1,0:T(8,128)(2,1)}, bf16[4,128,2048]{2,1,0:T(8,128)(2,1)}, bf16[4,128,2048]{2,1,0:T(8,128)(2,1)}, f32[1,1792]{1,0:T(1,128)}) custom-call(s32[1]{0:T(128)} %bitcast.5.refs_0_, bf16[128,2048]{1,0:T(8,128)(2,1)} %get-tuple-element.361.refs_1_.refs_0_, bf16[128,2048]{1,0:T(8,128)(2,1)} %copy-done.17, ...), custom_call_target="tpu_custom_call" | custom-call | flops 1024 | bytes 1024 | tf_op jit(solution)/shard_map/block_reverse/pallas_call | solution.py:338
  664.3 6.8 collective-permute-done.102.refs_2_
  691.0 11.7 %collective-permute-done.107.refs_3_ = bf16[896,256]{1,0:T(8,128)(2,1)S(1)} collective-permute-done((bf16[896,256]{1,0:T(8,128)(2,1)S(1)}, bf16[896,256]{1,0:T(8,128)(2,1)S(1)}, u32[]{:S(2)}, u32[]{:S(2)}) %collective-permute-start.107) | collective-permute-done | bytes 458784 | tf_op jit(solution)/shard_map/ppermute | solution.py:37
  747.5 8.4 collective-permute-done.113
  758.2 11.9 %collective-permute-start.114 = (bf16[128,2048]{1,0:T(8,128)(2,1)}, bf16[128,2048]{1,0:T(8,128)(2,1)S(1)}, u32[]{:S(2)}, u32[]{:S(2)}) collective-permute-start(bf16[128,2048]{1,0:T(8,128)(2,1)} %add_convert_fusion), channel_id=1, source_target_pairs={{0,8},{8,16},{16,24},{1,9},{9,17},{17,25},{2,10},{10,18},{18,26},{... | collective-permute-start | bytes 1572872 | tf_op jit(solution)/shard_map/ppermute | solution.py:510
  773.8 9.2 %adam_back.2 = (f32[2,512,256]{2,1,0:T(8,128)}, f32[2,512,256]{2,1,0:T(8,128)}, f32[2,512,256]{2,1,0:T(8,128)}, f32[2,512,256]{2,1,0:T(8,128)}, f32[2,2048,256]{...) custom-call(s32[1]{0:T(128)} %bitcast.5.refs_0_, ...), custom_call_target="tpu_custom_call" | custom-call | flops 1024 | bytes 1024 | tf_op jit(solution)/shard_map/adam_back/pallas_call | solution.py:787
  782.9 11.1 %adam_front.2 = (f32[2,3,256,512]{3,2,1,0:T(8,128)}, f32[2,3,256,512]{3,2,1,0:T(8,128)}, f32[2,3,256,512]{3,2,1,0:T(8,128)}, f32[2,3,256,512]{3,2,1,0:T(8,128)},...) custom-call(s32[1]{0:T(128)} %bitcast.5.refs_0_, ...), custom_call_target="tpu_custom_call" | custom-call | flops 1024 | bytes 1024 | tf_op jit(solution)/shard_map/adam_front/pallas_call | solution.py:787
  819.9 11.2 %adam_front.3 = (f32[2,3,256,512]{3,2,1,0:T(8,128)}, f32[2,3,256,512]{3,2,1,0:T(8,128)}, f32[2,3,256,512]{3,2,1,0:T(8,128)}, f32[2,3,256,512]{3,2,1,0:T(8,128)},...) custom-call(s32[1]{0:T(128)} %bitcast.5.refs_0_, ...), custom_call_target="tpu_custom_call", output_to_operand_aliasing={{0}: (11, {}), {1}: (12, {}), {2}: (13, {}), {3}: (14, {}),... | custom-call | flops 1024 | bytes 1024 | tf_op jit(solution)/shard_map/adam_front/pallas_call | solution.py:787
  849.8 9.1 %adam_back.3 = (f32[2,512,256]{2,1,0:T(8,128)}, f32[2,512,256]{2,1,0:T(8,128)}, f32[2,512,256]{2,1,0:T(8,128)}, f32[2,512,256]{2,1,0:T(8,128)}, f32[2,2048,256]{...) custom-call(s32[1]{0:T(128)} %bitcast.5.refs_0_, ...), custom_call_target="tpu_custom_call", output_to_operand_aliasing={{0}: (11, {}), {1}: (12, {}), {2}: (13, {}), {3}: (14, {}),... | custom-call | flops 1024 | bytes 1024 | tf_op jit(solution)/shard_map/adam_back/pallas_call | solution.py:787
  (669 shorter events, 469.7 us)
Async XLA Ops:
  24.5 31.6 %collective-permute-start.8 = (bf16[896,256]{1,0:T(8,128)(2,1)}, bf16[896,256]{1,0:T(8,128)(2,1)S(1)}, u32[]{:S(2)}, u32[]{:S(2)}) collective-permute-start(bf16[896,256]{1,0:T(8,128)(2,1)} %get-tuple-element.245), channel_id=1, source_target_pairs={{0,16},{8,24},{16,0},{24,8},{1,17},{9,25},{17,1},{25,9},{2,18},{10... | collective-permute-start | bytes 1376264 | tf_op jit(solution)/shard_map/ppermute | solution.py:37
  60.1 46.3 %collective-permute-start.17 = (bf16[896,768]{1,0:T(8,128)(2,1)}, bf16[896,768]{1,0:T(8,128)(2,1)S(1)}, u32[]{:S(2)}, u32[]{:S(2)}) collective-permute-start(bf16[896,768]{1,0:T(8,128)(2,1)} %stack.68.refs_14_), channel_id=1, source_target_pairs={{0,4},{4,0},{1,5},{5,1},{2,6},{6,2},{3,7},{7,3},{8,12},{12,8},{9,1... | collective-permute-start | bytes 4128776 | tf_op jit(solution)/shard_map/ppermute | solution.py:41
  61.6 46.5 %collective-permute-start.18 = (bf16[896,768]{1,0:T(8,128)(2,1)}, bf16[896,768]{1,0:T(8,128)(2,1)S(1)}, u32[]{:S(2)}, u32[]{:S(2)}) collective-permute-start(bf16[896,768]{1,0:T(8,128)(2,1)} %stack.68.refs_14_), channel_id=1, source_target_pairs={{0,2},{2,0},{1,3},{3,1},{4,6},{6,4},{5,7},{7,5},{8,10},{10,8},{9,1... | collective-permute-start | bytes 4128776 | tf_op jit(solution)/shard_map/ppermute | solution.py:41
  130.9 44.2 %collective-permute-start.30 = (bf16[640,1024]{1,0:T(8,128)(2,1)}, bf16[640,1024]{1,0:T(8,128)(2,1)S(1)}, u32[]{:S(2)}, u32[]{:S(2)}) collective-permute-start(bf16[640,1024]{1,0:T(8,128)(2,1)} %stack.69.refs_2_.refs_19_), channel_id=1, source_target_pairs={{0,4},{4,0},{1,5},{5,1},{2,6},{6,2},{3,7},{7,3},{8,12},{12,8},{9,1... | collective-permute-start | bytes 3932168 | tf_op jit(solution)/shard_map/ppermute | solution.py:41
  146.4 39.6 %collective-permute-start.31 = (bf16[640,1024]{1,0:T(8,128)(2,1)S(1)}, bf16[640,1024]{1,0:T(8,128)(2,1)S(1)}, u32[]{:S(2)}, u32[]{:S(2)}) collective-permute-start(bf16[640,1024]{1,0:T(8,128)(2,1)S(1)} %copy-done.1), channel_id=1, source_target_pairs={{0,2},{2,0},{1,3},{3,1},{4,6},{6,4},{5,7},{7,5},{8,10},{10,8},{9,1... | collective-permute-start | bytes 3932168 | tf_op jit(solution)/shard_map/ppermute | solution.py:41
  149.6 35.1 %collective-permute-start.28 = (bf16[1536,256]{1,0:T(8,128)(2,1)}, bf16[1536,256]{1,0:T(8,128)(2,1)}, u32[]{:S(2)}, u32[]{:S(2)}) collective-permute-start(bf16[1536,256]{1,0:T(8,128)(2,1)} %get-tuple-element.268), channel_id=1, source_target_pairs={{0,8},{8,16},{16,24},{24,0},{1,9},{9,17},{17,25},{25,1},{2,10},{10... | collective-permute-start | bytes 2359304 | tf_op jit(solution)/shard_map/ppermute | solution.py:37
  188.4 36.6 %collective-permute-start.34 = (bf16[1536,256]{1,0:T(8,128)(2,1)}, bf16[1536,256]{1,0:T(8,128)(2,1)}, u32[]{:S(2)}, u32[]{:S(2)}) collective-permute-start(bf16[1536,256]{1,0:T(8,128)(2,1)} %get-tuple-element.275), channel_id=1, source_target_pairs={{0,16},{8,24},{16,0},{24,8},{1,17},{9,25},{17,1},{25,9},{2,18},{10... | collective-permute-start | bytes 2359304 | tf_op jit(solution)/shard_map/ppermute | solution.py:37
  226.8 37.2 %collective-permute-start.43 = (bf16[1536,512]{1,0:T(8,128)(2,1)S(1)}, bf16[1536,512]{1,0:T(8,128)(2,1)S(1)}, u32[]{:S(2)}, u32[]{:S(2)}) collective-permute-start(bf16[1536,512]{1,0:T(8,128)(2,1)S(1)} %copy-done), channel_id=1, source_target_pairs={{0,4},{4,0},{1,5},{5,1},{2,6},{6,2},{3,7},{7,3},{8,12},{12,8},{9,1... | collective-permute-start | bytes 4718600 | tf_op jit(solution)/shard_map/ppermute | solution.py:41
  227.2 37.2 %collective-permute-start.44 = (bf16[1536,512]{1,0:T(8,128)(2,1)S(1)}, bf16[1536,512]{1,0:T(8,128)(2,1)S(1)}, u32[]{:S(2)}, u32[]{:S(2)}) collective-permute-start(bf16[1536,512]{1,0:T(8,128)(2,1)S(1)} %copy-done), channel_id=1, source_target_pairs={{0,2},{2,0},{1,3},{3,1},{4,6},{6,4},{5,7},{7,5},{8,10},{10,8},{9,1... | collective-permute-start | bytes 4718600 | tf_op jit(solution)/shard_map/ppermute | solution.py:41
  265.8 31.0 %collective-permute-start.50 = (bf16[1536,256]{1,0:T(8,128)(2,1)}, bf16[1536,256]{1,0:T(8,128)(2,1)S(1)}, u32[]{:S(2)}, u32[]{:S(2)}) collective-permute-start(bf16[1536,256]{1,0:T(8,128)(2,1)} %collective-permute-done.34.refs_19_), channel_id=1, source_target_pairs={{0,2},{2,0},{1,3},{3,1},{4,6},{6,4},{5,7},{7,5},{8,10},{10,8},{9,1... | collective-permute-start | bytes 2359304 | tf_op jit(solution)/shard_map/ppermute | solution.py:41
  336.5 36.0 %collective-permute-start.62 = (bf16[128,2048]{1,0:T(8,128)(2,1)S(1)}, bf16[128,2048]{1,0:T(8,128)(2,1)S(1)}, u32[]{:S(2)}, u32[]{:S(2)}) collective-permute-start(bf16[128,2048]{1,0:T(8,128)(2,1)S(1)} %copy-done.14), channel_id=1, source_target_pairs={{0,8},{8,16},{16,24},{24,0},{1,9},{9,17},{17,25},{25,1},{2,10},{10... | collective-permute-start | bytes 1572872 | tf_op jit(solution)/shard_map/ppermute | solution.py:37
  336.5 38.2 %collective-permute-start.63 = (bf16[128,2048]{1,0:T(8,128)(2,1)S(1)}, bf16[128,2048]{1,0:T(8,128)(2,1)S(1)}, u32[]{:S(2)}, u32[]{:S(2)}) collective-permute-start(bf16[128,2048]{1,0:T(8,128)(2,1)S(1)} %copy-done.14), channel_id=1, source_target_pairs={{0,16},{8,24},{16,0},{24,8},{1,17},{9,25},{17,1},{25,9},{2,18},{10... | collective-permute-start | bytes 1572872 | tf_op jit(solution)/shard_map/ppermute | solution.py:37
  339.5 35.3 %collective-permute-start.64 = (bf16[128,2048]{1,0:T(8,128)(2,1)S(1)}, bf16[128,2048]{1,0:T(8,128)(2,1)S(1)}, u32[]{:S(2)}, u32[]{:S(2)}) collective-permute-start(bf16[128,2048]{1,0:T(8,128)(2,1)S(1)} %copy-done.14), channel_id=1, source_target_pairs={{0,24},{8,0},{16,8},{24,16},{1,25},{9,1},{17,9},{25,17},{2,26},{10... | collective-permute-start | bytes 1572872 | tf_op jit(solution)/shard_map/ppermute | solution.py:37
  387.3 48.5 %collective-permute-start.66 = (bf16[128,2048]{1,0:T(8,128)(2,1)}, bf16[128,2048]{1,0:T(8,128)(2,1)S(1)}, u32[]{:S(2)}, u32[]{:S(2)}) collective-permute-start(bf16[128,2048]{1,0:T(8,128)(2,1)} %get-tuple-element.298), channel_id=1, source_target_pairs={{0,24},{8,0},{16,8},{24,16},{1,25},{9,1},{17,9},{25,17},{2,26},{10... | collective-permute-start | bytes 1572872 | tf_op jit(solution)/shard_map/ppermute | solution.py:37
  398.1 47.5 %collective-permute-start.67 = (bf16[128,2048]{1,0:T(8,128)(2,1)}, bf16[128,2048]{1,0:T(8,128)(2,1)S(1)}, u32[]{:S(2)}, u32[]{:S(2)}) collective-permute-start(bf16[128,2048]{1,0:T(8,128)(2,1)} %get-tuple-element.299), channel_id=1, source_target_pairs={{0,16},{8,24},{16,0},{24,8},{1,17},{9,25},{17,1},{25,9},{2,18},{10... | collective-permute-start | bytes 1572872 | tf_op jit(solution)/shard_map/ppermute | solution.py:37
  399.7 45.8 %collective-permute-start.68 = (bf16[128,2048]{1,0:T(8,128)(2,1)}, bf16[128,2048]{1,0:T(8,128)(2,1)S(1)}, u32[]{:S(2)}, u32[]{:S(2)}) collective-permute-start(bf16[128,2048]{1,0:T(8,128)(2,1)} %get-tuple-element.300), channel_id=1, source_target_pairs={{0,8},{8,16},{16,24},{24,0},{1,9},{9,17},{17,25},{25,1},{2,10},{10... | collective-permute-start | bytes 1572872 | tf_op jit(solution)/shard_map/ppermute | solution.py:37
  494.9 30.2 %collective-permute-start.89 = (bf16[640,1024]{1,0:T(8,128)(2,1)}, bf16[640,1024]{1,0:T(8,128)(2,1)S(1)}, u32[]{:S(2)}, u32[]{:S(2)}) collective-permute-start(bf16[640,1024]{1,0:T(8,128)(2,1)} %get-tuple-element.313), channel_id=1, source_target_pairs={{0,4},{4,0},{1,5},{5,1},{2,6},{6,2},{3,7},{7,3},{8,12},{12,8},{9,1... | collective-permute-start | bytes 3932168 | tf_op jit(solution)/shard_map/ppermute | solution.py:41
  495.8 30.7 %collective-permute-start.90 = (bf16[640,1024]{1,0:T(8,128)(2,1)}, bf16[640,1024]{1,0:T(8,128)(2,1)S(1)}, u32[]{:S(2)}, u32[]{:S(2)}) collective-permute-start(bf16[640,1024]{1,0:T(8,128)(2,1)} %get-tuple-element.314), channel_id=1, source_target_pairs={{0,2},{2,0},{1,3},{3,1},{4,6},{6,4},{5,7},{7,5},{8,10},{10,8},{9,1... | collective-permute-start | bytes 3932168 | tf_op jit(solution)/shard_map/ppermute | solution.py:41
  577.7 63.9 %collective-permute-start.97 = (bf16[896,1024]{1,0:T(8,128)(2,1)}, bf16[896,1024]{1,0:T(8,128)(2,1)S(1)}, u32[]{:S(2)}, u32[]{:S(2)}) collective-permute-start(bf16[896,1024]{1,0:T(8,128)(2,1)} %get-tuple-element.326), channel_id=1, source_target_pairs={{0,4},{4,0},{1,5},{5,1},{2,6},{6,2},{3,7},{7,3},{8,12},{12,8},{9,1... | collective-permute-start | bytes 5505032 | tf_op jit(solution)/shard_map/ppermute | solution.py:41
  578.7 62.9 %collective-permute-start.98 = (bf16[896,1024]{1,0:T(8,128)(2,1)}, bf16[896,1024]{1,0:T(8,128)(2,1)}, u32[]{:S(2)}, u32[]{:S(2)}) collective-permute-start(bf16[896,1024]{1,0:T(8,128)(2,1)} %get-tuple-element.327), channel_id=1, source_target_pairs={{0,2},{2,0},{1,3},{3,1},{4,6},{6,4},{5,7},{7,5},{8,10},{10,8},{9,1... | collective-permute-start | bytes 5505032 | tf_op jit(solution)/shard_map/ppermute | solution.py:41
  588.4 41.0 %collective-permute-start.101 = (bf16[640,256]{1,0:T(8,128)(2,1)}, bf16[640,256]{1,0:T(8,128)(2,1)S(1)}, u32[]{:S(2)}, u32[]{:S(2)}) collective-permute-start(bf16[640,256]{1,0:T(8,128)(2,1)} %get-tuple-element.342), channel_id=1, source_target_pairs={{0,24},{8,0},{16,8},{24,16},{1,25},{9,1},{17,9},{25,17},{2,26},{10... | collective-permute-start | bytes 983048 | tf_op jit(solution)/shard_map/ppermute | solution.py:37
  589.6 39.8 %collective-permute-start.100 = (bf16[640,256]{1,0:T(8,128)(2,1)}, bf16[640,256]{1,0:T(8,128)(2,1)S(1)}, u32[]{:S(2)}, u32[]{:S(2)}) collective-permute-start(bf16[640,256]{1,0:T(8,128)(2,1)} %get-tuple-element.340), channel_id=1, source_target_pairs={{0,16},{8,24},{16,0},{24,8},{1,17},{9,25},{17,1},{25,9},{2,18},{10... | collective-permute-start | bytes 983048 | tf_op jit(solution)/shard_map/ppermute | solution.py:37
  589.6 39.8 %collective-permute-start.99 = (bf16[640,256]{1,0:T(8,128)(2,1)}, bf16[640,256]{1,0:T(8,128)(2,1)S(1)}, u32[]{:S(2)}, u32[]{:S(2)}) collective-permute-start(bf16[640,256]{1,0:T(8,128)(2,1)} %get-tuple-element.338), channel_id=1, source_target_pairs={{0,8},{8,16},{16,24},{24,0},{1,9},{9,17},{17,25},{25,1},{2,10},{10... | collective-permute-start | bytes 983048 | tf_op jit(solution)/shard_map/ppermute | solution.py:37
  671.9 30.8 %collective-permute-start.106 = (bf16[4,128,2048]{2,1,0:T(8,128)(2,1)}, bf16[4,128,2048]{2,1,0:T(8,128)(2,1)S(1)}, u32[]{:S(2)}, u32[]{:S(2)}) collective-permute-start(bf16[4,128,2048]{2,1,0:T(8,128)(2,1)} %get-tuple-element.351), channel_id=1, source_target_pairs={{0,1},{1,0},{2,3},{3,2},{4,5},{5,4},{6,7},{7,6},{8,9},{9,8},{10,11... | collective-permute-start | bytes 6291464 | tf_op jit(solution)/shard_map/ppermute | solution.py:41
  671.9 44.6 %collective-permute-start.109 = (bf16[896,1024]{1,0:T(8,128)(2,1)}, bf16[896,1024]{1,0:T(8,128)(2,1)}, u32[]{:S(2)}, u32[]{:S(2)}) collective-permute-start(bf16[896,1024]{1,0:T(8,128)(2,1)} %get-tuple-element.349), channel_id=1, source_target_pairs={{0,4},{4,0},{1,5},{5,1},{2,6},{6,2},{3,7},{7,3},{8,12},{12,8},{9,1... | collective-permute-start | bytes 5505032 | tf_op jit(solution)/shard_map/ppermute | solution.py:41
  672.9 43.6 %collective-permute-start.110 = (bf16[896,1024]{1,0:T(8,128)(2,1)}, bf16[896,1024]{1,0:T(8,128)(2,1)}, u32[]{:S(2)}, u32[]{:S(2)}) collective-permute-start(bf16[896,1024]{1,0:T(8,128)(2,1)} %get-tuple-element.350), channel_id=1, source_target_pairs={{0,2},{2,0},{1,3},{3,1},{4,6},{6,4},{5,7},{7,5},{8,10},{10,8},{9,1... | collective-permute-start | bytes 5505032 | tf_op jit(solution)/shard_map/ppermute | solution.py:41
  735.6 34.5 %collective-permute-start.111 = (bf16[128,2048]{1,0:T(8,128)(2,1)}, bf16[128,2048]{1,0:T(8,128)(2,1)}, u32[]{:S(2)}, u32[]{:S(2)}) collective-permute-start(bf16[128,2048]{1,0:T(8,128)(2,1)} %add_convert_fusion.2), channel_id=1, source_target_pairs={{16,8},{24,16},{17,9},{25,17},{18,10},{26,18},{19,11},{27,19},{20,... | collective-permute-start | bytes 1572872 | tf_op jit(solution)/shard_map/ppermute | solution.py:510
  739.9 64.8 %collective-permute-start.116 = (bf16[896,256]{1,0:T(8,128)(2,1)}, bf16[896,256]{1,0:T(8,128)(2,1)}, u32[]{:S(2)}, u32[]{:S(2)}) collective-permute-start(bf16[896,256]{1,0:T(8,128)(2,1)} %get-tuple-element.371), channel_id=1, source_target_pairs={{0,16},{8,24},{16,0},{24,8},{1,17},{9,25},{17,1},{25,9},{2,18},{10... | collective-permute-start | bytes 1376264 | tf_op jit(solution)/shard_map/ppermute | solution.py:37
  745.0 52.9 %collective-permute-start.121 = (bf16[640,1024]{1,0:T(8,128)(2,1)}, bf16[640,1024]{1,0:T(8,128)(2,1)S(1)}, u32[]{:S(2)}, u32[]{:S(2)}) collective-permute-start(bf16[640,1024]{1,0:T(8,128)(2,1)} %get-tuple-element.378), channel_id=1, source_target_pairs={{0,2},{2,0},{1,3},{3,1},{4,6},{6,4},{5,7},{7,5},{8,10},{10,8},{9,1... | collective-permute-start | bytes 3932168 | tf_op jit(solution)/shard_map/ppermute | solution.py:41
  746.4 51.6 %collective-permute-start.120 = (bf16[640,1024]{1,0:T(8,128)(2,1)}, bf16[640,1024]{1,0:T(8,128)(2,1)}, u32[]{:S(2)}, u32[]{:S(2)}) collective-permute-start(bf16[640,1024]{1,0:T(8,128)(2,1)} %get-tuple-element.376), channel_id=1, source_target_pairs={{0,4},{4,0},{1,5},{5,1},{2,6},{6,2},{3,7},{7,3},{8,12},{12,8},{9,1... | collective-permute-start | bytes 3932168 | tf_op jit(solution)/shard_map/ppermute | solution.py:41
  758.2 46.5 %collective-permute-start.114 = (bf16[128,2048]{1,0:T(8,128)(2,1)}, bf16[128,2048]{1,0:T(8,128)(2,1)S(1)}, u32[]{:S(2)}, u32[]{:S(2)}) collective-permute-start(bf16[128,2048]{1,0:T(8,128)(2,1)} %add_convert_fusion), channel_id=1, source_target_pairs={{0,8},{8,16},{16,24},{1,9},{9,17},{17,25},{2,10},{10,18},{18,26},{... | collective-permute-start | bytes 1572872 | tf_op jit(solution)/shard_map/ppermute | solution.py:510
  772.4 32.3 %collective-permute-start.112 = (bf16[128,2048]{1,0:T(8,128)(2,1)}, bf16[128,2048]{1,0:T(8,128)(2,1)}, u32[]{:S(2)}, u32[]{:S(2)}) collective-permute-start(bf16[128,2048]{1,0:T(8,128)(2,1)} %add_convert_fusion.1), channel_id=1, source_target_pairs={{8,0},{16,8},{24,16},{9,1},{17,9},{25,17},{10,2},{18,10},{26,18},{... | collective-permute-start | bytes 1572872 | tf_op jit(solution)/shard_map/ppermute | solution.py:510
  (233 other events, 3133.0 us)

commit v3 on v2

--- a/solution.py
+++ b/solution.py
@@ -1177,7 +1177,6 @@
         second_front = second_hop(*hop_front)
         rows = [after(row, hop_front[0]) for row in rows]
     grads_back = weight_grads("back", flat(left), stack_rows(rows), cut_of("back"))
-    tokens = [step("back", 1, came_one[0], 0), step("front", 1, came_one[1], 0)]
     result_rows = give(place, results)
     if ny == 2:
         parts = scatter_line(
@@ -1193,7 +1192,7 @@
         late_far = [after(part, *second_front) for part in grads_back[:2]]
         hop_back = first_hop([late_far + grads_back[2:]])
         second_back = second_hop(*(after(p, came_front[1], came_front[3]) for p in hop_back))
-        sum_back = split(z_array, grads_back[4:], *second_back)
+        sum_back = split(z_array, grads_back[4:], *second_back, [result_rows])
         came_back = send_z(sum_back)
         norm_parts = [*parts[:2], after(parts[2], *came_front[1:], *second_back)]
     else:
@@ -1202,10 +1201,11 @@
         sum_back = sum_plain(place, [grads_back])
         came_back = send_z(sum_back)
         norm_parts = parts
-    grad_next, low, sums[0] = norm_back(
-        0, grad_next, hidden_in, norm_parts, model_vec, [*tokens, result_rows]
-    )
-    came_front = [came_front[0], *(after(piece, sum_back[0]) for piece in came_front[1:])]
+    grad_next, low, sums[0] = norm_back(0, grad_next, hidden_in, norm_parts, model_vec)
+    came_one = [[after(piece, sum_back[0]) for piece in pieces] for pieces in came_one]
+    came_front = [after(piece, sum_back[0]) for piece in came_front]
+    step("back", 1, came_one[0], 0)
+    step("front", 1, came_one[1], 0)
     token = step("front", 0, came_front, 0)
     step("back", 0, came_back, 0, [token])
     late = sum_back[0]

time: 875 us -> 887 us (1.014)
  starting transfers between devices: 190 us -> 207 us
    ppermute x30, starting transfers between devices: 69 us -> 83.7 us  [line_z(): return lax.ppermute(array, 'z', pairs)]
    unnamed x267 -> x269, local copies, waits for them, and re-layouts: 24 us -> 24.5 us
  transfers between devices with their start and end apart: 136 -> 136, of which waited for: 46 -> 51; matrix products, arithmetic and copies ran while one was open for 12% -> 12% of each run, Pallas kernels for 31% -> 31%
where the time goes in v3:
time: 887 us; the launch traced here: 878 us
  Pallas kernels  289 us (33%)
  waiting for transfers between devices  253 us (29%)
  starting transfers between devices  207 us (23%)
  matrix products  72.5 us (8%)
  local copies, waits for them, and re-layouts  32.6 us (4%)
  other arithmetic  21.5 us (2%)
    ppermute x30, waiting for transfers between devices, line_z(): return lax.ppermute(array, 'z', pairs)  124 us
    ppermute x30, starting transfers between devices, line_z(): return lax.ppermute(array, 'z', pairs)  83.7 us
    dot_general x20, matrix products, dot_tn(): lax.dot_general(left, right, (((0,), (0,)), ((), ())), preferred_element_...  69.1 us
    pallas_call x2, Pallas kernels, reverse(): pl.pallas_call(lambda *refs: reverse_kernel(layouts, len(weights), *refs)...  68.4 us
    ppermute x73, waiting for transfers between devices, swap(): return lax.ppermute(array, axis, [(0, 1), (1, 0)])  66.8 us
    ppermute x30, starting transfers between devices, shift_z(): return lax.ppermute(array, 'z', [(i, (i + step) % ZS) for i in range(ZS)])  63.1 us
    ppermute x30, waiting for transfers between devices, shift_z(): return lax.ppermute(array, 'z', [(i, (i + step) % ZS) for i in range(ZS)])  60.7 us
    ppermute x73, starting transfers between devices, swap(): return lax.ppermute(array, axis, [(0, 1), (1, 0)])  55.4 us
  transfers between devices with their start and end apart: 136, of which 51 were waited for; matrix products, arithmetic and copies ran while one was open for 12% of the time, Pallas kernels for 31%

profile of v3, /device:TPU:0, one launch (start us, length us, event | category | flops | bytes accessed | tf_op | source)
XLA Modules:
  0.0 878.2 jit_solution(18254061443335915023)
XLA Ops:
  61.6 9.6 %collective-permute-start.10 = (bf16[640,256]{1,0:T(8,128)(2,1)}, bf16[640,256]{1,0:T(8,128)(2,1)S(1)}, u32[]{:S(2)}, u32[]{:S(2)}) collective-permute-start(bf16[640,256]{1,0:T(8,128)(2,1)} %get-tuple-element.254), channel_id=1, source_target_pairs={{0,8},{8,16},{16,24},{24,0},{1,9},{9,17},{17,25},{25,1},{2,10},{10... | collective-permute-start | bytes 983048 | tf_op jit(solution)/shard_map/ppermute | solution.py:37
  81.4 10.2 %collective-permute-done.11.refs_3_ = bf16[640,256]{1,0:T(8,128)(2,1)S(1)} collective-permute-done((bf16[640,256]{1,0:T(8,128)(2,1)}, bf16[640,256]{1,0:T(8,128)(2,1)S(1)}, u32[]{:S(2)}, u32[]{:S(2)}) %collective-permute-start.11) | collective-permute-done | bytes 327712 | tf_op jit(solution)/shard_map/ppermute | solution.py:37
  92.2 9.2 %collective-permute-start.13 = (bf16[128,2048]{1,0:T(8,128)(2,1)}, bf16[128,2048]{1,0:T(8,128)(2,1)S(1)}, u32[]{:S(2)}, u32[]{:S(2)}) collective-permute-start(bf16[128,2048]{1,0:T(8,128)(2,1)} %get-tuple-element.259.refs_1_), channel_id=1, source_target_pairs={{0,8},{8,16},{16,24},{1,9},{9,17},{17,25},{2,10},{10,18},{18,26},{... | collective-permute-start | bytes 1572872 | tf_op jit(solution)/shard_map/ppermute | solution.py:510
  119.2 14.8 %collective-permute-done.21 = bf16[128,2048]{1,0:T(8,128)(2,1)S(1)} collective-permute-done((bf16[128,2048]{1,0:T(8,128)(2,1)S(1)}, bf16[128,2048]{1,0:T(8,128)(2,1)S(1)}, u32[]{:S(2)}, u32[]{:S(2)}) %collective-permute-start.21) | collective-permute-done | bytes 524320 | tf_op jit(solution)/shard_map/ppermute | solution.py:510
  139.8 13.6 %collective-permute-done.24 = bf16[128,2048]{1,0:T(8,128)(2,1)} collective-permute-done((bf16[128,2048]{1,0:T(8,128)(2,1)}, bf16[128,2048]{1,0:T(8,128)(2,1)}, u32[]{:S(2)}, u32[]{:S(2)}) %collective-permute-start.24) | collective-permute-done | bytes 524320 | tf_op jit(solution)/shard_map/ppermute | solution.py:510
  163.1 22.2 %block_front.2 = (bf16[2,4,128,2048]{3,2,1,0:T(8,128)(2,1)}, bf16[2,4,128,768]{3,2,1,0:T(8,128)(2,1)}, f32[2,4,128,256]{3,2,1,0:T(8,128)}, bf16[2,4,128,1280]{3,2,1,0:T(8,128)(2,1)}, bf16[2,4,128,1024]{3,2,1,0:T(8,128)(2,1)}) custom-call(s32[1]{0:T(128)} %bitcast.5.refs_0_, bf16[128,2048]{1,0:T(8,128)(2,1)} %get-tuple-element.259.refs_1_, ...), custom_call_target="tpu_custom_call" | custom-call | flops 1024 | bytes 1024 | tf_op jit(solution)/shard_map/block_front/pallas_call | solution.py:267
  185.3 8.0 collective-permute-done.29.refs_1_
  196.7 10.2 %collective-permute-done.32.refs_5_.refs_22_ = bf16[256,1024]{1,0:T(8,128)(2,1)S(1)} collective-permute-done((bf16[256,1024]{1,0:T(8,128)(2,1)S(1)}, bf16[256,1024]{1,0:T(8,128)(2,1)S(1)}, u32[]{:S(2)}, u32[]{:S(2)}) %collective-permute-start.32) | collective-permute-done | bytes 524320 | tf_op jit(solution)/shard_map/ppermute | solution.py:41
  215.9 11.1 %block_back.1 = (bf16[4,128,2048]{2,1,0:T(8,128)(2,1)}, bf16[4,128,2048]{2,1,0:T(8,128)(2,1)}) custom-call(s32[1]{0:T(128)} %bitcast.5.refs_0_, bf16[2,4,128,1280]{3,2,1,0:T(8,128)(2,1)} %get-tuple-element.277.refs_1_, bf16[640,1024]{1,0:T(8,128)(2,1)} %stack.69.refs_2_.refs_19_, bf16[640,1024]{1,0:T(8,128)(2,1)} %copy-done.5, bf16[640,1024]{1,0:T(8,128)(2,1)} %copy-done.7, ...), custom_call_target="tpu_custom_call" | custom-call | flops 1024 | bytes 1024 | tf_op jit(solution)/shard_map/block_back/pallas_call | solution.py:288
  243.2 11.7 %collective-permute-done.38 = bf16[128,2048]{1,0:T(8,128)(2,1)S(1)} collective-permute-done((bf16[128,2048]{1,0:T(8,128)(2,1)}, bf16[128,2048]{1,0:T(8,128)(2,1)S(1)}, u32[]{:S(2)}, u32[]{:S(2)}) %collective-permute-start.38) | collective-permute-done | bytes 524320 | tf_op jit(solution)/shard_map/ppermute | solution.py:510
  263.2 6.2 collective-permute-done.43.refs_15_
  273.1 7.3 collective-permute-start.42
  283.7 6.0 collective-permute-done.42.refs_3_
  301.0 10.1 %collective-permute-done.51.refs_17_ = bf16[768,512]{1,0:T(8,128)(2,1)S(1)} collective-permute-done((bf16[768,512]{1,0:T(8,128)(2,1)}, bf16[768,512]{1,0:T(8,128)(2,1)S(1)}, u32[]{:S(2)}, u32[]{:S(2)}) %collective-permute-start.51) | collective-permute-done | bytes 786464 | tf_op jit(solution)/shard_map/ppermute | solution.py:41
  317.4 14.1 %collective-permute-done.55 = bf16[128,2048]{1,0:T(8,128)(2,1)S(1)} collective-permute-done((bf16[128,2048]{1,0:T(8,128)(2,1)S(1)}, bf16[128,2048]{1,0:T(8,128)(2,1)S(1)}, u32[]{:S(2)}, u32[]{:S(2)}) %collective-permute-start.55) | collective-permute-done | bytes 524320 | tf_op jit(solution)/shard_map/ppermute | solution.py:510
  335.3 10.9 %collective-permute-done.56 = bf16[128,2048]{1,0:T(8,128)(2,1)S(1)} collective-permute-done((bf16[128,2048]{1,0:T(8,128)(2,1)S(1)}, bf16[128,2048]{1,0:T(8,128)(2,1)S(1)}, u32[]{:S(2)}, u32[]{:S(2)}) %collective-permute-start.56) | collective-permute-done | bytes 524320 | tf_op jit(solution)/shard_map/ppermute | solution.py:510
  352.3 30.6 %block_front.3 = (bf16[2,4,128,2048]{3,2,1,0:T(8,128)(2,1)}, bf16[2,4,128,768]{3,2,1,0:T(8,128)(2,1)}, f32[2,4,128,256]{3,2,1,0:T(8,128)}, bf16[2,4,128,1280]{3,...) custom-call(s32[1]{0:T(128)} %bitcast.5.refs_0_, ...), custom_call_target="tpu_custom_call" | custom-call | flops 1024 | bytes 1024 | tf_op jit(solution)/shard_map/block_front/pallas_call | solution.py:267
  386.4 6.2 collective-permute-done.65.refs_2_
  397.8 9.5 %collective-permute-start.66 = (bf16[128,2048]{1,0:T(8,128)(2,1)}, bf16[128,2048]{1,0:T(8,128)(2,1)S(1)}, u32[]{:S(2)}, u32[]{:S(2)}) collective-permute-start(bf16[128,2048]{1,0:T(8,128)(2,1)} %get-tuple-element.305), channel_id=1, source_target_pairs={{0,24},{8,0},{16,8},{24,16},{1,25},{9,1},{17,9},{25,17},{2,26},{10... | collective-permute-start | bytes 1572872 | tf_op jit(solution)/shard_map/ppermute | solution.py:37
  411.2 35.0 %block_reverse.2 = (bf16[2,4,128,1792]{3,2,1,0:T(8,128)(2,1)}, bf16[4,128,2048]{2,1,0:T(8,128)(2,1)}, bf16[4,128,2048]{2,1,0:T(8,128)(2,1)}, f32[1,1792]{1,0:T(1,128)}) custom-call(s32[1]{0:T(128)} %bitcast.5.refs_0_, bf16[128,2048]{1,0:T(8,128)(2,1)} %get-tuple-element.302.refs_1_.refs_0_, bf16[128,2048]{1,0:T(8,128)(2,1)} %copy-done.41, ...), custom_call_target="tpu_custom_call" | custom-call | flops 1024 | bytes 1024 | tf_op jit(solution)/shard_map/block_reverse/pallas_call | solution.py:338
  446.2 9.8 %collective-permute-done.67.refs_3_ = bf16[128,2048]{1,0:T(8,128)(2,1)S(1)} collective-permute-done((bf16[128,2048]{1,0:T(8,128)(2,1)}, bf16[128,2048]{1,0:T(8,128)(2,1)S(1)}, u32[]{:S(2)}, u32[]{:S(2)}) %collective-permute-start.67) | collective-permute-done | bytes 524320 | tf_op jit(solution)/shard_map/ppermute | solution.py:37
  475.6 5.7 collective-permute-done.77
  515.4 7.3 collective-permute-done.81.refs_3_
  559.3 6.1 collective-permute-done.88
  574.6 11.4 %collective-permute-done.93 = bf16[128,2048]{1,0:T(8,128)(2,1)S(1)} collective-permute-done((bf16[128,2048]{1,0:T(8,128)(2,1)S(1)}, bf16[128,2048]{1,0:T(8,128)(2,1)S(1)}, u32[]{:S(2)}, u32[]{:S(2)}) %collective-permute-start.93) | collective-permute-done | bytes 524320 | tf_op jit(solution)/shard_map/ppermute | solution.py:510
  608.1 33.4 %block_reverse.3 = (bf16[2,4,128,1792]{3,2,1,0:T(8,128)(2,1)}, bf16[4,128,2048]{2,1,0:T(8,128)(2,1)}, bf16[4,128,2048]{2,1,0:T(8,128)(2,1)}, f32[1,1792]{1,0:T(1,128)}) custom-call(s32[1]{0:T(128)} %bitcast.5.refs_0_, bf16[128,2048]{1,0:T(8,128)(2,1)} %get-tuple-element.368.refs_1_.refs_0_, bf16[128,2048]{1,0:T(8,128)(2,1)} %copy-done.17, ...), custom_call_target="tpu_custom_call" | custom-call | flops 1024 | bytes 1024 | tf_op jit(solution)/shard_map/block_reverse/pallas_call | solution.py:338
  702.2 11.3 %collective-permute-done.107.refs_3_ = bf16[896,256]{1,0:T(8,128)(2,1)S(1)} collective-permute-done((bf16[896,256]{1,0:T(8,128)(2,1)S(1)}, bf16[896,256]{1,0:T(8,128)(2,1)S(1)}, u32[]{:S(2)}, u32[]{:S(2)}) %collective-permute-start.107) | collective-permute-done | bytes 458784 | tf_op jit(solution)/shard_map/ppermute | solution.py:37
  768.1 16.3 %collective-permute-start.114 = (bf16[128,2048]{1,0:T(8,128)(2,1)}, bf16[128,2048]{1,0:T(8,128)(2,1)}, u32[]{:S(2)}, u32[]{:S(2)}) collective-permute-start(bf16[128,2048]{1,0:T(8,128)(2,1)} %add_convert_fusion), channel_id=1, source_target_pairs={{0,8},{8,16},{16,24},{1,9},{9,17},{17,25},{2,10},{10,18},{18,26},{... | collective-permute-start | bytes 1572872 | tf_op jit(solution)/shard_map/ppermute | solution.py:510
  808.7 11.3 %adam_front.2 = (f32[2,3,256,512]{3,2,1,0:T(8,128)}, f32[2,3,256,512]{3,2,1,0:T(8,128)}, f32[2,3,256,512]{3,2,1,0:T(8,128)}, f32[2,3,256,512]{3,2,1,0:T(8,128)},...) custom-call(s32[1]{0:T(128)} %bitcast.5.refs_0_, ...), custom_call_target="tpu_custom_call" | custom-call | flops 1024 | bytes 1024 | tf_op jit(solution)/shard_map/adam_front/pallas_call | solution.py:787
  820.0 9.2 %adam_back.2 = (f32[2,512,256]{2,1,0:T(8,128)}, f32[2,512,256]{2,1,0:T(8,128)}, f32[2,512,256]{2,1,0:T(8,128)}, f32[2,512,256]{2,1,0:T(8,128)}, f32[2,2048,256]{...) custom-call(s32[1]{0:T(128)} %bitcast.5.refs_0_, ...), custom_call_target="tpu_custom_call" | custom-call | flops 1024 | bytes 1024 | tf_op jit(solution)/shard_map/adam_back/pallas_call | solution.py:787
  829.3 11.2 %adam_front.3 = (f32[2,3,256,512]{3,2,1,0:T(8,128)}, f32[2,3,256,512]{3,2,1,0:T(8,128)}, f32[2,3,256,512]{3,2,1,0:T(8,128)}, f32[2,3,256,512]{3,2,1,0:T(8,128)},...) custom-call(s32[1]{0:T(128)} %bitcast.5.refs_0_, ...), custom_call_target="tpu_custom_call", output_to_operand_aliasing={{0}: (11, {}), {1}: (12, {}), {2}: (13, {}), {3}: (14, {}),... | custom-call | flops 1024 | bytes 1024 | tf_op jit(solution)/shard_map/adam_front/pallas_call | solution.py:787
  862.0 9.4 %adam_back.3 = (f32[2,512,256]{2,1,0:T(8,128)}, f32[2,512,256]{2,1,0:T(8,128)}, f32[2,512,256]{2,1,0:T(8,128)}, f32[2,512,256]{2,1,0:T(8,128)}, f32[2,2048,256]{...) custom-call(s32[1]{0:T(128)} %bitcast.5.refs_0_, ...), custom_call_target="tpu_custom_call", output_to_operand_aliasing={{0}: (11, {}), {1}: (12, {}), {2}: (13, {}), {3}: (14, {}),... | custom-call | flops 1024 | bytes 1024 | tf_op jit(solution)/shard_map/adam_back/pallas_call | solution.py:787
  (671 shorter events, 476.3 us)
Async XLA Ops:
  24.2 30.6 %collective-permute-start.8 = (bf16[896,256]{1,0:T(8,128)(2,1)}, bf16[896,256]{1,0:T(8,128)(2,1)S(1)}, u32[]{:S(2)}, u32[]{:S(2)}) collective-permute-start(bf16[896,256]{1,0:T(8,128)(2,1)} %get-tuple-element.252), channel_id=1, source_target_pairs={{0,16},{8,24},{16,0},{24,8},{1,17},{9,25},{17,1},{25,9},{2,18},{10... | collective-permute-start | bytes 1376264 | tf_op jit(solution)/shard_map/ppermute | solution.py:37
  58.9 47.3 %collective-permute-start.17 = (bf16[896,768]{1,0:T(8,128)(2,1)}, bf16[896,768]{1,0:T(8,128)(2,1)S(1)}, u32[]{:S(2)}, u32[]{:S(2)}) collective-permute-start(bf16[896,768]{1,0:T(8,128)(2,1)} %stack.68.refs_14_), channel_id=1, source_target_pairs={{0,4},{4,0},{1,5},{5,1},{2,6},{6,2},{3,7},{7,3},{8,12},{12,8},{9,1... | collective-permute-start | bytes 4128776 | tf_op jit(solution)/shard_map/ppermute | solution.py:41
  60.4 47.5 %collective-permute-start.18 = (bf16[896,768]{1,0:T(8,128)(2,1)}, bf16[896,768]{1,0:T(8,128)(2,1)S(1)}, u32[]{:S(2)}, u32[]{:S(2)}) collective-permute-start(bf16[896,768]{1,0:T(8,128)(2,1)} %stack.68.refs_14_), channel_id=1, source_target_pairs={{0,2},{2,0},{1,3},{3,1},{4,6},{6,4},{5,7},{7,5},{8,10},{10,8},{9,1... | collective-permute-start | bytes 4128776 | tf_op jit(solution)/shard_map/ppermute | solution.py:41
  139.3 46.0 %collective-permute-start.30 = (bf16[640,1024]{1,0:T(8,128)(2,1)}, bf16[640,1024]{1,0:T(8,128)(2,1)S(1)}, u32[]{:S(2)}, u32[]{:S(2)}) collective-permute-start(bf16[640,1024]{1,0:T(8,128)(2,1)} %stack.69.refs_2_.refs_19_), channel_id=1, source_target_pairs={{0,4},{4,0},{1,5},{5,1},{2,6},{6,2},{3,7},{7,3},{8,12},{12,8},{9,1... | collective-permute-start | bytes 3932168 | tf_op jit(solution)/shard_map/ppermute | solution.py:41
  154.8 39.1 %collective-permute-start.31 = (bf16[640,1024]{1,0:T(8,128)(2,1)S(1)}, bf16[640,1024]{1,0:T(8,128)(2,1)S(1)}, u32[]{:S(2)}, u32[]{:S(2)}) collective-permute-start(bf16[640,1024]{1,0:T(8,128)(2,1)S(1)} %copy-done.1), channel_id=1, source_target_pairs={{0,2},{2,0},{1,3},{3,1},{4,6},{6,4},{5,7},{7,5},{8,10},{10,8},{9,1... | collective-permute-start | bytes 3932168 | tf_op jit(solution)/shard_map/ppermute | solution.py:41
  156.4 37.0 %collective-permute-start.29 = (bf16[1536,256]{1,0:T(8,128)(2,1)}, bf16[1536,256]{1,0:T(8,128)(2,1)}, u32[]{:S(2)}, u32[]{:S(2)}) collective-permute-start(bf16[1536,256]{1,0:T(8,128)(2,1)} %get-tuple-element.276), channel_id=1, source_target_pairs={{0,24},{8,0},{16,8},{24,16},{1,25},{9,1},{17,9},{25,17},{2,26},{10... | collective-permute-start | bytes 2359304 | tf_op jit(solution)/shard_map/ppermute | solution.py:37
  194.5 35.8 %collective-permute-start.34 = (bf16[1536,256]{1,0:T(8,128)(2,1)}, bf16[1536,256]{1,0:T(8,128)(2,1)}, u32[]{:S(2)}, u32[]{:S(2)}) collective-permute-start(bf16[1536,256]{1,0:T(8,128)(2,1)} %get-tuple-element.282), channel_id=1, source_target_pairs={{0,16},{8,24},{16,0},{24,8},{1,17},{9,25},{17,1},{25,9},{2,18},{10... | collective-permute-start | bytes 2359304 | tf_op jit(solution)/shard_map/ppermute | solution.py:37
  232.2 37.2 %collective-permute-start.43 = (bf16[1536,512]{1,0:T(8,128)(2,1)S(1)}, bf16[1536,512]{1,0:T(8,128)(2,1)S(1)}, u32[]{:S(2)}, u32[]{:S(2)}) collective-permute-start(bf16[1536,512]{1,0:T(8,128)(2,1)S(1)} %copy-done), channel_id=1, source_target_pairs={{0,4},{4,0},{1,5},{5,1},{2,6},{6,2},{3,7},{7,3},{8,12},{12,8},{9,1... | collective-permute-start | bytes 4718600 | tf_op jit(solution)/shard_map/ppermute | solution.py:41
  233.7 37.2 %collective-permute-start.44 = (bf16[1536,512]{1,0:T(8,128)(2,1)S(1)}, bf16[1536,512]{1,0:T(8,128)(2,1)S(1)}, u32[]{:S(2)}, u32[]{:S(2)}) collective-permute-start(bf16[1536,512]{1,0:T(8,128)(2,1)S(1)} %copy-done), channel_id=1, source_target_pairs={{0,2},{2,0},{1,3},{3,1},{4,6},{6,4},{5,7},{7,5},{8,10},{10,8},{9,1... | collective-permute-start | bytes 4718600 | tf_op jit(solution)/shard_map/ppermute | solution.py:41
  347.0 35.9 %collective-permute-start.62 = (bf16[128,2048]{1,0:T(8,128)(2,1)S(1)}, bf16[128,2048]{1,0:T(8,128)(2,1)S(1)}, u32[]{:S(2)}, u32[]{:S(2)}) collective-permute-start(bf16[128,2048]{1,0:T(8,128)(2,1)S(1)} %copy-done.14), channel_id=1, source_target_pairs={{0,8},{8,16},{16,24},{24,0},{1,9},{9,17},{17,25},{25,1},{2,10},{10... | collective-permute-start | bytes 1572872 | tf_op jit(solution)/shard_map/ppermute | solution.py:37
  347.0 38.2 %collective-permute-start.63 = (bf16[128,2048]{1,0:T(8,128)(2,1)S(1)}, bf16[128,2048]{1,0:T(8,128)(2,1)S(1)}, u32[]{:S(2)}, u32[]{:S(2)}) collective-permute-start(bf16[128,2048]{1,0:T(8,128)(2,1)S(1)} %copy-done.14), channel_id=1, source_target_pairs={{0,16},{8,24},{16,0},{24,8},{1,17},{9,25},{17,1},{25,9},{2,18},{10... | collective-permute-start | bytes 1572872 | tf_op jit(solution)/shard_map/ppermute | solution.py:37
  347.1 38.2 %collective-permute-start.64 = (bf16[128,2048]{1,0:T(8,128)(2,1)S(1)}, bf16[128,2048]{1,0:T(8,128)(2,1)S(1)}, u32[]{:S(2)}, u32[]{:S(2)}) collective-permute-start(bf16[128,2048]{1,0:T(8,128)(2,1)S(1)} %copy-done.14), channel_id=1, source_target_pairs={{0,24},{8,0},{16,8},{24,16},{1,25},{9,1},{17,9},{25,17},{2,26},{10... | collective-permute-start | bytes 1572872 | tf_op jit(solution)/shard_map/ppermute | solution.py:37
  397.8 48.4 %collective-permute-start.66 = (bf16[128,2048]{1,0:T(8,128)(2,1)}, bf16[128,2048]{1,0:T(8,128)(2,1)S(1)}, u32[]{:S(2)}, u32[]{:S(2)}) collective-permute-start(bf16[128,2048]{1,0:T(8,128)(2,1)} %get-tuple-element.305), channel_id=1, source_target_pairs={{0,24},{8,0},{16,8},{24,16},{1,25},{9,1},{17,9},{25,17},{2,26},{10... | collective-permute-start | bytes 1572872 | tf_op jit(solution)/shard_map/ppermute | solution.py:37
  407.3 48.7 %collective-permute-start.67 = (bf16[128,2048]{1,0:T(8,128)(2,1)}, bf16[128,2048]{1,0:T(8,128)(2,1)S(1)}, u32[]{:S(2)}, u32[]{:S(2)}) collective-permute-start(bf16[128,2048]{1,0:T(8,128)(2,1)} %get-tuple-element.306), channel_id=1, source_target_pairs={{0,16},{8,24},{16,0},{24,8},{1,17},{9,25},{17,1},{25,9},{2,18},{10... | collective-permute-start | bytes 1572872 | tf_op jit(solution)/shard_map/ppermute | solution.py:37
  410.2 45.8 %collective-permute-start.68 = (bf16[128,2048]{1,0:T(8,128)(2,1)}, bf16[128,2048]{1,0:T(8,128)(2,1)S(1)}, u32[]{:S(2)}, u32[]{:S(2)}) collective-permute-start(bf16[128,2048]{1,0:T(8,128)(2,1)} %get-tuple-element.307), channel_id=1, source_target_pairs={{0,8},{8,16},{16,24},{24,0},{1,9},{9,17},{17,25},{25,1},{2,10},{10... | collective-permute-start | bytes 1572872 | tf_op jit(solution)/shard_map/ppermute | solution.py:37
  504.6 30.2 %collective-permute-start.89 = (bf16[640,1024]{1,0:T(8,128)(2,1)}, bf16[640,1024]{1,0:T(8,128)(2,1)S(1)}, u32[]{:S(2)}, u32[]{:S(2)}) collective-permute-start(bf16[640,1024]{1,0:T(8,128)(2,1)} %get-tuple-element.320), channel_id=1, source_target_pairs={{0,4},{4,0},{1,5},{5,1},{2,6},{6,2},{3,7},{7,3},{8,12},{12,8},{9,1... | collective-permute-start | bytes 3932168 | tf_op jit(solution)/shard_map/ppermute | solution.py:41
  506.1 29.9 %collective-permute-start.90 = (bf16[640,1024]{1,0:T(8,128)(2,1)}, bf16[640,1024]{1,0:T(8,128)(2,1)S(1)}, u32[]{:S(2)}, u32[]{:S(2)}) collective-permute-start(bf16[640,1024]{1,0:T(8,128)(2,1)} %get-tuple-element.321), channel_id=1, source_target_pairs={{0,2},{2,0},{1,3},{3,1},{4,6},{6,4},{5,7},{7,5},{8,10},{10,8},{9,1... | collective-permute-start | bytes 3932168 | tf_op jit(solution)/shard_map/ppermute | solution.py:41
  586.7 67.3 %collective-permute-start.97 = (bf16[896,1024]{1,0:T(8,128)(2,1)}, bf16[896,1024]{1,0:T(8,128)(2,1)S(1)}, u32[]{:S(2)}, u32[]{:S(2)}) collective-permute-start(bf16[896,1024]{1,0:T(8,128)(2,1)} %get-tuple-element.333), channel_id=1, source_target_pairs={{0,4},{4,0},{1,5},{5,1},{2,6},{6,2},{3,7},{7,3},{8,12},{12,8},{9,1... | collective-permute-start | bytes 5505032 | tf_op jit(solution)/shard_map/ppermute | solution.py:41
  590.1 63.8 %collective-permute-start.98 = (bf16[896,1024]{1,0:T(8,128)(2,1)}, bf16[896,1024]{1,0:T(8,128)(2,1)}, u32[]{:S(2)}, u32[]{:S(2)}) collective-permute-start(bf16[896,1024]{1,0:T(8,128)(2,1)} %get-tuple-element.334), channel_id=1, source_target_pairs={{0,2},{2,0},{1,3},{3,1},{4,6},{6,4},{5,7},{7,5},{8,10},{10,8},{9,1... | collective-permute-start | bytes 5505032 | tf_op jit(solution)/shard_map/ppermute | solution.py:41
  598.7 42.8 %collective-permute-start.99 = (bf16[640,256]{1,0:T(8,128)(2,1)}, bf16[640,256]{1,0:T(8,128)(2,1)S(1)}, u32[]{:S(2)}, u32[]{:S(2)}) collective-permute-start(bf16[640,256]{1,0:T(8,128)(2,1)} %get-tuple-element.345), channel_id=1, source_target_pairs={{0,8},{8,16},{16,24},{24,0},{1,9},{9,17},{17,25},{25,1},{2,10},{10... | collective-permute-start | bytes 983048 | tf_op jit(solution)/shard_map/ppermute | solution.py:37
  598.8 42.7 %collective-permute-start.100 = (bf16[640,256]{1,0:T(8,128)(2,1)}, bf16[640,256]{1,0:T(8,128)(2,1)S(1)}, u32[]{:S(2)}, u32[]{:S(2)}) collective-permute-start(bf16[640,256]{1,0:T(8,128)(2,1)} %get-tuple-element.347), channel_id=1, source_target_pairs={{0,16},{8,24},{16,0},{24,8},{1,17},{9,25},{17,1},{25,9},{2,18},{10... | collective-permute-start | bytes 983048 | tf_op jit(solution)/shard_map/ppermute | solution.py:37
  600.4 41.1 %collective-permute-start.101 = (bf16[640,256]{1,0:T(8,128)(2,1)}, bf16[640,256]{1,0:T(8,128)(2,1)S(1)}, u32[]{:S(2)}, u32[]{:S(2)}) collective-permute-start(bf16[640,256]{1,0:T(8,128)(2,1)} %get-tuple-element.349), channel_id=1, source_target_pairs={{0,24},{8,0},{16,8},{24,16},{1,25},{9,1},{17,9},{25,17},{2,26},{10... | collective-permute-start | bytes 983048 | tf_op jit(solution)/shard_map/ppermute | solution.py:37
  682.6 30.9 %collective-permute-start.106 = (bf16[4,128,2048]{2,1,0:T(8,128)(2,1)}, bf16[4,128,2048]{2,1,0:T(8,128)(2,1)S(1)}, u32[]{:S(2)}, u32[]{:S(2)}) collective-permute-start(bf16[4,128,2048]{2,1,0:T(8,128)(2,1)} %get-tuple-element.358), channel_id=1, source_target_pairs={{0,1},{1,0},{2,3},{3,2},{4,5},{5,4},{6,7},{7,6},{8,9},{9,8},{10,11... | collective-permute-start | bytes 6291464 | tf_op jit(solution)/shard_map/ppermute | solution.py:41
  682.6 44.6 %collective-permute-start.109 = (bf16[896,1024]{1,0:T(8,128)(2,1)}, bf16[896,1024]{1,0:T(8,128)(2,1)}, u32[]{:S(2)}, u32[]{:S(2)}) collective-permute-start(bf16[896,1024]{1,0:T(8,128)(2,1)} %get-tuple-element.356), channel_id=1, source_target_pairs={{0,4},{4,0},{1,5},{5,1},{2,6},{6,2},{3,7},{7,3},{8,12},{12,8},{9,1... | collective-permute-start | bytes 5505032 | tf_op jit(solution)/shard_map/ppermute | solution.py:41
  684.2 43.0 %collective-permute-start.110 = (bf16[896,1024]{1,0:T(8,128)(2,1)}, bf16[896,1024]{1,0:T(8,128)(2,1)}, u32[]{:S(2)}, u32[]{:S(2)}) collective-permute-start(bf16[896,1024]{1,0:T(8,128)(2,1)} %get-tuple-element.357), channel_id=1, source_target_pairs={{0,2},{2,0},{1,3},{3,1},{4,6},{6,4},{5,7},{7,5},{8,10},{10,8},{9,1... | collective-permute-start | bytes 5505032 | tf_op jit(solution)/shard_map/ppermute | solution.py:41
  755.5 38.7 %collective-permute-start.116 = (bf16[896,256]{1,0:T(8,128)(2,1)}, bf16[896,256]{1,0:T(8,128)(2,1)}, u32[]{:S(2)}, u32[]{:S(2)}) collective-permute-start(bf16[896,256]{1,0:T(8,128)(2,1)} %get-tuple-element.378), channel_id=1, source_target_pairs={{0,16},{8,24},{16,0},{24,8},{1,17},{9,25},{17,1},{25,9},{2,18},{10... | collective-permute-start | bytes 1376264 | tf_op jit(solution)/shard_map/ppermute | solution.py:37
  763.7 37.7 %collective-permute-start.112 = (bf16[128,2048]{1,0:T(8,128)(2,1)S(1)}, bf16[128,2048]{1,0:T(8,128)(2,1)}, u32[]{:S(2)}, u32[]{:S(2)}) collective-permute-start(bf16[128,2048]{1,0:T(8,128)(2,1)S(1)} %add_convert_fusion.1), channel_id=1, source_target_pairs={{8,0},{16,8},{24,16},{9,1},{17,9},{25,17},{10,2},{18,10},{26,18},{... | collective-permute-start | bytes 1572872 | tf_op jit(solution)/shard_map/ppermute | solution.py:510
  794.2 59.6 %collective-permute-start.122 = (bf16[640,256]{1,0:T(8,128)(2,1)}, bf16[640,256]{1,0:T(8,128)(2,1)S(1)}, u32[]{:S(2)}, u32[]{:S(2)}) collective-permute-start(bf16[640,256]{1,0:T(8,128)(2,1)} %get-tuple-element.388), channel_id=1, source_target_pairs={{0,8},{8,16},{16,24},{24,0},{1,9},{9,17},{17,25},{25,1},{2,10},{10... | collective-permute-start | bytes 983048 | tf_op jit(solution)/shard_map/ppermute | solution.py:37
  796.6 59.3 %collective-permute-start.123 = (bf16[640,256]{1,0:T(8,128)(2,1)}, bf16[640,256]{1,0:T(8,128)(2,1)S(1)}, u32[]{:S(2)}, u32[]{:S(2)}) collective-permute-start(bf16[640,256]{1,0:T(8,128)(2,1)} %get-tuple-element.389), channel_id=1, source_target_pairs={{0,16},{8,24},{16,0},{24,8},{1,17},{9,25},{17,1},{25,9},{2,18},{10... | collective-permute-start | bytes 983048 | tf_op jit(solution)/shard_map/ppermute | solution.py:37
  799.9 56.0 %collective-permute-start.124 = (bf16[640,256]{1,0:T(8,128)(2,1)}, bf16[640,256]{1,0:T(8,128)(2,1)S(1)}, u32[]{:S(2)}, u32[]{:S(2)}) collective-permute-start(bf16[640,256]{1,0:T(8,128)(2,1)} %get-tuple-element.390), channel_id=1, source_target_pairs={{0,24},{8,0},{16,8},{24,16},{1,25},{9,1},{17,9},{25,17},{2,26},{10... | collective-permute-start | bytes 983048 | tf_op jit(solution)/shard_map/ppermute | solution.py:37
  805.8 50.2 %collective-permute-start.126 = (bf16[128,2048]{1,0:T(8,128)(2,1)}, bf16[128,2048]{1,0:T(8,128)(2,1)S(1)}, u32[]{:S(2)}, u32[]{:S(2)}) collective-permute-start(bf16[128,2048]{1,0:T(8,128)(2,1)} %get-tuple-element.391.refs_0_), channel_id=1, source_target_pairs={{0,2},{2,0},{1,3},{3,1},{4,6},{6,4},{5,7},{7,5},{8,10},{10,8},{9,1... | collective-permute-start | bytes 1572872 | tf_op jit(solution)/shard_map/ppermute | solution.py:41
  807.2 33.2 %collective-permute-start.134 = (f32[2,896]{1,0:T(2,128)S(1)}, f32[2,896]{1,0:T(2,128)S(1)}, u32[]{:S(2)}, u32[]{:S(2)}) collective-permute-start(f32[2,896]{1,0:T(2,128)S(1)} %slice.235), channel_id=1, source_target_pairs={{0,2},{2,0},{1,3},{3,1},{4,6},{6,4},{5,7},{7,5},{8,10},{10,8},{9,1... | collective-permute-start | bytes 21512 | tf_op jit(solution)/shard_map/ppermute | solution.py:41
  (234 other events, 3268.6 us)
